TPU v7x, 32 devices: a whole 2x2x4 slice. The times are simulated.
32 devices in a mesh: dp: 4 (over z), row: 2 (over x), col: 4 (over y, core).
Axes of the slice: x: 2, y: 2, z: 4, core: 2. Of those that a mesh axis runs over, the one named last changes fastest.
Arguments:
- block_input: bfloat16 [2560, 2560], P('dp', 'col'), may hold values from -6 to 6
- segment_ids: int32 [4, 640], P('dp'), may hold values from 0 to 1, never falling along the last dimension, each value on 1 to 560 neighbouring positions
- output_cotangent: bfloat16 [2560, 2560], P('dp', 'col'), may hold values from -6 to 6
- norm_gains: float32 [2, 2560], P(None, 'col'), may hold values from 0.5 to 1.5
- branch_weights: bfloat16 [2, 2560, 2560], P(None, 'col', 'row'), may hold values from -0.125 to 0.125
- mixer_vectors: float32 [8, 2560], P(None, 'row'), may hold values from -9 to 1.5
- gate_blocks: bfloat16 [2, 10, 256, 256], P(None, 'row'), may hold values from -0.375 to 0.375
- output_weights: bfloat16 [2560, 2560], P('row', 'col'), may hold values from -0.5 to 0.5
- expand_weights: bfloat16 [2, 2560, 7680], P(None, 'col', 'row'), may hold values from -0.125 to 0.125
- contract_weights: bfloat16 [7680, 2560], P('row', 'col'), may hold values from -0.1875 to 0.1875
- gains_momentum: float32 [2, 2560], P(None, 'col'), may hold values from -32 to 32
- branch_momentum: float32 [2, 4, 640, 2560], P(None, 'col', 'dp', 'row'), may hold values from -32 to 32
- vectors_momentum: float32 [8, 2560], P(None, 'row'), may hold values from -32 to 32
- gates_momentum: float32 [2, 10, 256, 256], P(None, 'row'), may hold values from -32 to 32
- output_momentum: float32 [2, 1280, 2560], P('row', 'dp', 'col'), may hold values from -32 to 32
- expand_momentum: float32 [2, 4, 640, 7680], P(None, 'col', 'dp', 'row'), may hold values from -32 to 32
- contract_momentum: float32 [2, 3840, 2560], P('row', 'dp', 'col'), may hold values from -32 to 32
Outputs:
- block_output: bfloat16 [2560, 2560], P('dp', 'col')
- input_grad: bfloat16 [2560, 2560], P('dp', 'col')
- gains_grad: float32 [2, 2560], P(None, 'col')
- branch_grad: float32 [2, 4, 640, 2560], P(None, 'col', 'dp', 'row')
- vectors_grad: float32 [8, 2560], P(None, 'row')
- gates_grad: float32 [2, 10, 256, 256], P(None, 'row')
- output_grad: float32 [2, 1280, 2560], P('row', 'dp', 'col')
- expand_grad: float32 [2, 4, 640, 7680], P(None, 'col', 'dp', 'row')
- contract_grad: float32 [2, 3840, 2560], P('row', 'dp', 'col')
- gains_new: float32 [2, 2560], P(None, 'col')
- branch_new: float32 [2, 4, 640, 2560], P(None, 'col', 'dp', 'row')
- vectors_new: float32 [8, 2560], P(None, 'row')
- gates_new: float32 [2, 10, 256, 256], P(None, 'row')
- output_new: float32 [2, 1280, 2560], P('row', 'dp', 'col')
- expand_new: float32 [2, 4, 640, 7680], P(None, 'col', 'dp', 'row')
- contract_new: float32 [2, 3840, 2560], P('row', 'dp', 'col')
- gains_moment: float32 [2, 2560], P(None, 'col')
- branch_moment: float32 [2, 4, 640, 2560], P(None, 'col', 'dp', 'row')
- vectors_moment: float32 [8, 2560], P(None, 'row')
- gates_moment: float32 [2, 10, 256, 256], P(None, 'row')
- output_moment: float32 [2, 1280, 2560], P('row', 'dp', 'col')
- expand_moment: float32 [2, 4, 640, 7680], P(None, 'col', 'dp', 'row')
- contract_moment: float32 [2, 3840, 2560], P('row', 'dp', 'col')
All inputs are finite; a program needn't handle non-finite values.
Results may differ from a plain program's by a relative error of at most 0.012.
Values may be sent and summed in bfloat16 or wider, within the bound.
A program may use at most 256 MiB of HBM per device.

v0:
```python
import jax
import jax.numpy as jnp
from jax import lax
from jax.sharding import PartitionSpec as P

CONV = 4
GROUP = 128
HS = 256


eps_norm = 1e-06
eps_frob = 1e-07
poly_first = 3.4445
poly_second = -4.775
poly_third = 2.0315
momentum_rate = 0.9
muon_rate = 0.1
gate_rate = 0.02
vector_rate = 0.3
decay_scale = 8.0


def broadcast(value, axis, source):
    kept = jnp.where(lax.axis_index(axis) == source, value, 0).astype(value.dtype)
    return lax.psum(kept, axis)


def from_behind(value, axis, steps):
    count = lax.axis_size(axis)
    initial, last = (max(0, -steps), min(count, count - steps))
    return lax.ppermute(value, axis, [(source, source + steps) for source in range(initial, last)])


def prefix(value, axis, combine, identity, reverse):
    count, here = (lax.axis_size(axis), lax.axis_index(axis))
    everything = jax.tree.map(lambda part: lax.all_gather(part, axis), value)
    start = jax.tree.map(
        lambda part, zero: jnp.broadcast_to(jnp.asarray(zero, part.dtype), part.shape),
        value,
        identity,
    )

    def lap(k, before):
        at = count - 1 - k if reverse else k
        reached = at > here if reverse else at < here
        new = combine(before, jax.tree.map(lambda part: part[at], everything))
        return jax.tree.map(lambda a, b: jnp.where(reached, a, b), new, before)

    return lax.fori_loop(0, count, lap, start)


def gelu_tanh(value):
    return jax.nn.gelu(value, approximate=True)


def product(left, right):
    return jnp.dot(left, right, preferred_element_type=jnp.float32)


def product_tn(left, right):
    return lax.dot_general(
        left, right, (((0,), (0,)), ((), ())), preferred_element_type=jnp.float32
    )


def product_nt(left, right):
    return lax.dot_general(
        left, right, (((1,), (1,)), ((), ())), preferred_element_type=jnp.float32
    )


def link(first, second):
    return (first[0] * second[0], second[0] * first[1] + second[1])


def token_total(values):
    return lax.psum(values, "col")


def feature_total(values):
    return lax.psum(values, "row")


def owner_rows(term, count):
    return lax.psum_scatter(
        term(jnp.int32(0), count * lax.axis_size("col")), "col", scatter_dimension=0, tiled=True
    )


def all_tokens(piece):
    return lax.all_gather(piece, "col", axis=0, tiled=True)


def owner_send(block, root):
    return broadcast(block, "dp", root)


def norm_forward(stream, gain, width):
    total = token_total(jnp.sum(stream * stream, axis=1))
    scale = lax.rsqrt(total / width + eps_norm)
    return (scale, stream * scale[:, None] * gain[None, :])


def norm_backward(stream, scale, gain, grad_normed, width):
    weighted = grad_normed * gain[None, :]
    inner = token_total(jnp.sum(stream * weighted, axis=1))
    grad_stream = (
        scale[:, None] * weighted - stream * (scale * scale * scale * inner / width)[:, None]
    )
    grad_gain = jnp.sum(grad_normed * stream * scale[:, None], axis=0)
    return (grad_stream, grad_gain)


def orthogonalize(block):
    work = block
    values = work.astype(jnp.float32)
    work = (values / (jnp.sqrt(jnp.sum(values * values)) + eps_frob)).astype(jnp.bfloat16)
    for step in range(5):
        gram = product_nt(work, work).astype(jnp.bfloat16)
        poly = (poly_second * gram.astype(jnp.float32) + poly_third * product(gram, gram)).astype(
            jnp.bfloat16
        )
        work = (poly_first * work.astype(jnp.float32) + product(poly, work)).astype(jnp.bfloat16)
    return work


def owner_results(blocks, dp_place, dp_count):
    results = [None, None, None, None, None, None]
    for members in ((0, 1, 2), (3, 4, 5)):
        flipped = [blocks[number].shape[0] > blocks[number].shape[1] for number in members]
        wide = [
            blocks[number].T if turn else blocks[number] for number, turn in zip(members, flipped)
        ]
        chosen = wide[0]
        for number, candidate in zip(members[1:], wide[1:]):
            chosen = jnp.where(dp_place == number % dp_count, candidate, chosen)
        done = orthogonalize(chosen)
        for number, turn in zip(members, flipped):
            kept = jnp.where(dp_place == number % dp_count, done, jnp.zeros_like(done))
            results[number] = kept.T if turn else kept
    return results


def grouped_step(grad, moment, weight, rate):
    new_moment = momentum_rate * moment + grad
    rows, cols = new_moment.shape
    grouped = new_moment.reshape(rows, cols // GROUP, GROUP)
    norm_sq = jnp.mean(grouped * grouped, axis=2, keepdims=True)
    update = (grouped * lax.rsqrt(norm_sq + eps_norm)).reshape(rows, cols)
    return (new_moment, weight - rate * update)


def shards(
    block_input,
    segment_ids,
    output_cotangent,
    norm_gains,
    branch_weights,
    mixer_vectors,
    gate_blocks,
    output_weights,
    expand_weights,
    contract_weights,
    gains_momentum,
    branch_momentum,
    vectors_momentum,
    gates_momentum,
    output_momentum,
    expand_momentum,
    contract_momentum,
):
    f32 = jnp.float32
    bf16 = jnp.bfloat16
    col_count = lax.axis_size("col")
    col_place = lax.axis_index("col")
    dp_count = lax.axis_size("dp")
    dp_place = lax.axis_index("dp")
    group_rows = block_input.shape[0]
    rows = group_rows // col_count
    lanes = mixer_vectors.shape[1]
    heads_here = lanes // HS
    feature_count = block_input.shape[1]
    width = feature_count * col_count
    first_row = col_place * rows
    reach = CONV - 1
    seg_row = segment_ids[0]
    seg_ext = jnp.concatenate(
        [jnp.full((reach,), -1, jnp.int32), seg_row, jnp.full((reach,), -2, jnp.int32)]
    )
    seg_here = lax.dynamic_slice_in_dim(seg_ext, first_row + reach, rows + reach)
    masks = []
    for shift in range(CONV):
        earlier = lax.dynamic_slice_in_dim(seg_ext, first_row + reach - shift, rows + reach)
        masks.append((earlier == seg_here).astype(f32))
    reset_rows = masks[1][:rows] < 0.5
    stream = block_input.astype(f32)
    scale_one, normed_one = norm_forward(stream, norm_gains[0], width)
    normed_low = normed_one.astype(bf16)

    def branch_term(start, count):
        return jnp.einsum("td,kdl->tkl", normed_low, branch_weights, preferred_element_type=f32)

    branch_pre = owner_rows(branch_term, rows)
    mixed = branch_pre[:, 0]
    gelu_in = branch_pre[:, 1]
    edge = from_behind(mixed[rows - reach :], "col", 1)
    extended = jnp.concatenate([edge, mixed], axis=0)
    windows = []
    conv_out = jnp.zeros((rows, lanes), f32) + mixer_vectors[CONV][None, :]
    for shift in range(CONV):
        window = extended[reach - shift : reach - shift + rows] * masks[shift][:rows, None]
        windows.append(window)
        conv_out = conv_out + mixer_vectors[shift][None, :] * window
    conv_low = conv_out.astype(bf16).reshape(rows, heads_here, HS)
    gate_pre = jnp.einsum(
        "thi,ghij->tghj", conv_low, gate_blocks, preferred_element_type=f32
    ).reshape(rows, 2, lanes)
    gate_pre = gate_pre + mixer_vectors[CONV + 1 : CONV + 3][None]

    def recurrence_terms(conv_values, gate_values, rate_values):
        input_gate = jax.nn.sigmoid(gate_values[:, 0])
        decay_gate = jax.nn.sigmoid(gate_values[:, 1])
        log_decay = -decay_scale * decay_gate * jax.nn.softplus(rate_values)[None, :]
        inject_scale = jnp.where(reset_rows[:, None], 1.0, jnp.sqrt(1.0 - jnp.exp(2.0 * log_decay)))
        decay_values = jnp.where(reset_rows[:, None], 0.0, jnp.exp(log_decay))
        return (decay_values, inject_scale * input_gate * conv_values)

    (decay, inject), pull_terms = jax.vjp(
        recurrence_terms, conv_out, gate_pre, mixer_vectors[CONV + 3]
    )
    local_a, local_b = lax.associative_scan(link, (decay, inject), axis=0)
    identity = (jnp.ones((lanes,), f32), jnp.zeros((lanes,), f32))
    incoming = prefix((local_a[-1], local_b[-1]), "col", link, identity, False)
    carried = incoming[1]
    state = local_a * carried[None, :] + local_b
    gelu_out, pull_gelu = jax.vjp(gelu_tanh, gelu_in)
    hidden = (gelu_out * state).astype(bf16)
    hidden_all = all_tokens(hidden)
    middle = stream + feature_total(product(hidden_all, output_weights))
    scale_two, normed_two = norm_forward(middle, norm_gains[1], width)
    normed_two_low = normed_two.astype(bf16)

    def expand_term(start, count):
        return jnp.einsum("td,kdf->tkf", normed_two_low, expand_weights, preferred_element_type=f32)

    expand_pre = owner_rows(expand_term, rows)

    def geglu(gate_values, up_values):
        return gelu_tanh(gate_values) * up_values

    activated, pull_geglu = jax.vjp(geglu, expand_pre[:, 0], expand_pre[:, 1])
    activated_low = activated.astype(bf16)
    activated_all = all_tokens(activated_low)
    block_output = (middle + feature_total(product(activated_all, contract_weights))).astype(bf16)
    cot_values = output_cotangent.astype(f32)
    contract_grad = product_tn(activated_all, output_cotangent)

    def contract_term(start, count):
        return product_nt(output_cotangent, contract_weights)

    grad_activated = owner_rows(contract_term, rows)
    grad_gate, grad_up = pull_geglu(grad_activated)
    grad_expand_low = jnp.stack([grad_gate, grad_up], axis=1).astype(bf16)
    grad_expand_all = all_tokens(grad_expand_low)
    expand_grad = jnp.einsum(
        "td,tkf->kdf", normed_two_low, grad_expand_all, preferred_element_type=f32
    )
    grad_normed_two = feature_total(
        jnp.einsum("tkf,kdf->td", grad_expand_all, expand_weights, preferred_element_type=f32)
    )
    grad_middle_norm, gain_two_grad = norm_backward(
        middle, scale_two, norm_gains[1], grad_normed_two, width
    )
    grad_middle = cot_values + grad_middle_norm
    grad_branch_low = grad_middle.astype(bf16)
    output_grad = product_tn(hidden_all, grad_branch_low)

    def output_term(start, count):
        return product_nt(grad_branch_low, output_weights)

    grad_hidden = owner_rows(output_term, rows)
    grad_state = grad_hidden * gelu_out
    (grad_gelu_in,) = pull_gelu(grad_hidden * state)
    shifted_decay = jnp.concatenate([decay[1:], jnp.ones((1, lanes), f32)], axis=0)
    back_a, back_b = lax.associative_scan(link, (shifted_decay, grad_state), reverse=True, axis=0)
    from_later = prefix((decay[0] * back_a[0], decay[0] * back_b[0]), "col", link, identity, True)
    grad_total = back_a * from_later[1][None, :] + back_b
    previous = jnp.concatenate([carried[None, :], state[:-1]], axis=0)
    grad_conv_direct, grad_gate_pre, grad_rate = pull_terms((grad_total * previous, grad_total))
    grad_gate_low = grad_gate_pre.astype(bf16)
    grad_gate_heads = grad_gate_low.reshape(rows, 2, heads_here, HS)
    grad_conv = grad_conv_direct + jnp.einsum(
        "tghj,ghij->thi", grad_gate_heads, gate_blocks, preferred_element_type=f32
    ).reshape(rows, lanes)
    gates_grad = jnp.einsum("thi,tghj->ghij", conv_low, grad_gate_heads, preferred_element_type=f32)
    gate_bias_grad = jnp.sum(grad_gate_low.astype(f32), axis=0)
    after = from_behind(grad_conv[:reach], "col", -1)
    grad_conv_ext = jnp.concatenate([grad_conv, after], axis=0)
    grad_mixed = jnp.zeros((rows, lanes), f32)
    tap_grads = []
    for shift in range(CONV):
        masked = grad_conv_ext * masks[shift][:, None]
        grad_mixed = grad_mixed + mixer_vectors[shift][None, :] * masked[shift : shift + rows]
        tap_grads.append(jnp.sum(grad_conv * windows[shift], axis=0))
    vector_rows = tap_grads + [
        jnp.sum(grad_conv, axis=0),
        gate_bias_grad[0],
        gate_bias_grad[1],
        grad_rate,
    ]
    vectors_grad = jnp.stack(vector_rows)
    grad_branch_pre = jnp.stack([grad_mixed, grad_gelu_in], axis=1).astype(bf16)
    grad_branch_all = all_tokens(grad_branch_pre)
    branch_grad = jnp.einsum("td,tkl->kdl", normed_low, grad_branch_all, preferred_element_type=f32)
    grad_normed_one = feature_total(
        jnp.einsum("tkl,kdl->td", grad_branch_all, branch_weights, preferred_element_type=f32)
    )
    grad_stream_norm, gain_one_grad = norm_backward(
        stream, scale_one, norm_gains[0], grad_normed_one, width
    )
    input_grad = (grad_middle + grad_stream_norm).astype(bf16)
    gain_slots = jnp.zeros((col_count, 2, feature_count), f32)
    gain_slots = lax.dynamic_update_slice_in_dim(
        gain_slots, jnp.stack([gain_one_grad, gain_two_grad])[None], col_place, 0
    )
    gates_total, vectors_total, slots_total = lax.psum(
        (gates_grad, vectors_grad, gain_slots), ("dp", "col")
    )
    gains_total = lax.dynamic_index_in_dim(slots_total, col_place, 0, keepdims=False)
    summed = (
        lax.psum_scatter(branch_grad[0], "dp", scatter_dimension=0, tiled=True),
        lax.psum_scatter(branch_grad[1], "dp", scatter_dimension=0, tiled=True),
        lax.psum_scatter(output_grad, "dp", scatter_dimension=0, tiled=True),
        lax.psum_scatter(expand_grad[0], "dp", scatter_dimension=0, tiled=True),
        lax.psum_scatter(expand_grad[1], "dp", scatter_dimension=0, tiled=True),
        lax.psum_scatter(contract_grad, "dp", scatter_dimension=0, tiled=True),
    )
    moments_old = (
        branch_momentum[0, 0],
        branch_momentum[1, 0],
        output_momentum[0],
        expand_momentum[0, 0],
        expand_momentum[1, 0],
        contract_momentum[0],
    )
    weights_full = (
        branch_weights[0],
        branch_weights[1],
        output_weights,
        expand_weights[0],
        expand_weights[1],
        contract_weights,
    )
    moments_new = tuple((momentum_rate * old + fresh for old, fresh in zip(moments_old, summed)))
    block_shapes = [
        (summed[number].shape[0] * dp_count, summed[number].shape[1]) for number in range(6)
    ]
    gathered = (
        lax.all_gather(moments_new[0].astype(bf16), "dp", axis=0, tiled=True),
        lax.all_gather(moments_new[1].astype(bf16), "dp", axis=0, tiled=True),
        lax.all_gather(moments_new[2].astype(bf16), "dp", axis=0, tiled=True),
        lax.all_gather(moments_new[3].astype(bf16), "dp", axis=0, tiled=True),
        lax.all_gather(moments_new[4].astype(bf16), "dp", axis=0, tiled=True),
        lax.all_gather(moments_new[5].astype(bf16), "dp", axis=0, tiled=True),
    )
    orth = owner_results(list(gathered), dp_place, dp_count)
    pieces = tuple(
        (
            lax.dynamic_slice_in_dim(
                owner_send(orth[number], number % dp_count),
                dp_place * summed[number].shape[0],
                summed[number].shape[0],
                0,
            ).astype(f32)
            for number in range(6)
        )
    )
    new_pieces = []
    for number in range(6):
        block_rows, block_cols = block_shapes[number]
        piece_rows = summed[number].shape[0]
        weight_piece = lax.dynamic_slice_in_dim(
            weights_full[number], dp_place * piece_rows, piece_rows, 0
        ).astype(f32)
        new_pieces.append(
            weight_piece - muon_rate * max(1.0, block_rows / block_cols) ** 0.5 * pieces[number]
        )
    gates_moment = momentum_rate * gates_momentum + gates_total
    gate_sq = jnp.mean(gates_moment * gates_moment, axis=(2, 3), keepdims=True)
    gates_new = gate_blocks.astype(f32) - gate_rate * gates_moment * lax.rsqrt(gate_sq + eps_norm)
    vectors_moment, vectors_new = grouped_step(
        vectors_total, vectors_momentum, mixer_vectors, vector_rate
    )
    gains_moment, gains_new = grouped_step(gains_total, gains_momentum, norm_gains, vector_rate)
    return (
        block_output,
        input_grad,
        gains_total,
        jnp.stack([summed[0], summed[1]])[:, None],
        vectors_total,
        gates_total,
        summed[2][None],
        jnp.stack([summed[3], summed[4]])[:, None],
        summed[5][None],
        gains_new,
        jnp.stack([new_pieces[0], new_pieces[1]])[:, None],
        vectors_new,
        gates_new,
        new_pieces[2][None],
        jnp.stack([new_pieces[3], new_pieces[4]])[:, None],
        new_pieces[5][None],
        gains_moment,
        jnp.stack([moments_new[0], moments_new[1]])[:, None],
        vectors_moment,
        gates_moment,
        moments_new[2][None],
        jnp.stack([moments_new[3], moments_new[4]])[:, None],
        moments_new[5][None],
    )


def solution(mesh):
    return jax.shard_map(
        shards,
        mesh=mesh,
        in_specs=(
            P("dp", "col"),
            P("dp", None),
            P("dp", "col"),
            P(None, "col"),
            P(None, "col", "row"),
            P(None, "row"),
            P(None, "row", None, None),
            P("row", "col"),
            P(None, "col", "row"),
            P("row", "col"),
            P(None, "col"),
            P(None, "col", "dp", "row"),
            P(None, "row"),
            P(None, "row", None, None),
            P("row", "dp", "col"),
            P(None, "col", "dp", "row"),
            P("row", "dp", "col"),
        ),
        out_specs=(
            P("dp", "col"),
            P("dp", "col"),
            P(None, "col"),
            P(None, "col", "dp", "row"),
            P(None, "row"),
            P(None, "row", None, None),
            P("row", "dp", "col"),
            P(None, "col", "dp", "row"),
            P("row", "dp", "col"),
            P(None, "col"),
            P(None, "col", "dp", "row"),
            P(None, "row"),
            P(None, "row", None, None),
            P("row", "dp", "col"),
            P(None, "col", "dp", "row"),
            P("row", "dp", "col"),
            P(None, "col"),
            P(None, "col", "dp", "row"),
            P(None, "row"),
            P(None, "row", None, None),
            P("row", "dp", "col"),
            P(None, "col", "dp", "row"),
            P("row", "dp", "col"),
        ),
        check_vma=False,
    )
```

profile of v0, /device:TPU:24, one launch (start us, length us, event | category | flops | bytes accessed | tf_op | source)
XLA Modules:
  0.0 3004.1 jit_solution(10844004488599774710)
XLA Ops:
  30.5 55.0 %reduce-scatter.19.cloned.1.call-done = f32[160,2,1280]{2,0,1:T(8,128)} async-done(((f32[640,2,1280]{2,0,1:T(8,128)}), f32[160,2,1280]{2,0,1:T(8,128)}) %reduce-scatter.19.cloned.1.call-update) | async-done | bytes 1638416 | tf_op jit(solution)/shard_map/reduce_scatter | solution.py:85
  212.7 21.1 all-gather.15.cloned.1.call-done
  238.4 9.0 fusion.200
  247.5 44.0 %all-reduce.69.cloned.1.call-done = f32[640,640]{1,0:T(8,128)} async-done(((f32[640,640]{1,0:T(8,128)}), f32[640,640]{1,0:T(8,128)}) %all-reduce.69.cloned.1.call-update) | async-done | bytes 1638416 | tf_op jit(solution)/shard_map/psum | solution.py:81
  300.3 16.8 fusion.135
  317.1 57.9 %reduce-scatter.23.cloned.1.call-done = f32[160,3840]{1,0:T(8,128)} async-done(((f32[640,3840]{1,0:T(8,128)}), f32[160,3840]{1,0:T(8,128)}) %reduce-scatter.23.cloned.1.call-update) | async-done | bytes 2457616 | tf_op jit(solution)/shard_map/reduce_scatter | solution.py:85
  375.0 147.1 %reduce-scatter.21.cloned.1.call-done = f32[160,2,3840]{2,0,1:T(8,128)} async-done(((f32[640,2,3840]{2,0,1:T(8,128)}), f32[160,2,3840]{2,0,1:T(8,128)}) %reduce-scatter.21.cloned.1.call-update) | async-done | bytes 4915216 | tf_op jit(solution)/shard_map/reduce_scatter | solution.py:85
  528.8 66.6 %all-gather.19.cloned.1.call-done = bf16[640,2,3840]{2,0,1:T(8,128)(2,1)} async-done(((bf16[160,2,3840]{2,0,1:T(8,128)(2,1)}), bf16[640,2,3840]{2,0,1:T(8,128)(2,1)}) %all-gather.19.cloned.1.call-update) | async-done | bytes 9830416 | tf_op jit(solution)/shard_map/all_gather | solution.py:91
  595.4 13.1 convolution_bitcast_fusion.3
  608.5 53.0 %all-reduce.71.cloned.1.call-done = f32[640,640]{1,0:T(8,128)} async-done(((f32[640,640]{1,0:T(8,128)}), f32[640,640]{1,0:T(8,128)}) %all-reduce.71.cloned.1.call-update) | async-done | bytes 1638416 | tf_op jit(solution)/shard_map/psum | solution.py:81
  706.9 8.6 reduce-scatter.25.cloned.1.call-done
  887.5 10.1 rev.9
  897.5 10.1 rev.8
  933.5 30.3 %all-gather.21.cloned.1.call-done = bf16[640,2,1280]{2,0,1:T(8,128)(2,1)} async-done(((bf16[160,2,1280]{2,0,1:T(8,128)(2,1)}), bf16[640,2,1280]{2,0,1:T(8,128)(2,1)}) %all-gather.21.cloned.1.call-update) | async-done | bytes 3276816 | tf_op jit(solution)/shard_map/all_gather | solution.py:91
  988.6 12.0 convolution_bitcast_fusion
  1007.7 11.2 copy.232
  1019.2 11.1 copy.230
  1031.5 9.4 fusion.201
  1042.8 25.9 reduce-scatter.33.cloned.1.call-done
  1074.4 59.6 %reduce-scatter.31.cloned.1.call-done = f32[160,1280]{1,0:T(8,128)} async-done(((f32[640,1280]{1,0:T(8,128)}), f32[160,1280]{1,0:T(8,128)}) %reduce-scatter.31.cloned.1.call-update) | async-done | bytes 819216
  1138.0 62.0 %reduce-scatter.27.cloned.1.call-done = f32[320,640]{1,0:T(8,128)} async-done(((f32[1280,640]{1,0:T(8,128)}), f32[320,640]{1,0:T(8,128)}) %reduce-scatter.27.cloned.1.call-update) | async-done | bytes 819216 | tf_op jit(solution)/shard_map/reduce_scatter | solution.py:333
  1211.6 159.3 %reduce-scatter.37.cloned.1.call-done = f32[160,3840]{1,0:T(8,128)} async-done(((f32[640,3840]{1,0:T(8,128)}), f32[160,3840]{1,0:T(8,128)}) %reduce-scatter.37.cloned.1.call-update) | async-done | bytes 2457616
  1389.1 152.4 %reduce-scatter.35.cloned.1.call-done = f32[160,3840]{1,0:T(8,128)} async-done(((f32[640,3840]{1,0:T(8,128)}), f32[160,3840]{1,0:T(8,128)}) %reduce-scatter.35.cloned.1.call-update) | async-done | bytes 2457616
  1554.3 158.7 %reduce-scatter.29.cloned.1.call-done = f32[960,640]{1,0:T(8,128)} async-done(((f32[3840,640]{1,0:T(8,128)}), f32[960,640]{1,0:T(8,128)}) %reduce-scatter.29.cloned.1.call-update) | async-done | bytes 2457616 | tf_op jit(solution)/shard_map/reduce_scatter | solution.py:336
  1720.0 9.3 fusion.199
  1733.3 19.1 all-gather.25.cloned.1.call-done
  1755.2 36.2 %all-gather.27.cloned.1.call-done = bf16[640,1280]{1,0:T(8,128)(2,1)} async-done(((bf16[160,1280]{1,0:T(8,128)(2,1)}), bf16[640,1280]{1,0:T(8,128)(2,1)}) %all-gather.27.cloned.1.call-update) | async-done | bytes 1638416 | tf_op jit(solution)/shard_map/all_gather | solution.py:359
  1794.5 36.1 %all-gather.23.cloned.1.call-done = bf16[1280,640]{1,0:T(8,128)(2,1)} async-done(((bf16[320,640]{1,0:T(8,128)(2,1)}), bf16[1280,640]{1,0:T(8,128)(2,1)}) %all-gather.23.cloned.1.call-update) | async-done | bytes 1638416 | tf_op jit(solution)/shard_map/all_gather | solution.py:361
  1870.7 52.6 %all-gather.31.cloned.1.call-done = bf16[640,3840]{1,0:T(8,128)(2,1)} async-done(((bf16[160,3840]{1,0:T(8,128)(2,1)}), bf16[640,3840]{1,0:T(8,128)(2,1)}) %all-gather.31.cloned.1.call-update) | async-done | bytes 4915216 | tf_op jit(solution)/shard_map/all_gather | solution.py:363
  1931.0 85.6 %all-gather.33.cloned.1.call-done = bf16[640,3840]{1,0:T(8,128)(2,1)} async-done(((bf16[160,3840]{1,0:T(8,128)(2,1)}), bf16[640,3840]{1,0:T(8,128)(2,1)}) %all-gather.33.cloned.1.call-update) | async-done | bytes 4915216 | tf_op jit(solution)/shard_map/all_gather | solution.py:362
  2024.4 84.9 %all-gather.29.cloned.1.call-done = bf16[3840,640]{1,0:T(8,128)(2,1)} async-done(((bf16[960,640]{1,0:T(8,128)(2,1)}), bf16[3840,640]{1,0:T(8,128)(2,1)}) %all-gather.29.cloned.1.call-update) | async-done | bytes 4915216 | tf_op jit(solution)/shard_map/all_gather | solution.py:364
  2109.3 9.3 fusion
  2119.3 8.3 convolution_convert_fusion.4
  2127.6 11.4 add_convert_fusion.4
  2139.0 8.1 convolution_convert_fusion.3
  2147.1 11.4 add_convert_fusion.3
  2158.6 8.0 convolution_convert_fusion.2
  2166.6 11.6 add_convert_fusion.2
  2178.2 7.9 convolution_convert_fusion.1
  2186.1 11.6 add_convert_fusion.1
  2197.7 8.1 convolution_convert_fusion
  2205.8 14.0 select_bitcast_fusion
  2257.0 50.0 %all-reduce.75.cloned.1.call-done = (f32[640,640]{1,0:T(8,128)}, f32[640,640]{1,0:T(8,128)}) async-done(((f32[640,640]{1,0:T(8,128)}, f32[640,640]{1,0:T(8,128)}), (f32[640,640]{1,0:T(8,128)}, f32[640,640]{1,0:T(8,128)})) %all-reduce.75.cloned.1.call-update) | async-done | bytes 3276816 | tf_op jit(solution)/shard_map/psum | solution.py:81
  2309.2 63.6 %all-reduce.60 = (f32[4,2,640]{2,1,0:T(2,128)S(1)}, f32[8,1280]{1,0:T(8,128)S(1)}) all-reduce(f32[4,2,640]{2,1,0:T(2,128)S(1)} %fusion.142, f32[8,1280]{1,0:T(8,128)S(1)} %stack.124), channel_id=1, replica_groups=mesh['dp'=4,'row'=2,'col'=4] {'dp','col'}, use_global_device_ids=true, to_apply=%region_22.23 | all-reduce | flops 15360 | bytes 122880 | tf_op jit(solution)/shard_map/psum | solution.py:326
  2390.9 7.9 copy.202
  2406.2 8.2 copy.208
  2423.1 546.2 %all-reduce.77.cloned.1.call-done = (bf16[640,1280]{0,1:T(8,128)(2,1)}, bf16[640,1280]{0,1:T(8,128)(2,1)}, bf16[1280,640]{1,0:T(8,128)(2,1)}, bf16[640,3840]{0,1...) async-done(((bf16[640,1280]{0,1:T(8,128)(2,1)}, bf16[640,1280]{0,1:T(8,128)(2,1)}, bf16[1280,640]{1,0:T(8,128)(2,1)}, bf16[640,3840]{0,1:T(8,128)(2,1)}, ...) | async-done | bytes 19660816 | tf_op jit(solution)/shard_map/psum | solution.py:25
  2983.9 7.9 copy.205
  (694 shorter events, 665.4 us)
Async XLA Ops:
  7.2 78.3 %reduce-scatter.19.cloned.1.call-start = ((), (), s32[]{:S(2)}) async-start(), calls=%async_computation.10 | async-start | bytes 8192000 | tf_op jit(solution)/shard_map/reduce_scatter | solution.py:85
  25.2 208.6 %all-gather.15.cloned.1.call-start = ((), (), s32[]{:S(2)}) async-start(), calls=%async_computation.11 | async-start | bytes 2048000 | tf_op jit(solution)/shard_map/all_gather | solution.py:91
  27.1 64.1 %copy-start.4 = (bf16[2,5,256,256]{2,3,0,1:T(8,128)(2,1)}, bf16[2,5,256,256]{2,3,0,1:T(8,128)(2,1)S(1)}, u32[]{:S(2)}) copy-start(bf16[2,5,256,256]{2,3,0,1:T(8,128)(2,1)S(1)} %copy.183) | copy-start | bytes 3932164
  29.1 61.5 %copy-start.105 = (f32[160]{0:T(256)}, f32[160]{0:T(256)S(1)}, u32[]{:S(2)}) copy-start(f32[160]{0:T(256)S(1)} %get-tuple-element.568) | copy-start | bytes 1924
  29.8 60.9 %copy-start.107 = (f32[160]{0:T(256)}, f32[160]{0:T(256)S(1)}, u32[]{:S(2)}) copy-start(f32[160]{0:T(256)S(1)} %get-tuple-element.564) | copy-start | bytes 1924
  29.8 60.9 %copy-start.109 = (f32[160]{0:T(256)}, f32[160]{0:T(256)S(1)}, u32[]{:S(2)}) copy-start(f32[160]{0:T(256)S(1)} %get-tuple-element.569) | copy-start | bytes 1924
  30.4 60.2 %copy-start.61 = (f32[1280]{0:T(1024)}, f32[1280]{0:T(1024)S(1)}, u32[]{:S(2)}) copy-start(f32[1280]{0:T(1024)S(1)} %get-tuple-element.533) | copy-start | bytes 15364
  30.5 60.2 %copy-start.63 = (f32[1280]{0:T(1024)}, f32[1280]{0:T(1024)S(1)}, u32[]{:S(2)}) copy-start(f32[1280]{0:T(1024)S(1)} %get-tuple-element.534) | copy-start | bytes 15364
  30.5 60.2 %copy-start.65 = (f32[1280]{0:T(1024)}, f32[1280]{0:T(1024)S(1)}, u32[]{:S(2)}) copy-start(f32[1280]{0:T(1024)S(1)} %get-tuple-element.448) | copy-start | bytes 15364
  30.5 61.3 %copy-start.59 = (f32[1280]{0:T(1024)}, f32[1280]{0:T(1024)S(1)}, u32[]{:S(2)}) copy-start(f32[1280]{0:T(1024)S(1)} %get-tuple-element.532) | copy-start | bytes 15364
  86.3 3.0 collective-permute-start
  94.3 74.6 %copy-start.14 = (f32[160,1280]{1,0:T(8,128)}, f32[160,1280]{1,0:T(8,128)S(1)}, u32[]{:S(2)}) copy-start(f32[160,1280]{1,0:T(8,128)S(1)} %get-tuple-element.482) | copy-start | bytes 2457604
  212.5 79.0 %all-reduce.69.cloned.1.call-start = ((), (), s32[]{:S(2)}) async-start(), calls=%async_computation.12 | async-start | bytes 3276800 | tf_op jit(solution)/shard_map/psum | solution.py:81
  238.4 136.6 %reduce-scatter.23.cloned.1.call-start = ((), (), s32[]{:S(2)}) async-start(), calls=%async_computation.15 | async-start | bytes 12288000 | tf_op jit(solution)/shard_map/reduce_scatter | solution.py:85
  247.4 274.7 %reduce-scatter.21.cloned.1.call-start = ((), (), s32[]{:S(2)}) async-start(), calls=%async_computation.13 | async-start | bytes 24576000 | tf_op jit(solution)/shard_map/reduce_scatter | solution.py:85
  293.4 694.6 %copy-start.2 = (f32[640,640]{1,0:T(8,128)}, f32[640,640]{1,0:T(8,128)S(1)}, u32[]{:S(2)}) copy-start(f32[640,640]{1,0:T(8,128)S(1)} %get-tuple-element.443) | copy-start | bytes 4915204
  300.3 370.6 %copy-start.73 = (f32[640]{0:T(1024)}, f32[640]{0:T(1024)S(1)}, u32[]{:S(2)}) copy-start(f32[640]{0:T(1024)S(1)} %add_rsqrt_fusion.1) | copy-start | bytes 7684
  317.1 278.3 %all-gather.19.cloned.1.call-start = ((), (), s32[]{:S(2)}) async-start(), calls=%async_computation.16 | async-start | bytes 12288000 | tf_op jit(solution)/shard_map/all_gather | solution.py:91
  528.7 132.8 %all-reduce.71.cloned.1.call-start = ((), (), s32[]{:S(2)}) async-start(), calls=%async_computation.17 | async-start | bytes 3276800 | tf_op jit(solution)/shard_map/psum | solution.py:81
  608.5 107.0 %reduce-scatter.25.cloned.1.call-start = ((), (), s32[]{:S(2)}) async-start(), calls=%async_computation.18 | async-start | bytes 4096000 | tf_op jit(solution)/shard_map/reduce_scatter | solution.py:85
  677.4 286.4 %all-gather.21.cloned.1.call-start = ((), (), s32[]{:S(2)}) async-start(), calls=%async_computation.19 | async-start | bytes 4096000 | tf_op jit(solution)/shard_map/all_gather | solution.py:91
  927.7 3.1 collective-permute-start.1
  932.4 98.0 %all-gather.17.cloned.1.call-start = ((), (), s32[]{:S(2)}) async-start(), calls=%async_computation.14 | async-start | bytes 6144000 | tf_op jit(solution)/shard_map/all_gather | solution.py:91
  933.0 135.7 %reduce-scatter.33.cloned.1.call-start = ((), (), s32[]{:S(2)}) async-start(), calls=%async_computation.30 | async-start | bytes 4096000
  977.1 156.9 %reduce-scatter.31.cloned.1.call-start = ((), (), s32[]{:S(2)}) async-start(), calls=%async_computation.29 | async-start | bytes 4096000
  981.7 218.3 %reduce-scatter.27.cloned.1.call-start = ((), (), s32[]{:S(2)}) async-start(), calls=%async_computation.21 | async-start | bytes 4096000 | tf_op jit(solution)/shard_map/reduce_scatter | solution.py:333
  987.9 382.9 %reduce-scatter.37.cloned.1.call-start = ((), (), s32[]{:S(2)}) async-start(), calls=%async_computation.32 | async-start | bytes 12288000
  1019.0 522.5 %reduce-scatter.35.cloned.1.call-start = ((), (), s32[]{:S(2)}) async-start(), calls=%async_computation.31 | async-start | bytes 12288000
  1030.3 682.6 %reduce-scatter.29.cloned.1.call-start = ((), (), s32[]{:S(2)}) async-start(), calls=%async_computation.22 | async-start | bytes 12288000 | tf_op jit(solution)/shard_map/reduce_scatter | solution.py:336
  1040.9 711.5 %all-gather.25.cloned.1.call-start = ((), (), s32[]{:S(2)}) async-start(), calls=%async_computation.24 | async-start | bytes 2048000 | tf_op jit(solution)/shard_map/all_gather | solution.py:360
  1073.9 717.5 %all-gather.27.cloned.1.call-start = ((), (), s32[]{:S(2)}) async-start(), calls=%async_computation.25 | async-start | bytes 2048000 | tf_op jit(solution)/shard_map/all_gather | solution.py:359
  1138.0 692.6 %all-gather.23.cloned.1.call-start = ((), (), s32[]{:S(2)}) async-start(), calls=%async_computation.23 | async-start | bytes 2048000 | tf_op jit(solution)/shard_map/all_gather | solution.py:361
  1202.5 720.8 %all-gather.31.cloned.1.call-start = ((), (), s32[]{:S(2)}) async-start(), calls=%async_computation.27 | async-start | bytes 6144000 | tf_op jit(solution)/shard_map/all_gather | solution.py:363
  1386.0 630.6 %all-gather.33.cloned.1.call-start = ((), (), s32[]{:S(2)}) async-start(), calls=%async_computation.28 | async-start | bytes 6144000 | tf_op jit(solution)/shard_map/all_gather | solution.py:362
  1554.2 163.6 %copy-start.19 = (bf16[160,2,1280]{2,0,1:T(8,128)(2,1)S(1)}, bf16[160,2,1280]{2,0,1:T(8,128)(2,1)}, u32[]{:S(2)}) copy-start(bf16[160,2,1280]{2,0,1:T(8,128)(2,1)} %copy-done.18) | copy-start | bytes 2457604
  1554.2 163.6 %copy-start.30 = (bf16[160,5,256]{2,1,0:T(8,128)(2,1)S(1)}, bf16[160,5,256]{2,1,0:T(8,128)(2,1)}, u32[]{:S(2)}) copy-start(bf16[160,5,256]{2,1,0:T(8,128)(2,1)} %copy-done.29) | copy-start | bytes 1228804
  1554.2 555.1 %all-gather.29.cloned.1.call-start = ((), (), s32[]{:S(2)}) async-start(), calls=%async_computation.26 | async-start | bytes 6144000 | tf_op jit(solution)/shard_map/all_gather | solution.py:364
  1717.7 524.2 %all-reduce.73.cloned.1.call-start = ((), (), s32[]{:S(2)}) async-start(), calls=%async_computation.20 | async-start | bytes 5242880 | tf_op jit(solution)/shard_map/psum | solution.py:326
  1719.9 587.1 %all-reduce.75.cloned.1.call-start = ((), (), s32[]{:S(2)}) async-start(), calls=%async_computation.33 | async-start | bytes 6553600 | tf_op jit(solution)/shard_map/psum | solution.py:81
  1733.2 1236.0 %all-reduce.77.cloned.1.call-start = ((), (), s32[]{:S(2)}) async-start(), calls=%async_computation.34 | async-start | bytes 39321600 | tf_op jit(solution)/shard_map/psum | solution.py:25
  2253.4 53.6 %copy-start.79 = (f32[640]{0:T(1024)S(1)}, f32[640]{0:T(1024)}, u32[]{:S(2)}) copy-start(f32[640]{0:T(1024)} %copy-done.77) | copy-start | bytes 7684
  2253.4 53.6 %copy-start.82 = (f32[640]{0:T(1024)S(1)}, f32[640]{0:T(1024)}, u32[]{:S(2)}) copy-start(f32[640]{0:T(1024)} %copy-done.80) | copy-start | bytes 7684
  2257.0 115.9 %copy-start.113 = (f32[2,640]{1,0:T(2,128)S(1)}, f32[2,640]{1,0:T(2,128)}, u32[]{:S(2)}) copy-start(f32[2,640]{1,0:T(2,128)} %param.31) | copy-start | bytes 15364
  2257.0 122.6 %copy-start.67 = (f32[8,1280]{1,0:T(8,128)S(1)}, f32[8,1280]{1,0:T(8,128)}, u32[]{:S(2)}) copy-start(f32[8,1280]{1,0:T(8,128)} %param.33) | copy-start | bytes 122884
  2257.0 122.8 %copy-start.76 = (f32[640]{0:T(1024)S(1)}, f32[640]{0:T(1024)}, u32[]{:S(2)}) copy-start(f32[640]{0:T(1024)} %copy-done.75) | copy-start | bytes 7684
  2257.0 122.8 %copy-start.93 = (f32[2,640]{1,0:T(2,128)S(1)}, f32[2,640]{1,0:T(2,128)}, u32[]{:S(2)}) copy-start(f32[2,640]{1,0:T(2,128)} %param.24) | copy-start | bytes 15364
  2257.0 123.4 %copy-start.3 = (f32[640,640]{1,0:T(8,128)S(1)}, f32[640,640]{1,0:T(8,128)}, u32[]{:S(2)}) copy-start(f32[640,640]{1,0:T(8,128)} %copy-done.2) | copy-start | bytes 4915204
  2423.1 547.6 %copy-start.36 = (bf16[1,160,1280]{1,2,0:T(8,128)(2,1)S(1)}, bf16[1,160,1280]{1,2,0:T(8,128)(2,1)}, u32[]{:S(2)}) copy-start(bf16[1,160,1280]{1,2,0:T(8,128)(2,1)} %copy.239) | copy-start | bytes 1228804
  (98 other events, 733.7 us)
Sparse Core Ops, SparseCore 0:
  25.3 60.1 reduce-scatter.18
  212.6 21.2 all-gather.14
  238.5 52.9 all-reduce.68
  293.9 81.0 reduce-scatter.22
  377.5 144.5 reduce-scatter.20
  528.9 66.4 all-gather.18
  608.6 52.9 all-reduce.70
  677.6 37.8 reduce-scatter.24
  932.6 31.2 all-gather.20
  965.9 38.5 all-gather.16
  1007.5 61.1 reduce-scatter.32
  1071.5 62.4 reduce-scatter.30
  1137.6 62.3 reduce-scatter.26
  1202.4 168.4 reduce-scatter.36
  1373.1 168.4 reduce-scatter.34
  1544.5 168.4 reduce-scatter.28
  1715.0 37.3 all-gather.24
  1754.3 37.0 all-gather.26
  1793.5 37.0 all-gather.22
  1832.6 90.7 all-gather.30
  1925.5 91.0 all-gather.32
  2018.2 91.0 all-gather.28
  2113.5 100.8 all-reduce.72
  2217.8 89.1 all-reduce.74
  2311.2 658.0 all-reduce.76
where the time goes:
time: 3030 us; the launch traced here: 3000 us
  waiting for transfers between devices  2010 us (66%)
  local copies, waits for them, and re-layouts  429 us (14%)
  matrix products  238 us (8%)
  other arithmetic  188 us (6%)
  blocking collectives  111 us (4%)
    psum x1, waiting for transfers between devices, broadcast(): return lax.psum(kept, axis)  546 us
    unnamed x29, waiting for transfers between devices  398 us
    reduce_scatter x4, waiting for transfers between devices, owner_rows(): lax.psum_scatter(term(jnp.int32(0), count * lax.axis_size('col')), 'col',...  269 us
    reduce_scatter x1, waiting for transfers between devices, shards(): lax.psum_scatter(contract_grad, 'dp', scatter_dimension=0, tiled=True)  159 us
    psum x3, waiting for transfers between devices, feature_total(): return lax.psum(values, 'row')  147 us
    all_gather x4, waiting for transfers between devices, all_tokens(): return lax.all_gather(piece, 'col', axis=0, tiled=True)  118 us
    unnamed x270, local copies, waits for them, and re-layouts  117 us
    slice x53, local copies, waits for them, and re-layouts, shards(): lax.associative_scan(link, (shifted_decay, grad_state), reverse=True, axi...  109 us
  transfers between devices with their start and end apart: 27, of which 24 were waited for; matrix products, arithmetic and copies ran while one was open for 15% of the time, Pallas kernels for 0%

commit v1 on v0

--- a/solution.py
+++ b/solution.py
@@ -1,6 +1,10 @@
+import functools
+
 import jax
 import jax.numpy as jnp
 from jax import lax
+from jax.experimental import pallas as pl
+from jax.experimental.pallas import tpu as pltpu
 from jax.sharding import PartitionSpec as P
 
 CONV = 4
@@ -33,7 +37,8 @@
 
 def prefix(value, axis, combine, identity, reverse):
     count, here = (lax.axis_size(axis), lax.axis_index(axis))
-    everything = jax.tree.map(lambda part: lax.all_gather(part, axis), value)
+    joined = lax.all_gather(jnp.stack(value), axis)
+    everything = tuple(joined[:, k] for k in range(len(value)))
     start = jax.tree.map(
         lambda part, zero: jnp.broadcast_to(jnp.asarray(zero, part.dtype), part.shape),
         value,
@@ -73,22 +78,533 @@
     return (first[0] * second[0], second[0] * first[1] + second[1])
 
 
+def scan_kernel(reverse, decay_ref, value_ref, prod_ref, sum_ref):
+    rows, lanes = decay_ref.shape
+    groups = rows // 8
+
+    def lap(k, carry):
+        base = pl.multiple_of((groups - 1 - k if reverse else k) * 8, 8)
+        decay = decay_ref[pl.ds(base, 8), :]
+        value = value_ref[pl.ds(base, 8), :]
+        prod, total = carry
+        prods, totals = [None] * 8, [None] * 8
+        for j in range(7, -1, -1) if reverse else range(8):
+            prod = decay[j : j + 1] * prod
+            total = decay[j : j + 1] * total + value[j : j + 1]
+            prods[j], totals[j] = prod, total
+        prod_ref[pl.ds(base, 8), :] = jnp.concatenate(prods, axis=0)
+        sum_ref[pl.ds(base, 8), :] = jnp.concatenate(totals, axis=0)
+        return (prod, total)
+
+    start = (jnp.ones((1, lanes), jnp.float32), jnp.zeros((1, lanes), jnp.float32))
+    lax.fori_loop(0, groups, lap, start)
+
+
+def linear_scan(decay, value, reverse):
+    shape = jax.ShapeDtypeStruct(decay.shape, jnp.float32)
+    return pl.pallas_call(
+        functools.partial(scan_kernel, reverse),
+        out_shape=(shape, shape),
+        compiler_params=pltpu.CompilerParams(vmem_limit_bytes=16 * 1024 * 1024),
+    )(decay, value)
+
+
+MESH = pl.DeviceIdType.MESH
+MIB = 1024 * 1024
+
+
+def col_places():
+    me = lax.axis_index("col")
+    near_bit = lax.rem(me, 2)
+    far_bit = lax.div(me, 2)
+    return (me, near_bit, far_bit, me + 1 - 2 * near_bit, lax.rem(me + 2, 4))
+
+
+def greet(axis_places):
+    barrier = pltpu.get_barrier_semaphore()
+    for axis, place in axis_places:
+        pl.semaphore_signal(barrier, inc=1, device_id={axis: place}, device_id_type=MESH)
+    pl.semaphore_wait(barrier, len(axis_places))
+
+
+def dot_nn(left, right):
+    return lax.dot_general(
+        left, right, (((1,), (0,)), ((), ())), preferred_element_type=jnp.float32
+    )
+
+
+def dot_nt(left, right):
+    return lax.dot_general(
+        left, right, (((1,), (1,)), ((), ())), preferred_element_type=jnp.float32
+    )
+
+
+def columns_of(j, width, per):
+    return (lax.div(j, per), pl.ds(pl.multiple_of(lax.rem(j, per) * width, width), width))
+
+
+def spread_kernel(
+    flip, lhs, w, out, wbuf, send1, recv1, own, send2, recv2, wsem, s1s, s1r, s2s, s2r
+):
+    chunks, rows, width = send2.shape
+    per = out.shape[2] // width
+    me, near_bit, far_bit, near, far = col_places()
+    depth = lhs.shape[3]
+
+    def w_copy(j):
+        k, cols = columns_of(j, width, per)
+        return pltpu.make_async_copy(
+            w.at[cols, :] if flip else w.at[k, :, cols], wbuf.at[j], wsem.at[j]
+        )
+
+    def near_copy(j):
+        return pltpu.make_async_remote_copy(
+            src_ref=send1.at[j],
+            dst_ref=recv1.at[j],
+            send_sem=s1s.at[j],
+            recv_sem=s1r.at[j],
+            device_id={"col": near},
+            device_id_type=MESH,
+        )
+
+    def far_copy(j):
+        return pltpu.make_async_remote_copy(
+            src_ref=send2.at[j],
+            dst_ref=recv2.at[j],
+            send_sem=s2s.at[j],
+            recv_sem=s2r.at[j],
+            device_id={"col": far},
+            device_id_type=MESH,
+        )
+
+    def loop(count, act):
+        def lap(j, carry):
+            act(j)
+            return carry
+
+        lax.fori_loop(0, count, lap, 0)
+
+    loop(chunks, lambda j: w_copy(j).start())
+    greet((("col", near), ("col", far)))
+    dot = dot_nt if flip else dot_nn
+
+    def first(j):
+        w_copy(j).wait()
+        part = wbuf[j]
+        theirs = dot(lhs[:, 1 - near_bit].reshape(2 * rows, depth), part)
+        send1[j] = theirs.astype(jnp.bfloat16).reshape(2, rows, width)
+        near_copy(j).start()
+        mine = dot(lhs[:, near_bit].reshape(2 * rows, depth), part)
+        own[j] = mine.reshape(2, rows, width)
+
+    def second(j):
+        near_copy(j).wait_recv()
+        going = own[j, 1 - far_bit] + recv1[j, 1 - far_bit].astype(jnp.float32)
+        send2[j] = going.astype(jnp.bfloat16)
+        far_copy(j).start()
+        own[j, far_bit] = own[j, far_bit] + recv1[j, far_bit].astype(jnp.float32)
+
+    def third(j):
+        far_copy(j).wait_recv()
+        k, cols = columns_of(j, width, per)
+        out[k, :, cols] = own[j, far_bit] + recv2[j].astype(jnp.float32)
+
+    first(0)
+
+    def both(j):
+        first(j + 1)
+        second(j)
+
+    loop(chunks - 1, both)
+    second(chunks - 1)
+    loop(chunks, third)
+
+    def drain(j):
+        near_copy(j).wait_send()
+        far_copy(j).wait_send()
+
+    loop(chunks, drain)
+
+
+def spread_product(lhs, w, flip, width, collective):
+    tokens, depth = lhs.shape
+    rows = tokens // 4
+    pairs = 1 if flip else w.shape[0]
+    total = w.shape[0] if flip else w.shape[2]
+    chunks = pairs * total // width
+    tile = (width, depth) if flip else (depth, width)
+    bf16, f32 = jnp.bfloat16, jnp.float32
+    return pl.pallas_call(
+        functools.partial(spread_kernel, flip),
+        out_shape=jax.ShapeDtypeStruct((pairs, rows, total), f32),
+        in_specs=[pl.BlockSpec(memory_space=pltpu.VMEM), pl.BlockSpec(memory_space=pl.ANY)],
+        out_specs=pl.BlockSpec(memory_space=pltpu.VMEM),
+        scratch_shapes=[
+            pltpu.VMEM((chunks,) + tile, bf16),
+            pltpu.VMEM((chunks, 2, rows, width), bf16),
+            pltpu.VMEM((chunks, 2, rows, width), bf16),
+            pltpu.VMEM((chunks, 2, rows, width), f32),
+            pltpu.VMEM((chunks, rows, width), bf16),
+            pltpu.VMEM((chunks, rows, width), bf16),
+        ]
+        + [pltpu.SemaphoreType.DMA((chunks,))] * 5,
+        compiler_params=pltpu.CompilerParams(
+            collective_id=collective, has_side_effects=True, vmem_limit_bytes=56 * MIB
+        ),
+    )(lhs.reshape(2, 2, rows, depth), w)
+
+
+def meet_kernel(flip, grad_mode, *refs):
+    if grad_mode:
+        piece, w, side, prod, grad_out = refs[:5]
+        refs = refs[5:]
+    else:
+        piece, w, all_out, prod = refs[:4]
+        refs = refs[4:]
+    wbuf, buf, acc, sendx, recvx, wsem, osem, ns, nr, fs, fr, rs, rr, xs, xr = refs[:15]
+    if grad_mode:
+        stage, gsem = refs[15:]
+    chunks, _, _, rows, width = buf.shape
+    per = piece.shape[2] // width
+    me, near_bit, far_bit, near, far = col_places()
+    across = 1 - lax.axis_index("row")
+    f32, bf16 = jnp.float32, jnp.bfloat16
+
+    def w_copy(j):
+        k, cols = columns_of(j, width, per)
+        return pltpu.make_async_copy(
+            w.at[k, :, cols] if flip else w.at[cols, :], wbuf.at[j], wsem.at[j]
+        )
+
+    def move(j, source, near_place, far_place, sems, target):
+        return pltpu.make_async_remote_copy(
+            src_ref=source,
+            dst_ref=buf.at[j, far_place, near_place],
+            send_sem=sems[0].at[j],
+            recv_sem=sems[1].at[j],
+            device_id={"col": target},
+            device_id_type=MESH,
+        )
+
+    def piece_at(j):
+        k, cols = columns_of(j, width, per)
+        return piece.at[k, :, cols]
+
+    def far_copy(j):
+        return move(j, piece_at(j), near_bit, far_bit, (fs, fr), far)
+
+    def near_copy(j):
+        return move(j, piece_at(j), near_bit, far_bit, (ns, nr), near)
+
+    def relay(j):
+        return move(j, buf.at[j, 1 - far_bit, near_bit], near_bit, 1 - far_bit, (rs, rr), near)
+
+    def out_copy(j):
+        k, cols = columns_of(j, width, per)
+        return pltpu.make_async_copy(buf.at[j], all_out.at[k, :, :, :, cols], osem.at[j])
+
+    def cross(half):
+        return pltpu.make_async_remote_copy(
+            src_ref=sendx.at[half],
+            dst_ref=recvx.at[half],
+            send_sem=xs.at[half],
+            recv_sem=xr.at[half],
+            device_id={"row": across},
+            device_id_type=MESH,
+        )
+
+    def loop(count, act):
+        def lap(j, carry):
+            act(j)
+            return carry
+
+        lax.fori_loop(0, count, lap, 0)
+
+    loop(chunks, lambda j: w_copy(j).start())
+    greet((("col", near), ("col", far), ("row", across)))
+
+    def begin(j):
+        far_copy(j).start()
+        near_copy(j).start()
+        k, cols = columns_of(j, width, per)
+        buf[j, far_bit, near_bit] = piece[k, :, cols]
+
+    loop(chunks, begin)
+    acc[...] = jnp.zeros_like(acc)
+    dot = dot_nt if flip else dot_nn
+
+    def add(j, half):
+        both = buf[j, half].reshape(2 * rows, width)
+        acc[half] = acc[half] + dot(both, wbuf[j])
+
+    def here(j):
+        near_copy(j).wait_recv()
+        w_copy(j).wait()
+        add(j, far_bit)
+
+    loop(chunks, here)
+    sendx[far_bit] = acc[far_bit].astype(bf16)
+    cross(far_bit).start()
+
+    def grad_copy(j):
+        return grad_moves(j)
+
+    if grad_mode == "wide":
+        parts = grad_out.shape[0]
+
+        def grad_moves(j):
+            k, cols = columns_of(j, width, per)
+            return pltpu.make_async_copy(
+                stage.at[lax.rem(j, 2)], grad_out.at[:, k, :, cols], gsem.at[lax.rem(j, 2)]
+            )
+
+        def grad_part(j):
+            block = buf[j].reshape(4 * rows, width)
+            total = dot_nn(side[...], block).astype(bf16)
+            stage[lax.rem(j, 2)] = total.reshape(stage.shape[1:])
+
+    if grad_mode == "tall":
+
+        def grad_moves(j):
+            return pltpu.make_async_copy(
+                stage.at[lax.rem(j, 2)],
+                grad_out.at[pl.ds(pl.multiple_of(j * width, width), width), :],
+                gsem.at[lax.rem(j, 2)],
+            )
+
+        def grad_part(j):
+            block = buf[j].reshape(4 * rows, width)
+            stage[lax.rem(j, 2)] = dot_nn(block.T, side[...]).astype(bf16)
+
+    def pass_on(j):
+        far_copy(j).wait_recv()
+        relay(j).start()
+
+    def there(j):
+        relay(j).wait_recv()
+        if not grad_mode:
+            out_copy(j).start()
+        add(j, 1 - far_bit)
+        if grad_mode:
+
+            @pl.when(j >= 2)
+            def _():
+                grad_moves(j - 2).wait()
+
+            grad_part(j)
+            grad_moves(j).start()
+
+    pass_on(0)
+
+    def both(j):
+        pass_on(j + 1)
+        there(j)
+
+    loop(chunks - 1, both)
+    there(chunks - 1)
+    sendx[1 - far_bit] = acc[1 - far_bit].astype(bf16)
+    cross(1 - far_bit).start()
+
+    def settle(half):
+        cross(half).wait_recv()
+        prod[half] = sendx[half].astype(f32) + recvx[half].astype(f32)
+
+    settle(far_bit)
+    settle(1 - far_bit)
+
+    def drain(j):
+        near_copy(j).wait_send()
+        far_copy(j).wait_send()
+        relay(j).wait_send()
+        if not grad_mode:
+            out_copy(j).wait()
+
+    loop(chunks, drain)
+    cross(far_bit).wait_send()
+    cross(1 - far_bit).wait_send()
+    if grad_mode:
+        for j in range(max(0, chunks - 2), chunks):
+            grad_moves(j).wait()
+
+
+def meet_product(piece, w, flip, width, collective, side=None, grad_mode=None, parts=1):
+    pairs, rows, total = piece.shape
+    features = w.shape[1]
+    chunks = pairs * total // width
+    tile = (features, width) if flip else (width, features)
+    bf16, f32 = jnp.bfloat16, jnp.float32
+    inputs, in_specs = (
+        [piece, w],
+        [pl.BlockSpec(memory_space=pltpu.VMEM), pl.BlockSpec(memory_space=pl.ANY)],
+    )
+    shapes = [jax.ShapeDtypeStruct((2, 2 * rows, features), f32)]
+    out_specs = [pl.BlockSpec(memory_space=pltpu.VMEM)]
+    scratch = [
+        pltpu.VMEM((chunks,) + tile, bf16),
+        pltpu.VMEM((chunks, 2, 2, rows, width), bf16),
+        pltpu.VMEM((2, 2 * rows, features), f32),
+        pltpu.VMEM((2, 2 * rows, features), bf16),
+        pltpu.VMEM((2, 2 * rows, features), bf16),
+    ]
+    scratch += [pltpu.SemaphoreType.DMA((chunks,))] * 8 + [pltpu.SemaphoreType.DMA((2,))] * 2
+    if grad_mode:
+        inputs.append(side)
+        in_specs.append(pl.BlockSpec(memory_space=pltpu.VMEM))
+        out_specs.append(pl.BlockSpec(memory_space=pl.ANY))
+        if grad_mode == "wide":
+            shape = (parts, pairs, side.shape[0] // parts, total)
+            stage = (2, parts, side.shape[0] // parts, width)
+        else:
+            shape = (total, side.shape[1])
+            stage = (2, width, side.shape[1])
+        shapes.append(jax.ShapeDtypeStruct(shape, bf16))
+        scratch += [pltpu.VMEM(stage, bf16), pltpu.SemaphoreType.DMA((2,))]
+    else:
+        shapes.insert(0, jax.ShapeDtypeStruct((pairs, 2, 2, rows, total), bf16))
+        out_specs.insert(0, pl.BlockSpec(memory_space=pl.ANY))
+    result = pl.pallas_call(
+        functools.partial(meet_kernel, flip, grad_mode),
+        out_shape=tuple(shapes),
+        in_specs=in_specs,
+        out_specs=out_specs,
+        scratch_shapes=scratch,
+        compiler_params=pltpu.CompilerParams(
+            collective_id=collective, has_side_effects=True, vmem_limit_bytes=56 * MIB
+        ),
+    )(*inputs)
+    if grad_mode:
+        return (result[0].reshape(4 * rows, features), result[1])
+    return (result[0].reshape(pairs, 4 * rows, total), result[1].reshape(4 * rows, features))
+
+
+def block_steps(x, acc, gram, poly):
+    side, total = x.shape
+    step = 256
+    count = total // step
+    span = 1280 if total % 1280 == 0 else step
+    f32, bf16 = jnp.float32, jnp.bfloat16
+
+    def tile(k, size):
+        return pl.ds(pl.multiple_of(k * size, size), size)
+
+    def square(k, total):
+        values = x[:, tile(k, step)].astype(f32)
+        return total + jnp.sum(values * values, axis=0, keepdims=True)
+
+    sums = lax.fori_loop(0, count, square, jnp.zeros((1, step), f32))
+    norm = jnp.sqrt(jnp.sum(sums, axis=1, keepdims=True)) + eps_frob
+
+    def divide(k, carry):
+        x[:, tile(k, step)] = (x[:, tile(k, step)].astype(f32) / norm).astype(bf16)
+        return carry
+
+    lax.fori_loop(0, count, divide, 0)
+
+    def lap(k, carry):
+        acc[...] = jnp.zeros_like(acc)
+
+        def add(j, inner):
+            block = x[:, tile(j, span)]
+            acc[:step, :step] = acc[:step, :step] + dot_nt(block[:step], block[:step])
+            acc[step:, :] = acc[step:, :] + dot_nt(block[step:], block)
+            return inner
+
+        lax.fori_loop(0, total // span, add, 0)
+        acc[:step, step:] = acc[step:, :step].T
+        low = acc[...].astype(bf16)
+        gram[...] = low
+        square_gram = dot_nn(low, gram[...])
+        poly[...] = (poly_second * low.astype(f32) + poly_third * square_gram).astype(bf16)
+
+        def advance(j, inner):
+            block = x[:, tile(j, span)]
+            fresh = poly_first * block.astype(f32) + dot_nn(poly[...], block)
+            x[:, tile(j, span)] = fresh.astype(bf16)
+            return inner
+
+        lax.fori_loop(0, total // span, advance, 0)
+        return carry
+
+    lax.fori_loop(0, 5, lap, 0)
+
+
+def work_space(side):
+    return [
+        pltpu.VMEM((side, side), jnp.float32),
+        pltpu.VMEM((side, side), jnp.bfloat16),
+        pltpu.VMEM((side, side), jnp.bfloat16),
+    ]
+
+
+def gates_kernel(conv, first, second, out, full, came, send_sem, recv_sem):
+    me = lax.axis_index("col")
+    count = out.shape[0]
+    greet([("col", lax.rem(me + step, 4)) for step in range(1, 4)])
+    for k, grads in enumerate((first, second)):
+        for head in range(conv.shape[1] // HS):
+            columns = slice(head * HS, (head + 1) * HS)
+            block = dot_nn(conv[:, columns].T, grads[:, columns])
+            full[k * HS : (k + 1) * HS, columns] = block.astype(jnp.bfloat16)
+
+    def part(place):
+        return full.at[pl.ds(pl.multiple_of(place * count, count), count)]
+
+    def copy(step):
+        target = lax.rem(me + step, 4)
+        return pltpu.make_async_remote_copy(
+            src_ref=part(target),
+            dst_ref=came.at[step - 1],
+            send_sem=send_sem.at[step - 1],
+            recv_sem=recv_sem.at[step - 1],
+            device_id={"col": target},
+            device_id_type=MESH,
+        )
+
+    for step in range(1, 4):
+        copy(step).start()
+    total = part(me)[...].astype(jnp.float32)
+    for step in range(1, 4):
+        copy(step).wait_recv()
+        total = total + came[step - 1].astype(jnp.float32)
+    out[...] = total.astype(jnp.bfloat16)
+    for step in range(1, 4):
+        copy(step).wait_send()
+
+
+def gates_product(conv, first, second):
+    lanes = conv.shape[1]
+    count = 2 * HS // 4
+    bf16 = jnp.bfloat16
+    return pl.pallas_call(
+        gates_kernel,
+        out_shape=jax.ShapeDtypeStruct((count, lanes), bf16),
+        in_specs=[pl.BlockSpec(memory_space=pltpu.VMEM)] * 3,
+        out_specs=pl.BlockSpec(memory_space=pltpu.VMEM),
+        scratch_shapes=[
+            pltpu.VMEM((2 * HS, lanes), bf16),
+            pltpu.VMEM((3, count, lanes), bf16),
+            pltpu.SemaphoreType.DMA((3,)),
+            pltpu.SemaphoreType.DMA((3,)),
+        ],
+        compiler_params=pltpu.CompilerParams(
+            collective_id=12, has_side_effects=True, vmem_limit_bytes=16 * MIB
+        ),
+    )(conv, first, second)
+
+
 def token_total(values):
     return lax.psum(values, "col")
 
 
-def feature_total(values):
-    return lax.psum(values, "row")
-
-
-def owner_rows(term, count):
-    return lax.psum_scatter(
-        term(jnp.int32(0), count * lax.axis_size("col")), "col", scatter_dimension=0, tiled=True
-    )
-
-
-def all_tokens(piece):
-    return lax.all_gather(piece, "col", axis=0, tiled=True)
+def dp_sum(grad):
+    low = grad.astype(jnp.bfloat16)
+    return lax.psum_scatter(low, "dp", scatter_dimension=0, tiled=True).astype(jnp.float32)
+
+
+def pair_sum(grad, dp_count):
+    if grad.shape[0] == dp_count:
+        return lax.psum_scatter(grad, "dp", scatter_dimension=0)
+    return lax.psum_scatter(grad[0], "dp", scatter_dimension=1, tiled=True)
 
 
 def owner_send(block, root):
@@ -139,6 +655,288 @@
             kept = jnp.where(dp_place == number % dp_count, done, jnp.zeros_like(done))
             results[number] = kept.T if turn else kept
     return results
+
+
+def dp_moves(moves, sems):
+    local_sem, send_sem, recv_sem = sems
+    me = lax.axis_index("dp")
+
+    def remote(k, sender, target):
+        pairs, source, destination = moves[k]
+        return pltpu.make_async_remote_copy(
+            src_ref=source(sender, target),
+            dst_ref=destination(sender, target),
+            send_sem=send_sem.at[k, target],
+            recv_sem=recv_sem.at[k, sender],
+            device_id={"dp": target},
+            device_id_type=MESH,
+        )
+
+    def local(k, place):
+        pairs, source, destination = moves[k]
+        return pltpu.make_async_copy(
+            source(place, place), destination(place, place), local_sem.at[k]
+        )
+
+    def each(chosen, act):
+        for k in chosen:
+            for sender, target in moves[k][0]:
+                act(k, sender, target)
+
+    def start_one(k, sender, target):
+        @pl.when(me == sender)
+        def _():
+            if sender == target:
+                local(k, sender).start()
+            else:
+                remote(k, sender, target).start()
+
+    def arrive_one(k, sender, target):
+        @pl.when(me == target)
+        def _():
+            if sender == target:
+                local(k, sender).wait()
+            else:
+                remote(k, sender, target).wait_recv()
+
+    def sent_one(k, sender, target):
+        if sender != target:
+
+            @pl.when(me == sender)
+            def _():
+                remote(k, sender, target).wait_send()
+
+    return (
+        lambda *chosen: each(chosen, start_one),
+        lambda *chosen: each(chosen, arrive_one),
+        lambda *chosen: each(chosen, sent_one),
+    )
+
+
+def rows_at(ref, place):
+    def pick(sender, target):
+        index = sender if place == "sender" else target
+        count = ref.shape[0] // 4
+        return ref.at[pl.ds(index * count, count)]
+
+    return pick
+
+
+def entry(ref, place):
+    return lambda sender, target: ref.at[sender if place == "sender" else target]
+
+
+def whole(ref):
+    return lambda sender, target: ref
+
+
+def to_owner(owner):
+    return [(sender, owner) for sender in ((owner + step) % 4 for step in range(4))]
+
+
+def from_owner(owner):
+    return [(owner, target) for target in ((owner + step) % 4 for step in range(4))]
+
+
+SMALL_OWNER, CON_OWNER, GATE_OWNER, UP_OWNER = (0, 1, 2, 3)
+
+
+def pieces_at_owner(e0, e1, con, later):
+    me = lax.axis_index("dp")
+    rows = e0.shape[0]
+    packed = jnp.concatenate(
+        [con[k * rows : (k + 1) * rows] for k in range(con.shape[0] // rows)], axis=1
+    )
+
+    def piece_for(owner):
+        return jnp.where(owner == GATE_OWNER, e0, jnp.where(owner == UP_OWNER, e1, packed))
+
+    leaving = [piece_for(lax.rem(me + step, 4)) for step in range(4)]
+    leaving, later = lax.optimization_barrier((leaving, later))
+    pieces = leaving[:1]
+    for step in range(1, 4):
+        pairs = [(sender, (sender + step) % 4) for sender in range(4)]
+        pairs = [pair for pair in pairs if pair[1] != SMALL_OWNER]
+        pieces.append(lax.ppermute(leaving[step], "dp", pairs))
+    return (pieces, later)
+
+
+def share_parts(axis, buf, send_sem, recv_sem):
+    me = lax.axis_index(axis)
+
+    def copy(step):
+        return pltpu.make_async_remote_copy(
+            src_ref=buf.at[me],
+            dst_ref=buf.at[me],
+            send_sem=send_sem.at[step],
+            recv_sem=recv_sem.at[step],
+            device_id={axis: lax.rem(me + step, 4)},
+            device_id_type=MESH,
+        )
+
+    def start(value):
+        buf[me] = value
+        for step in range(1, 4):
+            copy(step).start()
+
+    def arrive():
+        for step in range(1, 4):
+            copy(step).wait_recv()
+
+    def finish():
+        for step in range(1, 4):
+            copy(step).wait_send()
+
+    return (start, arrive, finish)
+
+
+def tail_kernel(*refs):
+    large, (b0, b1, out) = refs[:4], refs[4:7]
+    gates_piece, col_part, dp_part = refs[7:10]
+    e0_o, e1_o, con_o, b0_o, b1_o, out_o, gates_o, col_o, dp_o = refs[10:19]
+    x, packed, pieces, first, second, third, out_v, acc, gram, poly, load_sem = refs[19:30]
+    col_buf, dp_buf, gates_dp, gates_col = refs[30:34]
+    shares = [
+        share_parts("col", col_buf, *refs[34:36]),
+        share_parts("dp", dp_buf, *refs[36:38]),
+        share_parts("dp", gates_dp, *refs[38:40]),
+        share_parts("col", gates_col, *refs[40:42]),
+    ]
+    sems = refs[42:]
+    place = lax.axis_index("col")
+    me = lax.axis_index("dp")
+    small = out.shape[0]
+    width = pieces.shape[1]
+    side = x.shape[0]
+    rows = side // 4
+    moves = [
+        (to_owner(SMALL_OWNER), whole(b0), rows_at(first, "sender")),
+        (to_owner(SMALL_OWNER), whole(b1), rows_at(second, "sender")),
+        (to_owner(SMALL_OWNER), whole(out), entry(out_v, "sender")),
+        (from_owner(GATE_OWNER), rows_at(x, "target"), whole(e0_o)),
+        (from_owner(UP_OWNER), rows_at(x, "target"), whole(e1_o)),
+        (from_owner(CON_OWNER), entry(pieces, "target"), whole(con_o)),
+        (from_owner(SMALL_OWNER), rows_at(first, "target"), whole(b0_o)),
+        (from_owner(SMALL_OWNER), rows_at(second, "target"), whole(b1_o)),
+        (from_owner(SMALL_OWNER), entry(out_v, "target"), whole(out_o)),
+    ]
+    start, arrive, sent = dp_moves(moves, sems)
+    greet(
+        [("dp", lax.rem(me + step, 4)) for step in range(1, 4)]
+        + [("col", lax.rem(place + step, 4)) for step in range(1, 4)]
+    )
+    shares[0][0](col_part[...])
+    shares[2][0](gates_piece[...])
+    start(0, 1, 2)
+    shares[0][1]()
+    summed = col_buf[0] + col_buf[1] + col_buf[2] + col_buf[3]
+    col_o[...] = summed
+    shares[1][0](jnp.concatenate([summed[:8], dp_part[...]], axis=0))
+    shares[2][1]()
+    shares[3][0](gates_dp[...].reshape(gates_col.shape[1:]))
+
+    def load(owner, target):
+        copies = [
+            pltpu.make_async_copy(large[step], target((owner - step) % 4), load_sem.at[step])
+            for step in range(4)
+        ]
+        for copy in copies:
+            copy.start()
+        for copy in copies:
+            copy.wait()
+
+    @pl.when(me == CON_OWNER)
+    def _():
+        load(CON_OWNER, lambda j: packed.at[j])
+        for j in range(4):
+            for k in range(width // rows):
+                first_column = j * width + k * rows
+                x[:, first_column : first_column + rows] = packed[j, :, k * side : (k + 1) * side].T
+
+    @pl.when(me == GATE_OWNER)
+    def _():
+        load(GATE_OWNER, lambda j: x.at[pl.ds(j * rows, rows)])
+
+    @pl.when(me == UP_OWNER)
+    def _():
+        load(UP_OWNER, lambda j: x.at[pl.ds(j * rows, rows)])
+
+    @pl.when(me != SMALL_OWNER)
+    def _():
+        block_steps(x, acc, gram, poly)
+
+    @pl.when(me == CON_OWNER)
+    def _():
+        for j in range(4):
+            pieces[j] = x[:, j * width : (j + 1) * width].T
+
+    start(3, 4, 5)
+    for k, part in enumerate((first, second, third)):
+        arrive(k)
+
+        @pl.when(me == SMALL_OWNER)
+        def _():
+            if k == 2:
+                for j in range(4):
+                    part[:, j * small : (j + 1) * small] = out_v[j].T
+            block_steps(part, acc, gram, poly)
+            if k == 2:
+                for j in range(4):
+                    out_v[j] = part[:, j * small : (j + 1) * small].T
+
+        start(6 + k)
+    shares[1][1]()
+    dp_o[...] = dp_buf[0] + dp_buf[1] + dp_buf[2] + dp_buf[3]
+    shares[3][1]()
+    gates_o[...] = gates_col[...].reshape(gates_o.shape)
+    arrive(6, 7, 8, 3, 4, 5)
+    sent(0, 1, 2, 3, 4, 5, 6, 7, 8)
+    for share in shares:
+        share[2]()
+
+
+def finish_blocks(large, con_shape, b0, b1, out, gates_piece, col_part, dp_part):
+    piece = large[0].shape
+    rows, total = piece
+    side = 4 * rows
+    f32, bf16 = jnp.float32, jnp.bfloat16
+    shape = jax.ShapeDtypeStruct
+    small = pltpu.VMEM((side, b0.shape[1]), bf16)
+    quarter = (4 * gates_piece.shape[0], gates_piece.shape[1])
+    anywhere = pl.BlockSpec(memory_space=pl.ANY)
+    local = pl.BlockSpec(memory_space=pltpu.VMEM)
+    sems = pltpu.SemaphoreType.DMA
+    shapes = [shape(s, bf16) for s in (piece, piece, con_shape, b0.shape, b1.shape, out.shape)]
+    shapes += [shape((4 * quarter[0], quarter[1]), bf16), shape(col_part.shape, f32)]
+    shapes += [shape(col_part.shape, f32)]
+    return pl.pallas_call(
+        tail_kernel,
+        out_shape=tuple(shapes),
+        in_specs=[anywhere] * 7 + [local] * 3,
+        out_specs=[anywhere] * 6 + [local] * 3,
+        scratch_shapes=[
+            pltpu.VMEM((side, total), bf16),
+            pltpu.VMEM((4,) + piece, bf16),
+            pltpu.VMEM((4,) + con_shape, bf16),
+            small,
+            small,
+            small,
+            pltpu.VMEM((4,) + out.shape, bf16),
+        ]
+        + work_space(side)
+        + [sems((4,))]
+        + [
+            pltpu.VMEM((4,) + col_part.shape, f32),
+            pltpu.VMEM((4,) + col_part.shape, f32),
+            pltpu.VMEM((4,) + gates_piece.shape, bf16),
+            pltpu.VMEM((4,) + quarter, bf16),
+        ]
+        + [sems((4,))] * 8
+        + [sems((9,)), sems((9, 4)), sems((9, 4))],
+        compiler_params=pltpu.CompilerParams(
+            collective_id=0, has_side_effects=True, vmem_limit_bytes=40 * MIB
+        ),
+    )(*large, b0, b1, out, gates_piece, col_part, dp_part)
 
 
 def grouped_step(grad, moment, weight, rate):
@@ -197,12 +995,12 @@
     scale_one, normed_one = norm_forward(stream, norm_gains[0], width)
     normed_low = normed_one.astype(bf16)
 
-    def branch_term(start, count):
-        return jnp.einsum("td,kdl->tkl", normed_low, branch_weights, preferred_element_type=f32)
-
-    branch_pre = owner_rows(branch_term, rows)
-    mixed = branch_pre[:, 0]
-    gelu_in = branch_pre[:, 1]
+    branch_pre = spread_product(normed_low, branch_weights, False, 640, 2)
+    contract_term = product_nt(output_cotangent, contract_weights).astype(bf16)
+    contract_term, branch_pre = lax.optimization_barrier((contract_term, branch_pre))
+    grad_activated = lax.psum_scatter(contract_term, "col", scatter_dimension=0, tiled=True)
+    mixed = branch_pre[0]
+    gelu_in = branch_pre[1]
     edge = from_behind(mixed[rows - reach :], "col", 1)
     extended = jnp.concatenate([edge, mixed], axis=0)
     windows = []
@@ -228,61 +1026,49 @@
     (decay, inject), pull_terms = jax.vjp(
         recurrence_terms, conv_out, gate_pre, mixer_vectors[CONV + 3]
     )
-    local_a, local_b = lax.associative_scan(link, (decay, inject), axis=0)
+    local_a, local_b = linear_scan(decay, inject, False)
     identity = (jnp.ones((lanes,), f32), jnp.zeros((lanes,), f32))
     incoming = prefix((local_a[-1], local_b[-1]), "col", link, identity, False)
     carried = incoming[1]
     state = local_a * carried[None, :] + local_b
     gelu_out, pull_gelu = jax.vjp(gelu_tanh, gelu_in)
     hidden = (gelu_out * state).astype(bf16)
-    hidden_all = all_tokens(hidden)
-    middle = stream + feature_total(product(hidden_all, output_weights))
+    hidden_all, branch_out = meet_product(hidden[None], output_weights, False, 256, 3)
+    middle = stream + branch_out
     scale_two, normed_two = norm_forward(middle, norm_gains[1], width)
     normed_two_low = normed_two.astype(bf16)
 
-    def expand_term(start, count):
-        return jnp.einsum("td,kdf->tkf", normed_two_low, expand_weights, preferred_element_type=f32)
-
-    expand_pre = owner_rows(expand_term, rows)
+    expand_pre = spread_product(normed_two_low, expand_weights, False, 768, 4)
 
     def geglu(gate_values, up_values):
         return gelu_tanh(gate_values) * up_values
 
-    activated, pull_geglu = jax.vjp(geglu, expand_pre[:, 0], expand_pre[:, 1])
+    activated, pull_geglu = jax.vjp(geglu, expand_pre[0], expand_pre[1])
     activated_low = activated.astype(bf16)
-    activated_all = all_tokens(activated_low)
-    block_output = (middle + feature_total(product(activated_all, contract_weights))).astype(bf16)
+    contracted, contract_grad = meet_product(
+        activated_low[None], contract_weights, False, 768, 5, output_cotangent, "tall"
+    )
+    block_output = (middle + contracted).astype(bf16)
     cot_values = output_cotangent.astype(f32)
-    contract_grad = product_tn(activated_all, output_cotangent)
-
-    def contract_term(start, count):
-        return product_nt(output_cotangent, contract_weights)
-
-    grad_activated = owner_rows(contract_term, rows)
+    grad_activated = grad_activated.astype(f32)
     grad_gate, grad_up = pull_geglu(grad_activated)
-    grad_expand_low = jnp.stack([grad_gate, grad_up], axis=1).astype(bf16)
-    grad_expand_all = all_tokens(grad_expand_low)
-    expand_grad = jnp.einsum(
-        "td,tkf->kdf", normed_two_low, grad_expand_all, preferred_element_type=f32
-    )
-    grad_normed_two = feature_total(
-        jnp.einsum("tkf,kdf->td", grad_expand_all, expand_weights, preferred_element_type=f32)
+    grad_expand_low = jnp.stack([grad_gate, grad_up]).astype(bf16)
+    grad_expand_low, contract_grad = lax.optimization_barrier((grad_expand_low, contract_grad))
+    parts = dp_count if feature_count % (16 * dp_count) == 0 else 1
+    grad_normed_two, expand_grad = meet_product(
+        grad_expand_low, expand_weights, True, 768, 7, normed_two_low.T, "wide", parts
     )
     grad_middle_norm, gain_two_grad = norm_backward(
         middle, scale_two, norm_gains[1], grad_normed_two, width
     )
     grad_middle = cot_values + grad_middle_norm
     grad_branch_low = grad_middle.astype(bf16)
-    output_grad = product_tn(hidden_all, grad_branch_low)
-
-    def output_term(start, count):
-        return product_nt(grad_branch_low, output_weights)
-
-    grad_hidden = owner_rows(output_term, rows)
+    output_grad = product_tn(hidden_all[0], grad_branch_low)
+    grad_hidden = spread_product(grad_branch_low, output_weights, True, 256, 8)[0]
     grad_state = grad_hidden * gelu_out
     (grad_gelu_in,) = pull_gelu(grad_hidden * state)
     shifted_decay = jnp.concatenate([decay[1:], jnp.ones((1, lanes), f32)], axis=0)
-    back_a, back_b = lax.associative_scan(link, (shifted_decay, grad_state), reverse=True, axis=0)
+    back_a, back_b = linear_scan(shifted_decay, grad_state, True)
     from_later = prefix((decay[0] * back_a[0], decay[0] * back_b[0]), "col", link, identity, True)
     grad_total = back_a * from_later[1][None, :] + back_b
     previous = jnp.concatenate([carried[None, :], state[:-1]], axis=0)
@@ -292,7 +1078,8 @@
     grad_conv = grad_conv_direct + jnp.einsum(
         "tghj,ghij->thi", grad_gate_heads, gate_blocks, preferred_element_type=f32
     ).reshape(rows, lanes)
-    gates_grad = jnp.einsum("thi,tghj->ghij", conv_low, grad_gate_heads, preferred_element_type=f32)
+    parts = dp_count if feature_count % (16 * dp_count) == 0 else 1
+    planes = dp_count == 4 and parts == 4 and 2 * feature_count <= lanes and group_rows <= lanes
     gate_bias_grad = jnp.sum(grad_gate_low.astype(f32), axis=0)
     after = from_behind(grad_conv[:reach], "col", -1)
     grad_conv_ext = jnp.concatenate([grad_conv, after], axis=0)
@@ -309,31 +1096,107 @@
         grad_rate,
     ]
     vectors_grad = jnp.stack(vector_rows)
-    grad_branch_pre = jnp.stack([grad_mixed, grad_gelu_in], axis=1).astype(bf16)
-    grad_branch_all = all_tokens(grad_branch_pre)
-    branch_grad = jnp.einsum("td,tkl->kdl", normed_low, grad_branch_all, preferred_element_type=f32)
-    grad_normed_one = feature_total(
-        jnp.einsum("tkl,kdl->td", grad_branch_all, branch_weights, preferred_element_type=f32)
-    )
-    grad_stream_norm, gain_one_grad = norm_backward(
-        stream, scale_one, norm_gains[0], grad_normed_one, width
-    )
+    grad_branch_pre = jnp.stack([grad_mixed, grad_gelu_in]).astype(bf16)
+    grad_normed_one, branch_grad = meet_product(
+        grad_branch_pre, branch_weights, True, 640, 9, normed_low.T, "wide", parts
+    )
+    weights_full = (
+        branch_weights[0],
+        branch_weights[1],
+        output_weights,
+        expand_weights[0],
+        expand_weights[1],
+        contract_weights,
+    )
+    if planes:
+        contract_sum = pair_sum(contract_grad.reshape((4, -1) + contract_grad.shape[1:]), 4)
+        expand_grad, contract_sum = lax.optimization_barrier((expand_grad, contract_sum))
+        expand_sum = pair_sum(expand_grad, 4)
+        con_low = (momentum_rate * contract_momentum[0] + contract_sum).astype(bf16)
+        weighted = grad_normed_one * norm_gains[0][None, :]
+        inner_part = jnp.sum(stream * weighted, axis=1)
+        gain_one_grad = jnp.sum(grad_normed_one * stream * scale_one[:, None], axis=0)
+        col_part = jnp.concatenate(
+            [
+                vectors_grad,
+                jnp.pad(inner_part, (0, lanes - group_rows))[None],
+                jnp.zeros((7, lanes), f32),
+            ]
+        )
+        gains_row = jnp.concatenate([gain_one_grad, gain_two_grad])
+        dp_part = jnp.pad(gains_row[None], ((0, 7), (0, lanes - 2 * feature_count)))
+        gates_part = gates_product(
+            conv_low.reshape(rows, lanes), grad_gate_low[:, 0], grad_gate_low[:, 1]
+        )
+        piece_rows = branch_grad.shape[2]
+        small_grad = jnp.concatenate(
+            [
+                branch_grad.reshape(4, 2 * piece_rows, lanes),
+                output_grad.astype(bf16).reshape(4, piece_rows, lanes),
+                gates_part.reshape(4, -1, lanes),
+            ],
+            axis=1,
+        )
+        con_low, expand_sum, col_part, dp_part, small_grad = lax.optimization_barrier(
+            (con_low, expand_sum, col_part, dp_part, small_grad)
+        )
+        expand_low = (momentum_rate * expand_momentum[:, 0] + expand_sum).astype(bf16)
+        small_grad, expand_sum = lax.optimization_barrier((small_grad, expand_sum))
+        large, (expand_sum, contract_sum) = pieces_at_owner(
+            expand_low[0], expand_low[1], con_low, (expand_sum, contract_sum)
+        )
+        small_sum = pair_sum(small_grad, 4)
+        branch_sum = small_sum[: 2 * piece_rows].reshape(2, piece_rows, lanes)
+        output_sum = small_sum[2 * piece_rows : 3 * piece_rows].reshape(output_momentum.shape[1:])
+        branch_low = (momentum_rate * branch_momentum[:, 0] + branch_sum).astype(bf16)
+        output_low = (momentum_rate * output_momentum[0] + output_sum).astype(bf16)
+        e0, e1, con, b0, b1, out, gates_all, col_total, dp_total = finish_blocks(
+            large,
+            con_low.shape,
+            branch_low[0],
+            branch_low[1],
+            output_low,
+            small_sum[3 * piece_rows :],
+            col_part,
+            dp_part,
+        )
+        pieces = [piece.astype(f32) for piece in (b0, b1, out, e0, e1, con)]
+        output_sum = output_sum.astype(f32)
+        gates_total = gates_all.reshape(2, HS, heads_here, HS).transpose(0, 2, 1, 3).astype(f32)
+        vectors_total = dp_total[:8]
+        gains_total = dp_total[8, : 2 * feature_count].reshape(2, feature_count)
+        inner = col_total[8, :group_rows]
+        grad_stream_norm = (
+            scale_one[:, None] * weighted
+            - stream * (scale_one * scale_one * scale_one * inner / width)[:, None]
+        )
+    else:
+        grad_stream_norm, gain_one_grad = norm_backward(
+            stream, scale_one, norm_gains[0], grad_normed_one, width
+        )
+        vectors_total, gains_total = lax.psum(
+            (lax.psum(vectors_grad, "col"), jnp.stack([gain_one_grad, gain_two_grad])), "dp"
+        )
+        gates_grad = jnp.einsum(
+            "thi,tghj->ghij", conv_low, grad_gate_heads, preferred_element_type=f32
+        ).astype(bf16)
+        branch_sum = pair_sum(branch_grad, dp_count)
+        expand_sum = pair_sum(expand_grad, dp_count)
+        output_sum = dp_sum(output_grad)
+        contract_sum = dp_sum(contract_grad)
+        gates_total = lax.psum(gates_grad, ("dp", "col")).astype(f32)
+        pieces = None
     input_grad = (grad_middle + grad_stream_norm).astype(bf16)
-    gain_slots = jnp.zeros((col_count, 2, feature_count), f32)
-    gain_slots = lax.dynamic_update_slice_in_dim(
-        gain_slots, jnp.stack([gain_one_grad, gain_two_grad])[None], col_place, 0
-    )
-    gates_total, vectors_total, slots_total = lax.psum(
-        (gates_grad, vectors_grad, gain_slots), ("dp", "col")
-    )
-    gains_total = lax.dynamic_index_in_dim(slots_total, col_place, 0, keepdims=False)
+    branch_sum = branch_sum.astype(f32)
+    expand_sum = expand_sum.astype(f32)
+    contract_sum = contract_sum.astype(f32)
     summed = (
-        lax.psum_scatter(branch_grad[0], "dp", scatter_dimension=0, tiled=True),
-        lax.psum_scatter(branch_grad[1], "dp", scatter_dimension=0, tiled=True),
-        lax.psum_scatter(output_grad, "dp", scatter_dimension=0, tiled=True),
-        lax.psum_scatter(expand_grad[0], "dp", scatter_dimension=0, tiled=True),
-        lax.psum_scatter(expand_grad[1], "dp", scatter_dimension=0, tiled=True),
-        lax.psum_scatter(contract_grad, "dp", scatter_dimension=0, tiled=True),
+        branch_sum[0],
+        branch_sum[1],
+        output_sum,
+        expand_sum[0],
+        expand_sum[1],
+        contract_sum,
     )
     moments_old = (
         branch_momentum[0, 0],
@@ -343,29 +1206,15 @@
         expand_momentum[1, 0],
         contract_momentum[0],
     )
-    weights_full = (
-        branch_weights[0],
-        branch_weights[1],
-        output_weights,
-        expand_weights[0],
-        expand_weights[1],
-        contract_weights,
-    )
-    moments_new = tuple((momentum_rate * old + fresh for old, fresh in zip(moments_old, summed)))
+    moments_new = tuple(momentum_rate * old + fresh for old, fresh in zip(moments_old, summed))
     block_shapes = [
         (summed[number].shape[0] * dp_count, summed[number].shape[1]) for number in range(6)
     ]
-    gathered = (
-        lax.all_gather(moments_new[0].astype(bf16), "dp", axis=0, tiled=True),
-        lax.all_gather(moments_new[1].astype(bf16), "dp", axis=0, tiled=True),
-        lax.all_gather(moments_new[2].astype(bf16), "dp", axis=0, tiled=True),
-        lax.all_gather(moments_new[3].astype(bf16), "dp", axis=0, tiled=True),
-        lax.all_gather(moments_new[4].astype(bf16), "dp", axis=0, tiled=True),
-        lax.all_gather(moments_new[5].astype(bf16), "dp", axis=0, tiled=True),
-    )
-    orth = owner_results(list(gathered), dp_place, dp_count)
-    pieces = tuple(
-        (
+    if pieces is None:
+        lows = [moment.astype(bf16) for moment in moments_new]
+        gathered = [lax.all_gather(low, "dp", axis=0, tiled=True) for low in lows]
+        orth = owner_results(gathered, dp_place, dp_count)
+        pieces = [
             lax.dynamic_slice_in_dim(
                 owner_send(orth[number], number % dp_count),
                 dp_place * summed[number].shape[0],
@@ -373,8 +1222,7 @@
                 0,
             ).astype(f32)
             for number in range(6)
-        )
-    )
+        ]
     new_pieces = []
     for number in range(6):
         block_rows, block_cols = block_shapes[number]

time: 3030 us -> 985 us (0.33)
  waiting for transfers between devices: 2010 us -> 188 us
  Pallas kernels: 0 us -> 511 us
  local copies, waits for them, and re-layouts: 429 us -> 96.3 us
  matrix products: 238 us -> 11.2 us
  other arithmetic: 188 us -> 98.1 us
  blocking collectives: 111 us -> 32.6 us
    psum x5 -> x0, waiting for transfers between devices: 693 us -> none  [the longest x1 546 us: broadcast(): return lax.psum(kept, axis)]
    pallas_call x0 -> x11, Pallas kernels: none -> 511 us  [the longest x4 194 us: meet_product(): pl.pallas_call(functools.partial(meet_kernel, flip, grad_mode), out_shape...]
    all_gather x10 -> x0, waiting for transfers between devices: 432 us -> none  [the longest x4 118 us: all_tokens(): return lax.all_gather(piece, 'col', axis=0, tiled=True)]
    unnamed x29 -> x4, waiting for transfers between devices: 398 us -> 0.07 us
    reduce_scatter x6 -> x4, waiting for transfers between devices: 489 us -> 149 us  [the longest x3 149 us: pair_sum(): return lax.psum_scatter(grad, 'dp', scatter_dimension=0)]
    slice x103 -> x7, local copies, waits for them, and re-layouts: 178 us -> 2.13 us  [the longest x1 1.29 us: shards(): small_sum[3 * piece_rows:]]
    dot_general x19 -> x0, matrix products: 157 us -> none  [the longest x12 95.9 us: product(): return jnp.dot(left, right, preferred_element_type=jnp.float32)]
    unnamed x270 -> x173, local copies, waits for them, and re-layouts: 117 us -> 52 us
  transfers between devices with their start and end apart: 27 -> 9, of which waited for: 24 -> 4; matrix products, arithmetic and copies ran while one was open for 15% -> 12% of each run, Pallas kernels for 0% -> 30%
where the time goes in v1:
time: 985 us; the launch traced here: 966 us
  Pallas kernels  511 us (52%)
  waiting for transfers between devices  188 us (19%)
  other arithmetic  98.1 us (10%)
  local copies, waits for them, and re-layouts  96.3 us (10%)
  blocking collectives  32.6 us (3%)
  between operations  15.4 us (2%)
  starting transfers between devices  12.9 us (1%)
  matrix products  11.2 us (1%)
    pallas_call x4, Pallas kernels, meet_product(): pl.pallas_call(functools.partial(meet_kernel, flip, grad_mode), out_shape...  194 us
    pallas_call x1, Pallas kernels, finish_blocks(): pl.pallas_call(tail_kernel, out_shape=tuple(shapes), in_specs=[anywhere]...  192 us
    reduce_scatter x3, waiting for transfers between devices, pair_sum(): return lax.psum_scatter(grad, 'dp', scatter_dimension=0)  149 us
    pallas_call x3, Pallas kernels, spread_product(): pl.pallas_call(functools.partial(spread_kernel, flip), out_shape=jax.Shap...  104 us
    unnamed x173, local copies, waits for them, and re-layouts  52 us
    ppermute x3, waiting for transfers between devices, pieces_at_owner(): pieces.append(lax.ppermute(leaving[step], 'dp', pairs))  39 us
    psum x3, blocking collectives, token_total(): return lax.psum(values, 'col')  21.5 us
  transfers between devices with their start and end apart: 9, of which 4 were waited for; matrix products, arithmetic and copies ran while one was open for 12% of the time, Pallas kernels for 30%

profile of v1, /device:TPU:24, one launch (start us, length us, event | category | flops | bytes accessed | tf_op | source)
XLA Modules:
  0.0 965.9 jit_solution(7909050604979209139)
XLA Ops:
  9.3 6.9 psum.21
  17.8 25.7 %shard_map.344 = f32[2,160,1280]{2,1,0:T(8,128)} custom-call(bf16[2,2,160,640]{3,2,1,0:T(8,128)(2,1)} %bitcast.313, bf16[2,640,1280]{2,1,0:T(8,128)(2,1)} %refs_1_.7), custom_call_target="tpu_custom_call" | custom-call | tf_op jit(solution)/shard_map/pallas_call | solution.py:237
  43.6 5.7 convolution_convert_fusion
  60.7 5.8 all-gather.2
  66.9 2.5 fusion.86
  69.4 36.4 %shard_map.346 = (bf16[1,2,2,160,1280]{4,3,2,1,0:T(8,128)(2,1)}, f32[2,320,640]{2,1,0:T(8,128)}) custom-call(bf16[1,160,1280]{2,1,0:T(8,128)(2,1)} %get-tuple-element.510.refs_0_, bf16[1280,640]{1,0:T(8,128)(2,1)} %w.5), custom_call_target="tpu_custom_call" | custom-call | tf_op jit(solution)/shard_map/pallas_call | solution.py:465
  105.8 2.7 copy.139
  110.4 7.4 psum.22
  121.1 62.0 %shard_map.347 = f32[2,160,3840]{2,1,0:T(8,128)} custom-call(bf16[2,2,160,640]{3,2,1,0:T(8,128)(2,1)} %bitcast.314, bf16[2,640,3840]{2,1,0:T(8,128)(2,1)} %refs_1_.6), custom_call_target="tpu_custom_call" | custom-call | tf_op jit(solution)/shard_map/pallas_call | solution.py:237
  183.2 4.3 fusion.18.refs_0_
  187.5 45.8 %shard_map.348 = (f32[2,320,640]{2,1,0:T(8,128)}, bf16[3840,640]{1,0:T(8,128)(2,1)}) custom-call(bf16[1,160,3840]{2,1,0:T(8,128)(2,1)} %fusion.18.refs_0_, bf16[3840,640]{1,0:T(8,128)(2,1)} %refs_1_.5, bf16[640,640]{1,0:T(8,128)(2,1)} %refs_2_.1), custom_call_target="tpu_custom_call" | custom-call | tf_op jit(solution)/shard_map/pallas_call | solution.py:465
  233.3 3.9 fusion.35
  240.2 73.0 %shard_map.349 = (f32[2,320,640]{2,1,0:T(8,128)}, bf16[4,2,160,3840]{3,2,1,0:T(8,128)(2,1)}) custom-call(bf16[2,160,3840]{2,1,0:T(8,128)(2,1)} %pad_maximum_fusion.1.refs_0_, bf16[2,640,3840]{2,1,0:T(8,128)(2,1)} %refs_1_.6, bf16[640,640]{1,0:T(8,128)(2,1)} %fusion.118.refs_2_), custom_call_target="tpu_custom_call" | custom-call | tf_op jit(solution)/shard_map/pallas_call | solution.py:465
  313.2 13.6 %reduce-scatter.7.cloned.1.call-done = bf16[1,960,640]{2,1,0:T(8,128)(2,1)} async-done(((bf16[4,960,640]{2,1,0:T(8,128)(2,1)}), bf16[1,960,640]{2,1,0:T(8,128)(2,1)}) %reduce-scatter.7.cloned.1.call-update) | async-done | bytes 1228816 | tf_op jit(solution)/shard_map/reduce_scatter | solution.py:606
  330.5 2.7 copy.143
  333.2 3.1 multiply_reduce_fusion.1
  336.3 7.2 psum.23
  343.5 3.2 fusion.100
  348.9 16.0 %shard_map.350 = f32[1,160,1280]{2,1,0:T(8,128)} custom-call(bf16[2,2,160,640]{3,2,1,0:T(8,128)(2,1)} %bitcast.310, bf16[1280,640]{1,0:T(8,128)(2,1)} %w.5), custom_call_target="tpu_custom_call" | custom-call | tf_op jit(solution)/shard_map/pallas_call | solution.py:237
  369.4 5.2 all-gather.3
  375.1 3.5 multiply_reduce_fusion.4
  385.8 2.9 convolution_convert_fusion.1
  388.6 3.7 reshape.273
  392.4 17.9 %shard_map.353 = bf16[128,1280]{1,0:T(8,128)(2,1)S(1)} custom-call(bf16[160,1280]{1,0:T(8,128)(2,1)S(1)} %get-tuple-element.512.conv, bf16[160,1280]{1,0:T(8,128)(2,1)S(1)} %get-tuple-element.547.first, bf16[160,1280]{1,0:T(8,128)(2,1)S(1)} %get-tuple-element.546.second), custom_call_target="tpu_custom_call" | custom-call | tf_op jit(solution)/shard_map/pallas_call | solution.py:578
  411.8 38.6 %shard_map.352 = (f32[2,320,640]{2,1,0:T(8,128)}, bf16[4,2,160,1280]{3,2,1,0:T(8,128)(2,1)}) custom-call(bf16[2,160,1280]{2,1,0:T(8,128)(2,1)} %pad_maximum_fusion.4.refs_0_, bf16[2,640,1280]{2,1,0:T(8,128)(2,1)} %refs_1_.7, bf16[640,640]{1,0:T(8,128)(2,1)} %fusion.117.refs_2_), custom_call_target="tpu_custom_call" | custom-call | tf_op jit(solution)/shard_map/pallas_call | solution.py:465
  453.6 5.2 pad_maximum_fusion
  458.7 3.4 fusion.21
  462.1 35.5 %reduce-scatter.9.cloned.1.call-done = bf16[1,2,160,3840]{3,2,1,0:T(8,128)(2,1)} async-done(((bf16[4,2,160,3840]{3,2,1,0:T(8,128)(2,1)}), bf16[1,2,160,3840]{3,2,1,0:T(8,128)(2,1)}) %reduce-scatter.9.cloned.1.call-update) | async-done | bytes 2457616 | tf_op jit(solution)/shard_map/reduce_scatter | solution.py:606
  498.9 2.7 copy.154
  501.6 5.3 copy.155
  509.0 8.3 fusion.105
  517.3 2.9 copy.141
  526.0 3.1 fusion
  532.6 5.8 collective-permute-start.3
  543.9 3.0 fusion.107
  547.5 2.6 maximum_bitcast_fusion.1
  550.1 99.7 %reduce-scatter.11.cloned.1.call-done = bf16[1,512,1280]{2,1,0:T(8,128)(2,1)} async-done(((bf16[4,512,1280]{2,1,0:T(8,128)(2,1)}), bf16[1,512,1280]{2,1,0:T(8,128)(2,1)}) %reduce-scatter.11.cloned.1.call-update) | async-done | bytes 1310736 | tf_op jit(solution)/shard_map/reduce_scatter | solution.py:606
  658.9 39.0 %collective-permute-done.3.refs_2_ = bf16[160,3840]{1,0:T(8,128)(2,1)} collective-permute-done((bf16[160,3840]{1,0:T(8,128)(2,1)}, bf16[160,3840]{1,0:T(8,128)(2,1)}, u32[]{:S(2)}, u32[]{:S(2)}) %collective-permute-start.3) | collective-permute-done | bytes 1228832 | tf_op jit(solution)/shard_map/ppermute | solution.py:760
  699.2 192.3 %shard_map.354 = (bf16[160,3840]{1,0:T(8,128)(2,1)S(1)}, bf16[160,3840]{1,0:T(8,128)(2,1)S(1)}, bf16[960,640]{1,0:T(8,128)(2,1)S(1)}, bf16[160,1280]{1,0:T(8,128...) custom-call(bf16[160,3840]{1,0:T(8,128)(2,1)S(1)} %get-tuple-element, ...), custom_call_target="tpu_custom_call" | custom-call | tf_op jit(solution)/shard_map/pallas_call | solution.py:912
  898.5 4.4 reshape.282
  902.9 6.2 multiply_reduce_fusion
  909.1 5.2 copy.167
  914.4 4.7 multiply_subtract_fusion
  919.1 5.1 copy.164
  925.1 5.3 copy.161
  931.2 4.6 fusion.32
  946.4 2.6 maximum_bitcast_fusion
  953.8 3.0 subtract_bitcast_fusion
  (313 shorter events, 101.3 us)
Async XLA Ops:
  7.2 9.1 copy-start.58
  7.2 226.1 %reduce-scatter.5.cloned.1.call-start = ((), (), s32[]{:S(2)}) async-start(), calls=%async_computation.4 | async-start | bytes 6144000 | tf_op jit(solution)/shard_map/reduce_scatter | solution.py:1001
  9.1 8.7 copy-start.18
  17.8 25.8 %copy-start.34 = (bf16[3840,640]{1,0:T(8,128)(2,1)S(1)}, bf16[3840,640]{1,0:T(8,128)(2,1)}, u32[]{:S(2)}) copy-start(bf16[3840,640]{1,0:T(8,128)(2,1)} %refs_1_.5) | copy-start | bytes 14745604
  17.8 25.8 %copy-start.49 = (bf16[640,640]{1,0:T(8,128)(2,1)S(1)}, bf16[640,640]{1,0:T(8,128)(2,1)}, u32[]{:S(2)}) copy-start(bf16[640,640]{1,0:T(8,128)(2,1)} %refs_2_.1) | copy-start | bytes 2457604
  49.3 2.8 copy-start.73
  49.3 4.3 copy-start.53
  49.3 277.4 %reduce-scatter.7.cloned.1.call-start = ((), (), s32[]{:S(2)}) async-start(), calls=%async_computation.5 | async-start | bytes 6144000 | tf_op jit(solution)/shard_map/reduce_scatter | solution.py:606
  50.7 3.7 collective-permute-start
  54.3 3.2 copy-start.36
  54.4 324.2 %copy-start.67 = (pred[160]{0:T(512)(128)(4,1)}, pred[160]{0:T(512)(128)(4,1)S(1)}, u32[]{:S(2)}) copy-start(pred[160]{0:T(512)(128)(4,1)S(1)} %broadcast_compare_fusion) | copy-start | bytes 484
  110.4 128.7 %copy-start.14 = (f32[640,640]{0,1:T(8,128)}, f32[640,640]{0,1:T(8,128)S(1)}, u32[]{:S(2)}) copy-start(f32[640,640]{0,1:T(8,128)S(1)} %get-tuple-element.509) | copy-start | bytes 4915204
  238.9 258.8 %reduce-scatter.9.cloned.1.call-start = ((), (), s32[]{:S(2)}) async-start(), calls=%async_computation.6 | async-start | bytes 12288000 | tf_op jit(solution)/shard_map/reduce_scatter | solution.py:606
  326.8 322.9 %reduce-scatter.11.cloned.1.call-start = ((), (), s32[]{:S(2)}) async-start(), calls=%async_computation.7 | async-start | bytes 6553600 | tf_op jit(solution)/shard_map/reduce_scatter | solution.py:606
  333.2 10.3 %copy-start.38 = (bf16[640,640]{0,1:T(8,128)(2,1)S(1)}, bf16[640,640]{0,1:T(8,128)(2,1)}, u32[]{:S(2)}) copy-start(bf16[640,640]{0,1:T(8,128)(2,1)} %copy.142) | copy-start | bytes 2457604
  348.9 16.0 %copy-start.24 = (f32[2,160,1280]{2,1,0:T(8,128)S(1)}, f32[2,160,1280]{2,1,0:T(8,128)}, u32[]{:S(2)}) copy-start(f32[2,160,1280]{2,1,0:T(8,128)} %shard_map.344) | copy-start | bytes 4915204
  348.9 16.0 %copy-start.35 = (f32[160,1280]{1,0:T(8,128)S(1)}, f32[160,1280]{1,0:T(8,128)}, u32[]{:S(2)}) copy-start(f32[160,1280]{1,0:T(8,128)} %get-tuple-element.511) | copy-start | bytes 2457604
  375.1 3.5 copy-start.17
  375.1 3.5 copy-start.29
  382.5 3.2 copy-start.59
  382.5 3.3 copy-start.74
  383.8 26.5 %collective-permute-start.1 = (f32[3,1280]{1,0:T(4,128)S(1)}, f32[3,1280]{1,0:T(4,128)S(1)}, u32[]{:S(2)}, u32[]{:S(2)}) collective-permute-start(f32[3,1280]{1,0:T(4,128)S(1)} %slice.309), channel_id=1, source_target_pairs={{1,0},{2,1},{3,2},{5,4},{6,5},{7,6},{9,8},{10,9},{11,10},{13,12},{... | collective-permute-start | bytes 46088 | tf_op jit(solution)/shard_map/ppermute | solution.py:35
  392.3 18.0 %copy-start.70 = (f32[160]{0:T(256)S(1)}, f32[160]{0:T(256)}, u32[]{:S(2)}) copy-start(f32[160]{0:T(256)} %get-tuple-element.563) | copy-start | bytes 1924
  392.3 18.0 %copy-start.71 = (f32[160]{0:T(256)S(1)}, f32[160]{0:T(256)}, u32[]{:S(2)}) copy-start(f32[160]{0:T(256)} %get-tuple-element.559) | copy-start | bytes 1924
  392.3 18.0 %copy-start.72 = (f32[160]{0:T(256)S(1)}, f32[160]{0:T(256)}, u32[]{:S(2)}) copy-start(f32[160]{0:T(256)} %get-tuple-element.566) | copy-start | bytes 1924
  452.7 6.0 copy-start.27
  501.6 5.3 copy-start.22
  517.3 8.7 copy-start.32
  529.1 11.5 %copy-start.30 = (bf16[1,960,640]{2,1,0:T(8,128)(2,1)S(1)}, bf16[1,960,640]{2,1,0:T(8,128)(2,1)}, u32[]{:S(2)}) copy-start(bf16[1,960,640]{2,1,0:T(8,128)(2,1)} %reduce-scatter.7.cloned.1.call-done) | copy-start | bytes 3686404
  531.2 11.0 %copy-start.31 = (f32[1,960,640]{2,1,0:T(8,128)S(1)}, f32[1,960,640]{2,1,0:T(8,128)}, u32[]{:S(2)}) copy-start(f32[1,960,640]{2,1,0:T(8,128)} %param.37) | copy-start | bytes 7372804
  531.2 126.6 %collective-permute-start.2 = (bf16[160,3840]{1,0:T(8,128)(2,1)}, bf16[160,3840]{1,0:T(8,128)(2,1)S(1)}, u32[]{:S(2)}, u32[]{:S(2)}) collective-permute-start(bf16[160,3840]{1,0:T(8,128)(2,1)} %get-tuple-element.314), channel_id=1, source_target_pairs={{0,8},{8,16},{16,24},{1,9},{9,17},{17,25},{2,10},{10,18},{18,26},{... | collective-permute-start | bytes 3686408 | tf_op jit(solution)/shard_map/ppermute | solution.py:760
  532.6 165.3 %collective-permute-start.3 = (bf16[160,3840]{1,0:T(8,128)(2,1)}, bf16[160,3840]{1,0:T(8,128)(2,1)}, u32[]{:S(2)}, u32[]{:S(2)}) collective-permute-start(bf16[160,3840]{1,0:T(8,128)(2,1)} %get-tuple-element.315), channel_id=1, source_target_pairs={{0,16},{8,24},{24,8},{1,17},{9,25},{25,9},{2,18},{10,26},{26,10},{... | collective-permute-start | bytes 3686408 | tf_op jit(solution)/shard_map/ppermute | solution.py:760
  538.4 159.5 %collective-permute-start.4 = (bf16[160,3840]{1,0:T(8,128)(2,1)}, bf16[160,3840]{1,0:T(8,128)(2,1)}, u32[]{:S(2)}, u32[]{:S(2)}) collective-permute-start(bf16[160,3840]{1,0:T(8,128)(2,1)} %get-tuple-element.316), channel_id=1, source_target_pairs={{0,24},{16,8},{24,16},{1,25},{17,9},{25,17},{2,26},{18,10},{26,18}... | collective-permute-start | bytes 3686408 | tf_op jit(solution)/shard_map/ppermute | solution.py:760
  540.5 3.4 copy-start.33
  542.1 4.8 slice-start
  543.9 3.0 slice-start.1
  909.1 5.2 copy-start.42
  919.1 5.2 copy-start.12
  919.1 5.2 copy-start.55
  919.1 5.8 copy-start.69
  924.9 24.1 %copy-start.54 = (f32[8,1280]{1,0:T(8,128)}, f32[8,1280]{1,0:T(8,128)S(1)}, u32[]{:S(2)}) copy-start(f32[8,1280]{1,0:T(8,128)S(1)} %get-tuple-element.498) | copy-start | bytes 122884
  924.9 5.5 copy-start.56
  924.9 28.3 %copy-start.57 = (f32[2,640]{1,0:T(2,128)}, f32[2,640]{1,0:T(2,128)S(1)}, u32[]{:S(2)}) copy-start(f32[2,640]{1,0:T(2,128)S(1)} %get-tuple-element.501) | copy-start | bytes 15364
  925.1 6.0 copy-start.15
  925.1 6.0 copy-start.21
  935.8 3.6 copy-start.45
  935.8 3.6 copy-start.47
  946.4 3.3 copy-start.10
  (38 other events, 57.4 us)
Sparse Core Ops, SparseCore 0:
  49.4 58.9 reduce-scatter.4
  239.0 87.7 reduce-scatter.6
  329.1 168.4 reduce-scatter.8
  499.9 149.7 reduce-scatter.10

commit v2 on v1

--- a/solution.py
+++ b/solution.py
@@ -143,9 +143,62 @@
     return (lax.div(j, per), pl.ds(pl.multiple_of(lax.rem(j, per) * width, width), width))
 
 
+def share_parts(axis, buf, send_sem, recv_sem):
+    me = lax.axis_index(axis)
+
+    def copy(step):
+        return pltpu.make_async_remote_copy(
+            src_ref=buf.at[me],
+            dst_ref=buf.at[me],
+            send_sem=send_sem.at[step],
+            recv_sem=recv_sem.at[step],
+            device_id={axis: lax.rem(me + step, 4)},
+            device_id_type=MESH,
+        )
+
+    def start(value):
+        buf[me] = value
+        for step in range(1, 4):
+            copy(step).start()
+
+    def arrive():
+        for step in range(1, 4):
+            copy(step).wait_recv()
+
+    def finish():
+        for step in range(1, 4):
+            copy(step).wait_send()
+
+    return (start, arrive, finish)
+
+
+def col_peers():
+    me = lax.axis_index("col")
+    return [("col", lax.rem(me + step, 4)) for step in range(1, 4)]
+
+
+def row_scales(values, share, buf):
+    tokens, features = values.shape
+    start, arrive, finish = share
+    squares = jnp.sum(values * values, axis=1, keepdims=True)
+    start(jnp.broadcast_to(squares, (tokens, 128)).T[:8])
+    arrive()
+    total = buf[0] + buf[1] + buf[2] + buf[3]
+    scales = lax.rsqrt(total / (4 * features) + eps_norm)
+    finish()
+    return (scales, jnp.broadcast_to(scales[:1], (128, tokens)).T[:, :1])
+
+
 def spread_kernel(
-    flip, lhs, w, out, wbuf, send1, recv1, own, send2, recv2, wsem, s1s, s1r, s2s, s2r
+    flip, normed, *refs
 ):
+    if normed:
+        stream, gain, w, out, low_out, scale_out, lhs, nbuf, nsend, nrecv = refs[:10]
+        refs = refs[10:]
+    else:
+        lhs, w, out = refs[:3]
+        refs = refs[3:]
+    wbuf, send1, recv1, own, send2, recv2, wsem, s1s, s1r, s2s, s2r = refs
     chunks, rows, width = send2.shape
     per = out.shape[2] // width
     me, near_bit, far_bit, near, far = col_places()
@@ -185,7 +238,16 @@
         lax.fori_loop(0, count, lap, 0)
 
     loop(chunks, lambda j: w_copy(j).start())
-    greet((("col", near), ("col", far)))
+    if normed:
+        greet(col_peers())
+        values = stream[...].astype(jnp.float32)
+        scales, column = row_scales(values, share_parts("col", nbuf, nsend, nrecv), nbuf)
+        scale_out[...] = scales
+        low = (values * column * gain[...]).astype(jnp.bfloat16)
+        low_out[...] = low
+        lhs[...] = low.reshape(lhs.shape)
+    else:
+        greet((("col", near), ("col", far)))
     dot = dot_nt if flip else dot_nn
 
     def first(j):
@@ -226,7 +288,7 @@
     loop(chunks, drain)
 
 
-def spread_product(lhs, w, flip, width, collective):
+def spread_product(lhs, w, flip, width, collective, gain=None):
     tokens, depth = lhs.shape
     rows = tokens // 4
     pairs = 1 if flip else w.shape[0]
@@ -234,12 +296,26 @@
     chunks = pairs * total // width
     tile = (width, depth) if flip else (depth, width)
     bf16, f32 = jnp.bfloat16, jnp.float32
-    return pl.pallas_call(
-        functools.partial(spread_kernel, flip),
-        out_shape=jax.ShapeDtypeStruct((pairs, rows, total), f32),
-        in_specs=[pl.BlockSpec(memory_space=pltpu.VMEM), pl.BlockSpec(memory_space=pl.ANY)],
-        out_specs=pl.BlockSpec(memory_space=pltpu.VMEM),
-        scratch_shapes=[
+    local = pl.BlockSpec(memory_space=pltpu.VMEM)
+    shapes = [jax.ShapeDtypeStruct((pairs, rows, total), f32)]
+    scratch = []
+    if gain is None:
+        inputs = [lhs.reshape(2, 2, rows, depth)]
+    else:
+        inputs = [lhs, gain[None]]
+        shapes += [
+            jax.ShapeDtypeStruct((tokens, depth), bf16),
+            jax.ShapeDtypeStruct((8, tokens), f32),
+        ]
+        scratch = [pltpu.VMEM((2, 2, rows, depth), bf16), pltpu.VMEM((4, 8, tokens), f32)]
+        scratch += [pltpu.SemaphoreType.DMA((4,))] * 2
+    result = pl.pallas_call(
+        functools.partial(spread_kernel, flip, gain is not None),
+        out_shape=tuple(shapes),
+        in_specs=[local] * len(inputs) + [pl.BlockSpec(memory_space=pl.ANY)],
+        out_specs=[local] * len(shapes),
+        scratch_shapes=scratch
+        + [
             pltpu.VMEM((chunks,) + tile, bf16),
             pltpu.VMEM((chunks, 2, rows, width), bf16),
             pltpu.VMEM((chunks, 2, rows, width), bf16),
@@ -251,7 +327,8 @@
         compiler_params=pltpu.CompilerParams(
             collective_id=collective, has_side_effects=True, vmem_limit_bytes=56 * MIB
         ),
-    )(lhs.reshape(2, 2, rows, depth), w)
+    )(*inputs, w)
+    return result[0] if gain is None else result
 
 
 def meet_kernel(flip, grad_mode, *refs):
@@ -259,8 +336,9 @@
         piece, w, side, prod, grad_out = refs[:5]
         refs = refs[5:]
     else:
-        piece, w, all_out, prod = refs[:4]
-        refs = refs[4:]
+        piece, w, stream, gain, all_out, prod, low_out, scale_out = refs[:8]
+        nbuf, nsend, nrecv = refs[-3:]
+        refs = refs[8:-3]
     wbuf, buf, acc, sendx, recvx, wsem, osem, ns, nr, fs, fr, rs, rr, xs, xr = refs[:15]
     if grad_mode:
         stage, gsem = refs[15:]
@@ -411,6 +489,12 @@
 
     settle(far_bit)
     settle(1 - far_bit)
+    if not grad_mode:
+        values = prod[...].reshape(stream.shape) + stream[...].astype(f32)
+        prod[...] = values.reshape(prod.shape)
+        scales, column = row_scales(values, share_parts("col", nbuf, nsend, nrecv), nbuf)
+        scale_out[...] = scales
+        low_out[...] = (values * column * gain[...]).astype(bf16)
 
     def drain(j):
         near_copy(j).wait_send()
@@ -427,7 +511,7 @@
             grad_moves(j).wait()
 
 
-def meet_product(piece, w, flip, width, collective, side=None, grad_mode=None, parts=1):
+def meet_product(piece, w, flip, width, collective, side=None, grad_mode=None, parts=1, stream=None, gain=None):
     pairs, rows, total = piece.shape
     features = w.shape[1]
     chunks = pairs * total // width
@@ -460,8 +544,15 @@
         shapes.append(jax.ShapeDtypeStruct(shape, bf16))
         scratch += [pltpu.VMEM(stage, bf16), pltpu.SemaphoreType.DMA((2,))]
     else:
+        local = pl.BlockSpec(memory_space=pltpu.VMEM)
+        inputs += [stream, gain[None]]
+        in_specs += [local, local]
         shapes.insert(0, jax.ShapeDtypeStruct((pairs, 2, 2, rows, total), bf16))
         out_specs.insert(0, pl.BlockSpec(memory_space=pl.ANY))
+        shapes.append(jax.ShapeDtypeStruct((4 * rows, features), bf16))
+        shapes.append(jax.ShapeDtypeStruct((8, 4 * rows), f32))
+        out_specs += [local, local]
+        scratch += [pltpu.VMEM((4, 8, 4 * rows), f32)] + [pltpu.SemaphoreType.DMA((4,))] * 2
     result = pl.pallas_call(
         functools.partial(meet_kernel, flip, grad_mode),
         out_shape=tuple(shapes),
@@ -474,7 +565,12 @@
     )(*inputs)
     if grad_mode:
         return (result[0].reshape(4 * rows, features), result[1])
-    return (result[0].reshape(pairs, 4 * rows, total), result[1].reshape(4 * rows, features))
+    return (
+        result[0].reshape(pairs, 4 * rows, total),
+        result[1].reshape(4 * rows, features),
+        result[2],
+        result[3][0],
+    )
 
 
 def block_steps(x, acc, gram, poly):
@@ -611,12 +707,6 @@
     return broadcast(block, "dp", root)
 
 
-def norm_forward(stream, gain, width):
-    total = token_total(jnp.sum(stream * stream, axis=1))
-    scale = lax.rsqrt(total / width + eps_norm)
-    return (scale, stream * scale[:, None] * gain[None, :])
-
-
 def norm_backward(stream, scale, gain, grad_normed, width):
     weighted = grad_normed * gain[None, :]
     inner = token_total(jnp.sum(stream * weighted, axis=1))
@@ -761,48 +851,19 @@
     return (pieces, later)
 
 
-def share_parts(axis, buf, send_sem, recv_sem):
-    me = lax.axis_index(axis)
-
-    def copy(step):
-        return pltpu.make_async_remote_copy(
-            src_ref=buf.at[me],
-            dst_ref=buf.at[me],
-            send_sem=send_sem.at[step],
-            recv_sem=recv_sem.at[step],
-            device_id={axis: lax.rem(me + step, 4)},
-            device_id_type=MESH,
-        )
-
-    def start(value):
-        buf[me] = value
-        for step in range(1, 4):
-            copy(step).start()
-
-    def arrive():
-        for step in range(1, 4):
-            copy(step).wait_recv()
-
-    def finish():
-        for step in range(1, 4):
-            copy(step).wait_send()
-
-    return (start, arrive, finish)
-
-
 def tail_kernel(*refs):
     large, (b0, b1, out) = refs[:4], refs[4:7]
     gates_piece, col_part, dp_part = refs[7:10]
-    e0_o, e1_o, con_o, b0_o, b1_o, out_o, gates_o, col_o, dp_o = refs[10:19]
-    x, packed, pieces, first, second, third, out_v, acc, gram, poly, load_sem = refs[19:30]
-    col_buf, dp_buf, gates_dp, gates_col = refs[30:34]
+    expand_o, con_o, branch_o, out_o, gates_o, col_o, dp_o = refs[10:17]
+    x, packed, pieces, first, second, third, out_v, acc, gram, poly, load_sem = refs[17:28]
+    col_buf, dp_buf, gates_dp, gates_col = refs[28:32]
     shares = [
-        share_parts("col", col_buf, *refs[34:36]),
-        share_parts("dp", dp_buf, *refs[36:38]),
-        share_parts("dp", gates_dp, *refs[38:40]),
-        share_parts("col", gates_col, *refs[40:42]),
+        share_parts("col", col_buf, *refs[32:34]),
+        share_parts("dp", dp_buf, *refs[34:36]),
+        share_parts("dp", gates_dp, *refs[36:38]),
+        share_parts("col", gates_col, *refs[38:40]),
     ]
-    sems = refs[42:]
+    sems = refs[40:]
     place = lax.axis_index("col")
     me = lax.axis_index("dp")
     small = out.shape[0]
@@ -813,11 +874,11 @@
         (to_owner(SMALL_OWNER), whole(b0), rows_at(first, "sender")),
         (to_owner(SMALL_OWNER), whole(b1), rows_at(second, "sender")),
         (to_owner(SMALL_OWNER), whole(out), entry(out_v, "sender")),
-        (from_owner(GATE_OWNER), rows_at(x, "target"), whole(e0_o)),
-        (from_owner(UP_OWNER), rows_at(x, "target"), whole(e1_o)),
+        (from_owner(GATE_OWNER), rows_at(x, "target"), whole(expand_o.at[0])),
+        (from_owner(UP_OWNER), rows_at(x, "target"), whole(expand_o.at[1])),
         (from_owner(CON_OWNER), entry(pieces, "target"), whole(con_o)),
-        (from_owner(SMALL_OWNER), rows_at(first, "target"), whole(b0_o)),
-        (from_owner(SMALL_OWNER), rows_at(second, "target"), whole(b1_o)),
+        (from_owner(SMALL_OWNER), rows_at(first, "target"), whole(branch_o.at[0])),
+        (from_owner(SMALL_OWNER), rows_at(second, "target"), whole(branch_o.at[1])),
         (from_owner(SMALL_OWNER), entry(out_v, "target"), whole(out_o)),
     ]
     start, arrive, sent = dp_moves(moves, sems)
@@ -888,7 +949,13 @@
     shares[1][1]()
     dp_o[...] = dp_buf[0] + dp_buf[1] + dp_buf[2] + dp_buf[3]
     shares[3][1]()
-    gates_o[...] = gates_col[...].reshape(gates_o.shape)
+    half = gates_col.shape[1]
+    for k in range(2):
+        for head in range(gates_o.shape[1]):
+            columns = slice(head * HS, (head + 1) * HS)
+            for j in range(HS // half):
+                lines = slice(j * half, (j + 1) * half)
+                gates_o[k, head, lines, :] = gates_col[k * (HS // half) + j][:, columns]
     arrive(6, 7, 8, 3, 4, 5)
     sent(0, 1, 2, 3, 4, 5, 6, 7, 8)
     for share in shares:
@@ -906,14 +973,14 @@
     anywhere = pl.BlockSpec(memory_space=pl.ANY)
     local = pl.BlockSpec(memory_space=pltpu.VMEM)
     sems = pltpu.SemaphoreType.DMA
-    shapes = [shape(s, bf16) for s in (piece, piece, con_shape, b0.shape, b1.shape, out.shape)]
-    shapes += [shape((4 * quarter[0], quarter[1]), bf16), shape(col_part.shape, f32)]
+    shapes = [shape(s, bf16) for s in ((2,) + piece, con_shape, (2,) + b0.shape, out.shape)]
+    shapes += [shape((2, quarter[1] // HS, HS, HS), bf16), shape(col_part.shape, f32)]
     shapes += [shape(col_part.shape, f32)]
     return pl.pallas_call(
         tail_kernel,
         out_shape=tuple(shapes),
         in_specs=[anywhere] * 7 + [local] * 3,
-        out_specs=[anywhere] * 6 + [local] * 3,
+        out_specs=[anywhere] * 4 + [local] * 3,
         scratch_shapes=[
             pltpu.VMEM((side, total), bf16),
             pltpu.VMEM((4,) + piece, bf16),
@@ -992,10 +1059,10 @@
         masks.append((earlier == seg_here).astype(f32))
     reset_rows = masks[1][:rows] < 0.5
     stream = block_input.astype(f32)
-    scale_one, normed_one = norm_forward(stream, norm_gains[0], width)
-    normed_low = normed_one.astype(bf16)
-
-    branch_pre = spread_product(normed_low, branch_weights, False, 640, 2)
+    branch_pre, normed_low, scale_rows = spread_product(
+        block_input, branch_weights, False, 640, 2, norm_gains[0]
+    )
+    scale_one = scale_rows[0]
     contract_term = product_nt(output_cotangent, contract_weights).astype(bf16)
     contract_term, branch_pre = lax.optimization_barrier((contract_term, branch_pre))
     grad_activated = lax.psum_scatter(contract_term, "col", scatter_dimension=0, tiled=True)
@@ -1033,11 +1100,15 @@
     state = local_a * carried[None, :] + local_b
     gelu_out, pull_gelu = jax.vjp(gelu_tanh, gelu_in)
     hidden = (gelu_out * state).astype(bf16)
-    hidden_all, branch_out = meet_product(hidden[None], output_weights, False, 256, 3)
-    middle = stream + branch_out
-    scale_two, normed_two = norm_forward(middle, norm_gains[1], width)
-    normed_two_low = normed_two.astype(bf16)
-
+    hidden_all, middle, normed_two_low, scale_two = meet_product(
+        hidden[None],
+        output_weights,
+        False,
+        256,
+        3,
+        stream=block_input,
+        gain=norm_gains[1],
+    )
     expand_pre = spread_product(normed_two_low, expand_weights, False, 768, 4)
 
     def geglu(gate_values, up_values):
@@ -1100,14 +1171,6 @@
     grad_normed_one, branch_grad = meet_product(
         grad_branch_pre, branch_weights, True, 640, 9, normed_low.T, "wide", parts
     )
-    weights_full = (
-        branch_weights[0],
-        branch_weights[1],
-        output_weights,
-        expand_weights[0],
-        expand_weights[1],
-        contract_weights,
-    )
     if planes:
         contract_sum = pair_sum(contract_grad.reshape((4, -1) + contract_grad.shape[1:]), 4)
         expand_grad, contract_sum = lax.optimization_barrier((expand_grad, contract_sum))
@@ -1150,7 +1213,7 @@
         output_sum = small_sum[2 * piece_rows : 3 * piece_rows].reshape(output_momentum.shape[1:])
         branch_low = (momentum_rate * branch_momentum[:, 0] + branch_sum).astype(bf16)
         output_low = (momentum_rate * output_momentum[0] + output_sum).astype(bf16)
-        e0, e1, con, b0, b1, out, gates_all, col_total, dp_total = finish_blocks(
+        expand_orth, con, branch_orth, out, gates_all, col_total, dp_total = finish_blocks(
             large,
             con_low.shape,
             branch_low[0],
@@ -1160,9 +1223,8 @@
             col_part,
             dp_part,
         )
-        pieces = [piece.astype(f32) for piece in (b0, b1, out, e0, e1, con)]
         output_sum = output_sum.astype(f32)
-        gates_total = gates_all.reshape(2, HS, heads_here, HS).transpose(0, 2, 1, 3).astype(f32)
+        gates_total = gates_all.astype(f32)
         vectors_total = dp_total[:8]
         gains_total = dp_total[8, : 2 * feature_count].reshape(2, feature_count)
         inner = col_total[8, :group_rows]
@@ -1185,54 +1247,41 @@
         output_sum = dp_sum(output_grad)
         contract_sum = dp_sum(contract_grad)
         gates_total = lax.psum(gates_grad, ("dp", "col")).astype(f32)
-        pieces = None
     input_grad = (grad_middle + grad_stream_norm).astype(bf16)
     branch_sum = branch_sum.astype(f32)
     expand_sum = expand_sum.astype(f32)
     contract_sum = contract_sum.astype(f32)
-    summed = (
-        branch_sum[0],
-        branch_sum[1],
-        output_sum,
-        expand_sum[0],
-        expand_sum[1],
-        contract_sum,
-    )
-    moments_old = (
-        branch_momentum[0, 0],
-        branch_momentum[1, 0],
-        output_momentum[0],
-        expand_momentum[0, 0],
-        expand_momentum[1, 0],
-        contract_momentum[0],
-    )
-    moments_new = tuple(momentum_rate * old + fresh for old, fresh in zip(moments_old, summed))
-    block_shapes = [
-        (summed[number].shape[0] * dp_count, summed[number].shape[1]) for number in range(6)
-    ]
-    if pieces is None:
-        lows = [moment.astype(bf16) for moment in moments_new]
+    branch_moment = momentum_rate * branch_momentum[:, 0] + branch_sum
+    expand_moment = momentum_rate * expand_momentum[:, 0] + expand_sum
+    output_moment = momentum_rate * output_momentum[0] + output_sum
+    contract_moment = momentum_rate * contract_momentum[0] + contract_sum
+    if not planes:
+        moments = (*branch_moment, output_moment, *expand_moment, contract_moment)
+        lows = [moment.astype(bf16) for moment in moments]
         gathered = [lax.all_gather(low, "dp", axis=0, tiled=True) for low in lows]
         orth = owner_results(gathered, dp_place, dp_count)
         pieces = [
             lax.dynamic_slice_in_dim(
                 owner_send(orth[number], number % dp_count),
-                dp_place * summed[number].shape[0],
-                summed[number].shape[0],
+                dp_place * lows[number].shape[0],
+                lows[number].shape[0],
                 0,
-            ).astype(f32)
+            )
             for number in range(6)
         ]
-    new_pieces = []
-    for number in range(6):
-        block_rows, block_cols = block_shapes[number]
-        piece_rows = summed[number].shape[0]
-        weight_piece = lax.dynamic_slice_in_dim(
-            weights_full[number], dp_place * piece_rows, piece_rows, 0
-        ).astype(f32)
-        new_pieces.append(
-            weight_piece - muon_rate * max(1.0, block_rows / block_cols) ** 0.5 * pieces[number]
-        )
+        branch_orth, expand_orth = jnp.stack(pieces[:2]), jnp.stack(pieces[3:5])
+        out, con = pieces[2], pieces[5]
+
+    def stepped(weight, orth, axis):
+        count = orth.shape[axis]
+        piece = lax.dynamic_slice_in_dim(weight, dp_place * count, count, axis).astype(f32)
+        tall = max(1.0, weight.shape[axis] / weight.shape[axis + 1]) ** 0.5
+        return piece - muon_rate * tall * orth.astype(f32)
+
+    branch_new = stepped(branch_weights, branch_orth, 1)
+    expand_new = stepped(expand_weights, expand_orth, 1)
+    output_new = stepped(output_weights, out, 0)
+    contract_new = stepped(contract_weights, con, 0)
     gates_moment = momentum_rate * gates_momentum + gates_total
     gate_sq = jnp.mean(gates_moment * gates_moment, axis=(2, 3), keepdims=True)
     gates_new = gate_blocks.astype(f32) - gate_rate * gates_moment * lax.rsqrt(gate_sq + eps_norm)
@@ -1244,26 +1293,26 @@
         block_output,
         input_grad,
         gains_total,
-        jnp.stack([summed[0], summed[1]])[:, None],
+        branch_sum[:, None],
         vectors_total,
         gates_total,
-        summed[2][None],
-        jnp.stack([summed[3], summed[4]])[:, None],
-        summed[5][None],
+        output_sum[None],
+        expand_sum[:, None],
+        contract_sum[None],
         gains_new,
-        jnp.stack([new_pieces[0], new_pieces[1]])[:, None],
+        branch_new[:, None],
         vectors_new,
         gates_new,
-        new_pieces[2][None],
-        jnp.stack([new_pieces[3], new_pieces[4]])[:, None],
-        new_pieces[5][None],
+        output_new[None],
+        expand_new[:, None],
+        contract_new[None],
         gains_moment,
-        jnp.stack([moments_new[0], moments_new[1]])[:, None],
+        branch_moment[:, None],
         vectors_moment,
         gates_moment,
-        moments_new[2][None],
-        jnp.stack([moments_new[3], moments_new[4]])[:, None],
-        moments_new[5][None],
+        output_moment[None],
+        expand_moment[:, None],
+        contract_moment[None],
     )
 
 

time: 985 us -> 938 us (0.952); the launches traced: 966 us -> 930 us
  local copies, waits for them, and re-layouts: 96.3 us -> 41.8 us
  waiting for transfers between devices: 188 us -> 213 us
  Pallas kernels: 511 us -> 534 us
  other arithmetic: 98.1 us -> 80.9 us
  blocking collectives: 32.6 us -> 17.9 us
    reduce_scatter x3, waiting for transfers between devices: 149 us -> 198 us  [pair_sum(): return lax.psum_scatter(grad, 'dp', scatter_dimension=0)]
    unnamed x173 -> x162, local copies, waits for them, and re-layouts: 52 us -> 25.4 us
    ppermute x3, waiting for transfers between devices: 39 us -> 14.6 us  [pieces_at_owner(): pieces.append(lax.ppermute(leaving[step], 'dp', pairs))]
    pallas_call x1, Pallas kernels: 192 us -> 207 us  [finish_blocks(): pl.pallas_call(tail_kernel, out_shape=tuple(shapes), in_specs=[anywhere]...]
    psum x3 -> x1, blocking collectives: 21.5 us -> 7.22 us  [token_total(): return lax.psum(values, 'col')]
    convert_element_type x5 -> x0, local copies, waits for them, and re-layouts: 12 us -> none  [the longest x2 6.28 us: shards(): gates_all.reshape(2, HS, heads_here, HS).transpose(0, 2, 1, 3).astype(f32)]
    reshape x4 -> x0, local copies, waits for them, and re-layouts: 10.5 us -> none  [the longest x3 7.81 us: meet_product(): return (result[0].reshape(4 * rows, features), result[1])]
  transfers between devices with their start and end apart: 9 -> 9, of which waited for: 4 -> 4; matrix products, arithmetic and copies ran while one was open for 12% -> 8% of each run, Pallas kernels for 30% -> 32%
where the time goes in v2:
time: 938 us; the launch traced here: 930 us
  Pallas kernels  534 us (57%)
  waiting for transfers between devices  213 us (23%)
  other arithmetic  80.9 us (9%)
  local copies, waits for them, and re-layouts  41.8 us (4%)
  blocking collectives  17.9 us (2%)
  between operations  15.4 us (2%)
  matrix products  13.9 us (1%)
  starting transfers between devices  13 us (1%)
    pallas_call x1, Pallas kernels, finish_blocks(): pl.pallas_call(tail_kernel, out_shape=tuple(shapes), in_specs=[anywhere]...  207 us
    pallas_call x4, Pallas kernels, meet_product(): pl.pallas_call(functools.partial(meet_kernel, flip, grad_mode), out_shape...  198 us
    reduce_scatter x3, waiting for transfers between devices, pair_sum(): return lax.psum_scatter(grad, 'dp', scatter_dimension=0)  198 us
    pallas_call x3, Pallas kernels, spread_product(): pl.pallas_call(functools.partial(spread_kernel, flip, gain is not None),...  108 us
    unnamed x162, local copies, waits for them, and re-layouts  25.4 us
  transfers between devices with their start and end apart: 9, of which 4 were waited for; matrix products, arithmetic and copies ran while one was open for 8% of the time, Pallas kernels for 32%

profile of v2, /device:TPU:24, one launch (start us, length us, event | category | flops | bytes accessed | tf_op | source)
XLA Modules:
  0.0 930.5 jit_solution(17443527725658450003)
XLA Ops:
  7.2 1.9 slice_reduce_fusion.10
  9.2 8.9 convolution_convert_fusion
  18.1 29.7 %shard_map.344 = (f32[2,160,1280]{2,1,0:T(8,128)}, bf16[640,640]{1,0:T(8,128)(2,1)}, f32[8,640]{1,0:T(8,128)}) custom-call(bf16[640,640]{1,0:T(8,128)(2,1)} %refs_2_.4, f32[1,640]{1,0:T(1,128)} %get-tuple-element.528.refs_1_, bf16[2,640,1280]{2,1,0:T(8,128)(2,1)} %refs_1_.11), custom_call_target="tpu_custom_call" | custom-call | tf_op jit(solution)/shard_map/pallas_call | solution.py:312
  58.1 1.7 shard_map.345
  59.9 5.5 all-gather.2
  65.8 2.5 fusion.84
  68.3 40.6 %shard_map.346 = (bf16[1,2,2,160,1280]{4,3,2,1,0:T(8,128)(2,1)}, f32[2,320,640]{2,1,0:T(8,128)}, bf16[640,640]{1,0:T(8,128)(2,1)}, f32[8,640]{1,0:T(8,128)}) custom-call(bf16[1,160,1280]{2,1,0:T(8,128)(2,1)} %get-tuple-element.492.refs_0_, bf16[1280,640]{1,0:T(8,128)(2,1)} %refs_1_.10, bf16[640,640]{1,0:T(8,128)(2,1)} %refs_2_.4, ...), custom_call_target="tpu_custom_call" | custom-call | tf_op jit(solution)/shard_map/pallas_call | solution.py:556
  108.9 62.1 %shard_map.347 = f32[2,160,3840]{2,1,0:T(8,128)} custom-call(bf16[2,2,160,640]{3,2,1,0:T(8,128)(2,1)} %bitcast.311, bf16[2,640,3840]{2,1,0:T(8,128)(2,1)} %refs_1_.9), custom_call_target="tpu_custom_call" | custom-call | tf_op jit(solution)/shard_map/pallas_call | solution.py:312
  171.0 4.3 fusion.19.refs_0_
  175.2 46.0 %shard_map.348 = (f32[2,320,640]{2,1,0:T(8,128)}, bf16[3840,640]{1,0:T(8,128)(2,1)}) custom-call(bf16[1,160,3840]{2,1,0:T(8,128)(2,1)} %fusion.19.refs_0_, bf16[3840,640]{1,0:T(8,128)(2,1)} %refs_1_.8, bf16[640,640]{1,0:T(8,128)(2,1)} %refs_2_.5), custom_call_target="tpu_custom_call" | custom-call | tf_op jit(solution)/shard_map/pallas_call | solution.py:556
  221.3 3.9 fusion.35
  229.3 73.0 %shard_map.349 = (f32[2,320,640]{2,1,0:T(8,128)}, bf16[4,2,160,3840]{3,2,1,0:T(8,128)(2,1)}) custom-call(bf16[2,160,3840]{2,1,0:T(8,128)(2,1)} %pad_maximum_fusion.1.refs_0_, bf16[2,640,3840]{2,1,0:T(8,128)(2,1)} %refs_1_.9, bf16[640,640]{1,0:T(8,128)(2,1)} %bitcast.306), custom_call_target="tpu_custom_call" | custom-call | tf_op jit(solution)/shard_map/pallas_call | solution.py:556
  302.2 12.5 %reduce-scatter.7.cloned.1.call-done = bf16[1,960,640]{2,1,0:T(8,128)(2,1)} async-done(((bf16[4,960,640]{2,1,0:T(8,128)(2,1)}), bf16[1,960,640]{2,1,0:T(8,128)(2,1)}) %reduce-scatter.7.cloned.1.call-update) | async-done | bytes 1228816 | tf_op jit(solution)/shard_map/reduce_scatter | solution.py:702
  318.9 2.5 multiply_reduce_fusion.1
  321.4 7.2 psum.7
  328.7 3.2 fusion.98
  331.9 16.0 %shard_map.350 = f32[1,160,1280]{2,1,0:T(8,128)} custom-call(bf16[2,2,160,640]{3,2,1,0:T(8,128)(2,1)} %bitcast.308, bf16[1280,640]{1,0:T(8,128)(2,1)} %refs_1_.10), custom_call_target="tpu_custom_call" | custom-call | tf_op jit(solution)/shard_map/pallas_call | solution.py:312
  347.9 1.8 bitcast_multiply_fusion.8
  349.7 1.8 shard_map.351
  352.4 5.2 all-gather.3
  358.1 3.5 multiply_reduce_fusion.3
  368.6 2.9 convolution_convert_fusion.1
  371.5 3.7 reshape.234
  375.2 17.8 %shard_map.353 = bf16[128,1280]{1,0:T(8,128)(2,1)S(1)} custom-call(bf16[160,1280]{1,0:T(8,128)(2,1)S(1)} %get-tuple-element.494.conv, bf16[160,1280]{1,0:T(8,128)(2,1)S(1)} %get-tuple-element.519.first, bf16[160,1280]{1,0:T(8,128)(2,1)S(1)} %get-tuple-element.518.second), custom_call_target="tpu_custom_call" | custom-call | tf_op jit(solution)/shard_map/pallas_call | solution.py:674
  394.6 38.7 %shard_map.352 = (f32[2,320,640]{2,1,0:T(8,128)}, bf16[4,2,160,1280]{3,2,1,0:T(8,128)(2,1)}) custom-call(bf16[2,160,1280]{2,1,0:T(8,128)(2,1)} %pad_maximum_fusion.4.refs_0_, bf16[2,640,1280]{2,1,0:T(8,128)(2,1)} %refs_1_.11, bf16[640,640]{1,0:T(8,128)(2,1)} %bitcast.305), custom_call_target="tpu_custom_call" | custom-call | tf_op jit(solution)/shard_map/pallas_call | solution.py:556
  433.4 2.2 fusion.25
  435.7 5.2 pad_maximum_fusion
  441.0 3.0 fusion.20
  444.0 41.6 %reduce-scatter.9.cloned.1.call-done = bf16[1,2,160,3840]{3,2,1,0:T(8,128)(2,1)} async-done(((bf16[4,2,160,3840]{3,2,1,0:T(8,128)(2,1)}), bf16[1,2,160,3840]{3,2,1,0:T(8,128)(2,1)}) %reduce-scatter.9.cloned.1.call-update) | async-done | bytes 2457616 | tf_op jit(solution)/shard_map/reduce_scatter | solution.py:702
  491.6 3.1 fusion.1
  494.7 2.2 select_select_fusion
  498.4 5.7 collective-permute-start.3
  504.1 2.1 collective-permute-start.4
  507.9 1.7 fusion.3
  510.5 2.6 convert_bitcast_fusion
  513.1 2.7 fusion
  515.8 143.9 %reduce-scatter.11.cloned.1.call-done = bf16[1,512,1280]{2,1,0:T(8,128)(2,1)} async-done(((bf16[4,512,1280]{2,1,0:T(8,128)(2,1)}), bf16[1,512,1280]{2,1,0:T(8,128)(2,1)}) %reduce-scatter.11.cloned.1.call-update) | async-done | bytes 1310736 | tf_op jit(solution)/shard_map/reduce_scatter | solution.py:702
  662.8 2.5 multiply_add_fusion.5
  665.4 1.9 copy-done.33
  671.3 14.6 %collective-permute-done.3.refs_2_ = bf16[160,3840]{1,0:T(8,128)(2,1)} collective-permute-done((bf16[160,3840]{1,0:T(8,128)(2,1)}, bf16[160,3840]{1,0:T(8,128)(2,1)}, u32[]{:S(2)}, u32[]{:S(2)}) %collective-permute-start.3) | collective-permute-done | bytes 1228832 | tf_op jit(solution)/shard_map/ppermute | solution.py:850
  687.1 207.1 %shard_map.354 = (bf16[2,160,3840]{2,1,0:T(8,128)(2,1)S(1)}, bf16[960,640]{1,0:T(8,128)(2,1)S(1)}, bf16[2,160,1280]{2,1,0:T(8,128)(2,1)S(1)}, bf16[320,640]{1,0:...) custom-call(bf16[160,3840]{1,0:T(8,128)(2,1)S(1)} %get-tuple-element.321.ref, ...), custom_call_target="tpu_custom_call" | custom-call | tf_op jit(solution)/shard_map/pallas_call | solution.py:979
  900.5 2.7 subtract_bitcast_fusion.2
  903.2 4.7 subtract_bitcast_fusion
  908.0 2.0 multiply_reduce_fusion
  913.2 1.9 fusion.28
  916.4 2.0 subtract_bitcast_fusion.3
  918.4 3.1 subtract_bitcast_fusion.1
  921.6 1.9 multiply_subtract_fusion
  (281 shorter events, 58.2 us)
Async XLA Ops:
  7.2 214.1 %reduce-scatter.5.cloned.1.call-start = ((), (), s32[]{:S(2)}) async-start(), calls=%async_computation.4 | async-start | bytes 6144000 | tf_op jit(solution)/shard_map/reduce_scatter | solution.py:1068
  9.2 319.5 %copy-start.52 = (f32[640]{0:T(1024)}, f32[640]{0:T(1024)S(1)}, u32[]{:S(2)}) copy-start(f32[640]{0:T(1024)S(1)} %get-tuple-element.457) | copy-start | bytes 7684
  47.8 4.4 copy-start.46
  47.9 266.8 %reduce-scatter.7.cloned.1.call-start = ((), (), s32[]{:S(2)}) async-start(), calls=%async_computation.5 | async-start | bytes 6144000 | tf_op jit(solution)/shard_map/reduce_scatter | solution.py:702
  49.3 3.8 collective-permute-start
  53.0 3.8 copy-start.26
  53.0 4.0 copy-start.67
  53.7 3.4 copy-start.17
  226.9 258.7 %reduce-scatter.9.cloned.1.call-start = ((), (), s32[]{:S(2)}) async-start(), calls=%async_computation.6 | async-start | bytes 12288000 | tf_op jit(solution)/shard_map/reduce_scatter | solution.py:702
  314.7 345.0 %reduce-scatter.11.cloned.1.call-start = ((), (), s32[]{:S(2)}) async-start(), calls=%async_computation.7 | async-start | bytes 6553600 | tf_op jit(solution)/shard_map/reduce_scatter | solution.py:702
  318.8 9.8 %copy-start.28 = (bf16[640,640]{1,0:T(8,128)(2,1)S(1)}, bf16[640,640]{1,0:T(8,128)(2,1)}, u32[]{:S(2)}) copy-start(bf16[640,640]{1,0:T(8,128)(2,1)} %refs_2_.5) | copy-start | bytes 2457604
  328.6 3.2 copy-start.55
  331.9 16.0 %copy-start.25 = (f32[160,1280]{1,0:T(8,128)S(1)}, f32[160,1280]{1,0:T(8,128)}, u32[]{:S(2)}) copy-start(f32[160,1280]{1,0:T(8,128)} %get-tuple-element.493) | copy-start | bytes 2457604
  331.9 16.0 %copy-start.31 = (f32[2,160,1280]{2,1,0:T(8,128)S(1)}, f32[2,160,1280]{2,1,0:T(8,128)}, u32[]{:S(2)}) copy-start(f32[2,160,1280]{2,1,0:T(8,128)} %get-tuple-element.293) | copy-start | bytes 4915204
  349.7 8.4 copy-start.68
  358.1 3.6 copy-start.11
  358.1 3.6 copy-start.18
  358.1 3.6 copy-start.51
  366.9 26.2 %collective-permute-start.1 = (f32[3,1280]{1,0:T(4,128)S(1)}, f32[3,1280]{1,0:T(4,128)S(1)}, u32[]{:S(2)}, u32[]{:S(2)}) collective-permute-start(f32[3,1280]{1,0:T(4,128)S(1)} %slice.265), channel_id=1, source_target_pairs={{1,0},{2,1},{3,2},{5,4},{6,5},{7,6},{9,8},{10,9},{11,10},{13,12},{... | collective-permute-start | bytes 46088 | tf_op jit(solution)/shard_map/ppermute | solution.py:35
  375.2 17.9 %copy-start.49 = (f32[1280]{0:T(1024)S(1)}, f32[1280]{0:T(1024)}, u32[]{:S(2)}) copy-start(f32[1280]{0:T(1024)} %copy-done.48) | copy-start | bytes 15364
  375.2 17.9 %copy-start.69 = (f32[160]{0:T(256)S(1)}, f32[160]{0:T(256)}, u32[]{:S(2)}) copy-start(f32[160]{0:T(256)} %get-tuple-element.537) | copy-start | bytes 1924
  375.2 17.9 %copy-start.70 = (f32[160]{0:T(256)S(1)}, f32[160]{0:T(256)}, u32[]{:S(2)}) copy-start(f32[160]{0:T(256)} %get-tuple-element.533) | copy-start | bytes 1924
  375.2 17.9 %copy-start.71 = (f32[160]{0:T(256)S(1)}, f32[160]{0:T(256)}, u32[]{:S(2)}) copy-start(f32[160]{0:T(256)} %get-tuple-element.540) | copy-start | bytes 1924
  394.6 38.8 %copy-start.19 = (bf16[640,640]{1,0:T(8,128)(2,1)S(1)}, bf16[640,640]{1,0:T(8,128)(2,1)}, u32[]{:S(2)}) copy-start(bf16[640,640]{1,0:T(8,128)(2,1)} %refs_2_.4) | copy-start | bytes 2457604
  394.6 38.8 %copy-start.54 = (f32[640]{0:T(1024)S(1)}, f32[640]{0:T(1024)}, u32[]{:S(2)}) copy-start(f32[640]{0:T(1024)} %get-tuple-element.456) | copy-start | bytes 7684
  435.7 5.3 copy-start.21
  485.6 6.0 copy-start.12
  494.6 11.7 %copy-start.22 = (bf16[1,960,640]{2,1,0:T(8,128)(2,1)S(1)}, bf16[1,960,640]{2,1,0:T(8,128)(2,1)}, u32[]{:S(2)}) copy-start(bf16[1,960,640]{2,1,0:T(8,128)(2,1)} %reduce-scatter.7.cloned.1.call-done) | copy-start | bytes 3686404
  494.6 18.4 %slice-start = ((s8[4915200]{0:T(1024)(128)(4,1)}), s8[4194304]{0:T(1024)(128)(4,1)S(1)}, s32[]{:S(2)}) async-start(s8[4915200]{0:T(1024)(128)(4,1)} %bitcast.294), calls=%async_computation.8 | async-start | bytes 8388608
  496.9 11.0 %copy-start.24 = (f32[1,960,640]{2,1,0:T(8,128)S(1)}, f32[1,960,640]{2,1,0:T(8,128)}, u32[]{:S(2)}) copy-start(f32[1,960,640]{2,1,0:T(8,128)} %param.37) | copy-start | bytes 7372804
  496.9 173.4 %collective-permute-start.2 = (bf16[160,3840]{1,0:T(8,128)(2,1)}, bf16[160,3840]{1,0:T(8,128)(2,1)S(1)}, u32[]{:S(2)}, u32[]{:S(2)}) collective-permute-start(bf16[160,3840]{1,0:T(8,128)(2,1)} %get-tuple-element.322), channel_id=1, source_target_pairs={{0,8},{8,16},{16,24},{1,9},{9,17},{17,25},{2,10},{10,18},{18,26},{... | collective-permute-start | bytes 3686408 | tf_op jit(solution)/shard_map/ppermute | solution.py:850
  498.4 187.4 %collective-permute-start.3 = (bf16[160,3840]{1,0:T(8,128)(2,1)}, bf16[160,3840]{1,0:T(8,128)(2,1)}, u32[]{:S(2)}, u32[]{:S(2)}) collective-permute-start(bf16[160,3840]{1,0:T(8,128)(2,1)} %get-tuple-element.323), channel_id=1, source_target_pairs={{0,16},{8,24},{24,8},{1,17},{9,25},{25,9},{2,18},{10,26},{26,10},{... | collective-permute-start | bytes 3686408 | tf_op jit(solution)/shard_map/ppermute | solution.py:850
  504.1 181.7 %collective-permute-start.4 = (bf16[160,3840]{1,0:T(8,128)(2,1)}, bf16[160,3840]{1,0:T(8,128)(2,1)}, u32[]{:S(2)}, u32[]{:S(2)}) collective-permute-start(bf16[160,3840]{1,0:T(8,128)(2,1)} %get-tuple-element.324), channel_id=1, source_target_pairs={{0,24},{16,8},{24,16},{1,25},{17,9},{25,17},{2,26},{18,10},{26,18}... | collective-permute-start | bytes 3686408 | tf_op jit(solution)/shard_map/ppermute | solution.py:850
  507.9 5.2 slice-start.1
  665.4 3.5 copy-start.14
  898.1 5.0 copy-start.57
  899.6 16.1 %copy-start.47 = (f32[8,1280]{1,0:T(8,128)}, f32[8,1280]{1,0:T(8,128)S(1)}, u32[]{:S(2)}) copy-start(f32[8,1280]{1,0:T(8,128)S(1)} %get-tuple-element.482) | copy-start | bytes 122884
  900.3 14.8 %copy-start.59 = (f32[2,640]{1,0:T(2,128)}, f32[2,640]{1,0:T(2,128)S(1)}, u32[]{:S(2)}) copy-start(f32[2,640]{1,0:T(2,128)S(1)} %get-tuple-element.485) | copy-start | bytes 15364
  903.2 4.7 copy-start.42
  907.9 3.4 copy-start.20
  907.9 4.3 copy-start.29
  907.9 4.8 copy-start.34
  907.9 5.3 copy-start.43
  908.0 5.2 copy-start.53
  908.0 5.2 copy-start.56
  909.9 11.6 %copy-start.23 = (f32[2,5,256,256]{3,2,1,0:T(8,128)}, f32[2,5,256,256]{3,2,1,0:T(8,128)S(1)}, u32[]{:S(2)}) copy-start(f32[2,5,256,256]{3,2,1,0:T(8,128)S(1)} %get-tuple-element.479) | copy-start | bytes 7864324
  913.2 3.2 copy-start.8
  915.1 3.3 copy-start.3
  (37 other events, 62.6 us)
Sparse Core Ops, SparseCore 0:
  48.0 58.0 reduce-scatter.4
  227.0 87.6 reduce-scatter.6
  317.1 168.4 reduce-scatter.8
  487.8 171.8 reduce-scatter.10

commit v3 on v2

--- a/solution.py
+++ b/solution.py
@@ -332,15 +332,19 @@
 
 
 def meet_kernel(flip, grad_mode, *refs):
-    if grad_mode:
+    lone = grad_mode == "lone"
+    if lone:
+        piece, side, all_out, grad_out, buf, osem, ns, nr, fs, fr, rs, rr, stage, gsem = refs
+    elif grad_mode:
         piece, w, side, prod, grad_out = refs[:5]
         refs = refs[5:]
     else:
         piece, w, stream, gain, all_out, prod, low_out, scale_out = refs[:8]
         nbuf, nsend, nrecv = refs[-3:]
         refs = refs[8:-3]
-    wbuf, buf, acc, sendx, recvx, wsem, osem, ns, nr, fs, fr, rs, rr, xs, xr = refs[:15]
-    if grad_mode:
+    if not lone:
+        wbuf, buf, acc, sendx, recvx, wsem, osem, ns, nr, fs, fr, rs, rr, xs, xr = refs[:15]
+    if grad_mode and not lone:
         stage, gsem = refs[15:]
     chunks, _, _, rows, width = buf.shape
     per = piece.shape[2] // width
@@ -398,8 +402,14 @@
 
         lax.fori_loop(0, count, lap, 0)
 
-    loop(chunks, lambda j: w_copy(j).start())
-    greet((("col", near), ("col", far), ("row", across)))
+    if not lone:
+        loop(chunks, lambda j: w_copy(j).start())
+    if lone:
+        greet((("col", near), ("col", far)))
+    elif grad_mode:
+        greet((("col", near), ("col", far), ("row", across)))
+    else:
+        greet(col_peers() + [("row", across)])
 
     def begin(j):
         far_copy(j).start()
@@ -408,7 +418,8 @@
         buf[j, far_bit, near_bit] = piece[k, :, cols]
 
     loop(chunks, begin)
-    acc[...] = jnp.zeros_like(acc)
+    if not lone:
+        acc[...] = jnp.zeros_like(acc)
     dot = dot_nt if flip else dot_nn
 
     def add(j, half):
@@ -417,12 +428,14 @@
 
     def here(j):
         near_copy(j).wait_recv()
-        w_copy(j).wait()
-        add(j, far_bit)
+        if not lone:
+            w_copy(j).wait()
+            add(j, far_bit)
 
     loop(chunks, here)
-    sendx[far_bit] = acc[far_bit].astype(bf16)
-    cross(far_bit).start()
+    if not lone:
+        sendx[far_bit] = acc[far_bit].astype(bf16)
+        cross(far_bit).start()
 
     def grad_copy(j):
         return grad_moves(j)
@@ -441,7 +454,7 @@
             total = dot_nn(side[...], block).astype(bf16)
             stage[lax.rem(j, 2)] = total.reshape(stage.shape[1:])
 
-    if grad_mode == "tall":
+    if lone:
 
         def grad_moves(j):
             return pltpu.make_async_copy(
@@ -460,9 +473,10 @@
 
     def there(j):
         relay(j).wait_recv()
-        if not grad_mode:
+        if lone or not grad_mode:
             out_copy(j).start()
-        add(j, 1 - far_bit)
+        if not lone:
+            add(j, 1 - far_bit)
         if grad_mode:
 
             @pl.when(j >= 2)
@@ -480,15 +494,16 @@
 
     loop(chunks - 1, both)
     there(chunks - 1)
-    sendx[1 - far_bit] = acc[1 - far_bit].astype(bf16)
-    cross(1 - far_bit).start()
-
-    def settle(half):
-        cross(half).wait_recv()
-        prod[half] = sendx[half].astype(f32) + recvx[half].astype(f32)
-
-    settle(far_bit)
-    settle(1 - far_bit)
+    if not lone:
+        sendx[1 - far_bit] = acc[1 - far_bit].astype(bf16)
+        cross(1 - far_bit).start()
+
+        def settle(half):
+            cross(half).wait_recv()
+            prod[half] = sendx[half].astype(f32) + recvx[half].astype(f32)
+
+        settle(far_bit)
+        settle(1 - far_bit)
     if not grad_mode:
         values = prod[...].reshape(stream.shape) + stream[...].astype(f32)
         prod[...] = values.reshape(prod.shape)
@@ -500,15 +515,40 @@
         near_copy(j).wait_send()
         far_copy(j).wait_send()
         relay(j).wait_send()
-        if not grad_mode:
+        if lone or not grad_mode:
             out_copy(j).wait()
 
     loop(chunks, drain)
-    cross(far_bit).wait_send()
-    cross(1 - far_bit).wait_send()
+    if not lone:
+        cross(far_bit).wait_send()
+        cross(1 - far_bit).wait_send()
     if grad_mode:
         for j in range(max(0, chunks - 2), chunks):
             grad_moves(j).wait()
+
+
+def meet_gradient(piece, width, collective, side):
+    pairs, rows, total = piece.shape
+    chunks = pairs * total // width
+    bf16 = jnp.bfloat16
+    local = pl.BlockSpec(memory_space=pltpu.VMEM)
+    anywhere = pl.BlockSpec(memory_space=pl.ANY)
+    everything, gradient = pl.pallas_call(
+        functools.partial(meet_kernel, False, "lone"),
+        out_shape=(
+            jax.ShapeDtypeStruct((pairs, 2, 2, rows, total), bf16),
+            jax.ShapeDtypeStruct((total, side.shape[1]), bf16),
+        ),
+        in_specs=[local, local],
+        out_specs=[anywhere, anywhere],
+        scratch_shapes=[pltpu.VMEM((chunks, 2, 2, rows, width), bf16)]
+        + [pltpu.SemaphoreType.DMA((chunks,))] * 7
+        + [pltpu.VMEM((2, width, side.shape[1]), bf16), pltpu.SemaphoreType.DMA((2,))],
+        compiler_params=pltpu.CompilerParams(
+            collective_id=collective, has_side_effects=True, vmem_limit_bytes=40 * MIB
+        ),
+    )(piece, side)
+    return (everything.reshape(pairs, 4 * rows, total), gradient)
 
 
 def meet_product(piece, w, flip, width, collective, side=None, grad_mode=None, parts=1, stream=None, gain=None):
@@ -828,7 +868,7 @@
     return [(owner, target) for target in ((owner + step) % 4 for step in range(4))]
 
 
-SMALL_OWNER, CON_OWNER, GATE_OWNER, UP_OWNER = (0, 1, 2, 3)
+SMALL_OWNER, CON_OWNER, GATE_OWNER, UP_OWNER = (2, 1, 3, 0)
 
 
 def pieces_at_owner(e0, e1, con, later):
@@ -1116,10 +1156,7 @@
 
     activated, pull_geglu = jax.vjp(geglu, expand_pre[0], expand_pre[1])
     activated_low = activated.astype(bf16)
-    contracted, contract_grad = meet_product(
-        activated_low[None], contract_weights, False, 768, 5, output_cotangent, "tall"
-    )
-    block_output = (middle + contracted).astype(bf16)
+    activated_all, contract_grad = meet_gradient(activated_low[None], 640, 5, output_cotangent)
     cot_values = output_cotangent.astype(f32)
     grad_activated = grad_activated.astype(f32)
     grad_gate, grad_up = pull_geglu(grad_activated)
@@ -1160,6 +1197,12 @@
         masked = grad_conv_ext * masks[shift][:, None]
         grad_mixed = grad_mixed + mixer_vectors[shift][None, :] * masked[shift : shift + rows]
         tap_grads.append(jnp.sum(grad_conv * windows[shift], axis=0))
+    grad_mixed, activated_all = lax.optimization_barrier((grad_mixed, activated_all))
+    contracted_low = product(activated_all[0], contract_weights).astype(bf16)
+    contracted = contracted_low.astype(f32) + lax.ppermute(
+        contracted_low, "row", [(0, 1), (1, 0)]
+    ).astype(f32)
+    block_output = (middle + contracted).astype(bf16)
     vector_rows = tap_grads + [
         jnp.sum(grad_conv, axis=0),
         gate_bias_grad[0],
@@ -1200,8 +1243,10 @@
             ],
             axis=1,
         )
-        con_low, expand_sum, col_part, dp_part, small_grad = lax.optimization_barrier(
-            (con_low, expand_sum, col_part, dp_part, small_grad)
+        con_low, expand_sum, col_part, dp_part, small_grad, block_output = (
+            lax.optimization_barrier(
+                (con_low, expand_sum, col_part, dp_part, small_grad, block_output)
+            )
         )
         expand_low = (momentum_rate * expand_momentum[:, 0] + expand_sum).astype(bf16)
         small_grad, expand_sum = lax.optimization_barrier((small_grad, expand_sum))

time: 938 us -> 893 us (0.952)
  Pallas kernels: 534 us -> 503 us
  waiting for transfers between devices: 213 us -> 187 us
    pallas_call x4 -> x3, Pallas kernels: 198 us -> 152 us  [meet_product(): pl.pallas_call(functools.partial(meet_kernel, flip, grad_mode), out_shape...]
    pallas_call x0 -> x1, Pallas kernels: none -> 31.6 us  [meet_gradient(): pl.pallas_call(functools.partial(meet_kernel, False, 'lone'), out_shape=(...]
    pallas_call x1, Pallas kernels: 207 us -> 189 us  [finish_blocks(): pl.pallas_call(tail_kernel, out_shape=tuple(shapes), in_specs=[anywhere]...]
    ppermute x3, waiting for transfers between devices: 14.6 us -> 0.01 us  [pieces_at_owner(): pieces.append(lax.ppermute(leaving[step], 'dp', pairs))]
    reduce_scatter x3, waiting for transfers between devices: 198 us -> 187 us  [pair_sum(): return lax.psum_scatter(grad, 'dp', scatter_dimension=0)]
    unnamed x162 -> x176, local copies, waits for them, and re-layouts: 25.4 us -> 21.8 us
  transfers between devices with their start and end apart: 9 -> 10, of which waited for: 4 -> 3; matrix products, arithmetic and copies ran while one was open for 8% -> 11% of each run, Pallas kernels for 32% -> 32%
where the time goes in v3:
time: 893 us; the launch traced here: 885 us
  Pallas kernels  503 us (56%)
  waiting for transfers between devices  187 us (21%)
  other arithmetic  82.4 us (9%)
  local copies, waits for them, and re-layouts  44.6 us (5%)
  matrix products  23.1 us (3%)
  blocking collectives  18 us (2%)
  between operations  15.2 us (2%)
  starting transfers between devices  11.5 us (1%)
    pallas_call x1, Pallas kernels, finish_blocks(): pl.pallas_call(tail_kernel, out_shape=tuple(shapes), in_specs=[anywhere]...  189 us
    reduce_scatter x3, waiting for transfers between devices, pair_sum(): return lax.psum_scatter(grad, 'dp', scatter_dimension=0)  187 us
    pallas_call x3, Pallas kernels, meet_product(): pl.pallas_call(functools.partial(meet_kernel, flip, grad_mode), out_shape...  152 us
    pallas_call x3, Pallas kernels, spread_product(): pl.pallas_call(functools.partial(spread_kernel, flip, gain is not None),...  108 us
    pallas_call x1, Pallas kernels, meet_gradient(): pl.pallas_call(functools.partial(meet_kernel, False, 'lone'), out_shape=(...  31.6 us
    unnamed x176, local copies, waits for them, and re-layouts  21.8 us
  transfers between devices with their start and end apart: 10, of which 3 were waited for; matrix products, arithmetic and copies ran while one was open for 11% of the time, Pallas kernels for 32%

profile of v3, /device:TPU:24, one launch (start us, length us, event | category | flops | bytes accessed | tf_op | source)
XLA Modules:
  0.0 884.9 jit_solution(9277630428383611058)
XLA Ops:
  7.2 1.9 slice_reduce_fusion.10
  9.2 8.9 %convolution_convert_fusion = bf16[640,3840]{1,0:T(8,128)(2,1)} fusion(bf16[640,640]{1,0:T(8,128)(2,1)} %refs_1_.8, bf16[3840,640]{1,0:T(8,128)(2,1)} %param.30), kind=kOutput, calls=%fused_computation.6 | convolution fusion | flops 3148185600 | bytes 10649600 | tf_op jit(solution)/shard_map/dot_general | solution.py:72
  18.1 29.7 %shard_map.344 = (f32[2,160,1280]{2,1,0:T(8,128)}, bf16[640,640]{1,0:T(8,128)(2,1)}, f32[8,640]{1,0:T(8,128)}) custom-call(bf16[640,640]{1,0:T(8,128)(2,1)} %refs_2_.3, f32[1,640]{1,0:T(1,128)} %get-tuple-element.532.refs_1_, bf16[2,640,1280]{2,1,0:T(8,128)(2,1)} %refs_1_.11), custom_call_target="tpu_custom_call" | custom-call | tf_op jit(solution)/shard_map/pallas_call | solution.py:312
  60.4 5.5 all-gather.2
  66.3 2.5 fusion.88
  68.8 40.5 %shard_map.346 = (bf16[1,2,2,160,1280]{4,3,2,1,0:T(8,128)(2,1)}, f32[2,320,640]{2,1,0:T(8,128)}, bf16[640,640]{1,0:T(8,128)(2,1)}, f32[8,640]{1,0:T(8,128)}) custom-call(bf16[1,160,1280]{2,1,0:T(8,128)(2,1)} %get-tuple-element.498.refs_0_, bf16[1280,640]{1,0:T(8,128)(2,1)} %refs_1_.10, bf16[640,640]{1,0:T(8,128)(2,1)} %refs_2_.3, ...), custom_call_target="tpu_custom_call" | custom-call | tf_op jit(solution)/shard_map/pallas_call | solution.py:596
  109.3 62.2 %shard_map.347 = f32[2,160,3840]{2,1,0:T(8,128)} custom-call(bf16[2,2,160,640]{3,2,1,0:T(8,128)(2,1)} %bitcast.318, bf16[2,640,3840]{2,1,0:T(8,128)(2,1)} %refs_1_.9), custom_call_target="tpu_custom_call" | custom-call | tf_op jit(solution)/shard_map/pallas_call | solution.py:312
  171.6 3.3 fusion.21.refs_0_
  174.9 31.6 %shard_map.348 = (bf16[1,2,2,160,3840]{4,3,2,1,0:T(8,128)(2,1)S(1)}, bf16[3840,640]{1,0:T(8,128)(2,1)S(1)}) custom-call(bf16[1,160,3840]{2,1,0:T(8,128)(2,1)S(1)} %fusion.21.refs_0_, bf16[640,640]{1,0:T(8,128)(2,1)S(1)} %copy-done), custom_call_target="tpu_custom_call" | custom-call | tf_op jit(solution)/shard_map/pallas_call | solution.py:536
  206.6 2.2 copy-done.1
  208.8 2.2 copy-done.14
  211.0 3.9 fusion.40
  219.0 73.3 %shard_map.349 = (f32[2,320,640]{2,1,0:T(8,128)}, bf16[4,2,160,3840]{3,2,1,0:T(8,128)(2,1)}) custom-call(bf16[2,160,3840]{2,1,0:T(8,128)(2,1)} %pad_maximum_fusion.1.refs_0_, bf16[2,640,3840]{2,1,0:T(8,128)(2,1)} %refs_1_.9, bf16[640,640]{1,0:T(8,128)(2,1)} %bitcast.313), custom_call_target="tpu_custom_call" | custom-call | tf_op jit(solution)/shard_map/pallas_call | solution.py:596
  292.3 12.0 %reduce-scatter.7.cloned.1.call-done = bf16[1,960,640]{2,1,0:T(8,128)(2,1)} async-done(((bf16[4,960,640]{2,1,0:T(8,128)(2,1)}), bf16[1,960,640]{2,1,0:T(8,128)(2,1)}) %reduce-scatter.7.cloned.1.call-update) | async-done | bytes 1228816 | tf_op jit(solution)/shard_map/reduce_scatter | solution.py:742
  310.9 2.0 multiply_reduce_fusion.1
  313.0 7.2 psum.7
  320.2 3.2 fusion.101
  323.5 16.1 %shard_map.350 = f32[1,160,1280]{2,1,0:T(8,128)} custom-call(bf16[2,2,160,640]{3,2,1,0:T(8,128)(2,1)} %bitcast.315, bf16[1280,640]{1,0:T(8,128)(2,1)} %refs_1_.10), custom_call_target="tpu_custom_call" | custom-call | tf_op jit(solution)/shard_map/pallas_call | solution.py:312
  339.5 2.5 fusion.90
  345.1 5.2 all-gather.3
  350.8 3.7 multiply_reduce_fusion.3
  361.4 2.8 convolution_convert_fusion.1
  364.3 3.6 reshape.234
  368.0 17.8 %shard_map.353 = bf16[128,1280]{1,0:T(8,128)(2,1)S(1)} custom-call(bf16[160,1280]{1,0:T(8,128)(2,1)S(1)} %get-tuple-element.500.conv, bf16[160,1280]{1,0:T(8,128)(2,1)S(1)} %get-tuple-element.523.first, bf16[160,1280]{1,0:T(8,128)(2,1)S(1)} %get-tuple-element.522.second), custom_call_target="tpu_custom_call" | custom-call | tf_op jit(solution)/shard_map/pallas_call | solution.py:714
  386.5 9.1 %fusion.36 = bf16[640,640]{1,0:T(8,128)(2,1)} fusion(bf16[3840,640]{1,0:T(8,128)(2,1)} %param.30, bf16[1,640,3840]{2,1,0:T(8,128)(2,1)} %bitcast.298), kind=kOutput, calls=%fused_computation.81 | convolution fusion | flops 3146137600 | bytes 10649600 | tf_op jit(solution)/shard_map/dot_general | solution.py:62
  398.0 38.4 %shard_map.352 = (f32[2,320,640]{2,1,0:T(8,128)}, bf16[4,2,160,1280]{3,2,1,0:T(8,128)(2,1)}) custom-call(bf16[2,160,1280]{2,1,0:T(8,128)(2,1)} %pad_maximum_fusion.4.refs_0_, bf16[2,640,1280]{2,1,0:T(8,128)(2,1)} %refs_1_.11, bf16[640,640]{1,0:T(8,128)(2,1)} %bitcast.312), custom_call_target="tpu_custom_call" | custom-call | tf_op jit(solution)/shard_map/pallas_call | solution.py:596
  436.4 2.2 fusion.27
  438.7 5.3 pad_maximum_fusion
  444.0 2.8 fusion.34
  448.3 26.9 %reduce-scatter.9.cloned.1.call-done = bf16[1,2,160,3840]{3,2,1,0:T(8,128)(2,1)} async-done(((bf16[4,2,160,3840]{3,2,1,0:T(8,128)(2,1)}), bf16[1,2,160,3840]{3,2,1,0:T(8,128)(2,1)}) %reduce-scatter.9.cloned.1.call-update) | async-done | bytes 2457616 | tf_op jit(solution)/shard_map/reduce_scatter | solution.py:742
  481.1 3.0 fusion.1
  484.1 2.2 select_select_fusion
  486.3 2.9 collective-permute-start.3
  489.3 1.9 collective-permute-start.4
  496.9 2.6 convert_bitcast_fusion
  499.5 2.7 fusion
  502.2 148.3 %reduce-scatter.11.cloned.1.call-done = bf16[1,512,1280]{2,1,0:T(8,128)(2,1)} async-done(((bf16[4,512,1280]{2,1,0:T(8,128)(2,1)}), bf16[1,512,1280]{2,1,0:T(8,128)(2,1)}) %reduce-scatter.11.cloned.1.call-update) | async-done | bytes 1310736 | tf_op jit(solution)/shard_map/reduce_scatter | solution.py:742
  650.5 1.9 slice_convert_fusion.1
  652.5 2.2 reshape.239
  654.6 2.2 reshape.237
  656.8 2.5 multiply_add_fusion.5
  666.6 189.4 %shard_map.354 = (bf16[2,160,3840]{2,1,0:T(8,128)(2,1)S(1)}, bf16[960,640]{1,0:T(8,128)(2,1)S(1)}, bf16[2,160,1280]{2,1,0:T(8,128)(2,1)S(1)}, bf16[320,640]{1,0:...) custom-call(bf16[160,3840]{1,0:T(8,128)(2,1)S(1)} %get-tuple-element.327.ref, ...), custom_call_target="tpu_custom_call" | custom-call | tf_op jit(solution)/shard_map/pallas_call | solution.py:1019
  856.2 2.2 fusion.30
  860.2 2.9 subtract_bitcast_fusion.2
  863.1 4.7 subtract_bitcast_fusion
  867.9 1.9 multiply_reduce_fusion
  871.2 2.0 subtract_bitcast_fusion.3
  873.2 3.1 subtract_bitcast_fusion.1
  (299 shorter events, 62.5 us)
Async XLA Ops:
  7.2 203.9 %reduce-scatter.5.cloned.1.call-start = ((), (), s32[]{:S(2)}) async-start(), calls=%async_computation.4 | async-start | bytes 6144000 | tf_op jit(solution)/shard_map/reduce_scatter | solution.py:1108
  9.2 311.0 %copy-start.57 = (f32[640]{0:T(1024)}, f32[640]{0:T(1024)S(1)}, u32[]{:S(2)}) copy-start(f32[640]{0:T(1024)S(1)} %get-tuple-element.463) | copy-start | bytes 7684
  47.9 3.9 copy-start.51
  47.9 256.4 %reduce-scatter.7.cloned.1.call-start = ((), (), s32[]{:S(2)}) async-start(), calls=%async_computation.5 | async-start | bytes 6144000 | tf_op jit(solution)/shard_map/reduce_scatter | solution.py:742
  48.7 4.9 collective-permute-start
  53.6 3.7 copy-start.34
  53.6 3.9 copy-start.73
  171.5 3.4 copy-start
  216.6 258.6 %reduce-scatter.9.cloned.1.call-start = ((), (), s32[]{:S(2)}) async-start(), calls=%async_computation.6 | async-start | bytes 12288000 | tf_op jit(solution)/shard_map/reduce_scatter | solution.py:742
  304.3 346.2 %reduce-scatter.11.cloned.1.call-start = ((), (), s32[]{:S(2)}) async-start(), calls=%async_computation.7 | async-start | bytes 6553600 | tf_op jit(solution)/shard_map/reduce_scatter | solution.py:742
  323.5 16.1 %copy-start.33 = (f32[160,1280]{1,0:T(8,128)S(1)}, f32[160,1280]{1,0:T(8,128)}, u32[]{:S(2)}) copy-start(f32[160,1280]{1,0:T(8,128)} %get-tuple-element.499) | copy-start | bytes 2457604
  323.5 16.1 %copy-start.36 = (f32[2,160,1280]{2,1,0:T(8,128)S(1)}, f32[2,160,1280]{2,1,0:T(8,128)}, u32[]{:S(2)}) copy-start(f32[2,160,1280]{2,1,0:T(8,128)} %get-tuple-element.297) | copy-start | bytes 4915204
  342.1 8.6 copy-start.74
  350.7 3.8 copy-start.16
  350.7 3.8 copy-start.25
  350.7 3.7 copy-start.56
  359.7 26.2 %collective-permute-start.1 = (f32[3,1280]{1,0:T(4,128)S(1)}, f32[3,1280]{1,0:T(4,128)S(1)}, u32[]{:S(2)}, u32[]{:S(2)}) collective-permute-start(f32[3,1280]{1,0:T(4,128)S(1)} %slice.265), channel_id=1, source_target_pairs={{1,0},{2,1},{3,2},{5,4},{6,5},{7,6},{9,8},{10,9},{11,10},{13,12},{... | collective-permute-start | bytes 46088 | tf_op jit(solution)/shard_map/ppermute | solution.py:35
  367.9 17.9 %copy-start.54 = (f32[1280]{0:T(1024)S(1)}, f32[1280]{0:T(1024)}, u32[]{:S(2)}) copy-start(f32[1280]{0:T(1024)} %copy-done.53) | copy-start | bytes 15364
  367.9 17.9 %copy-start.76 = (f32[160]{0:T(256)S(1)}, f32[160]{0:T(256)}, u32[]{:S(2)}) copy-start(f32[160]{0:T(256)} %get-tuple-element.541) | copy-start | bytes 1924
  367.9 18.0 %copy-start.77 = (f32[160]{0:T(256)S(1)}, f32[160]{0:T(256)}, u32[]{:S(2)}) copy-start(f32[160]{0:T(256)} %get-tuple-element.537) | copy-start | bytes 1924
  367.9 18.0 %copy-start.78 = (f32[160]{0:T(256)S(1)}, f32[160]{0:T(256)}, u32[]{:S(2)}) copy-start(f32[160]{0:T(256)} %get-tuple-element.544) | copy-start | bytes 1924
  386.5 10.5 %copy-start.48 = (bf16[1,160,1280]{2,1,0:T(8,128)(2,1)S(1)}, bf16[1,160,1280]{2,1,0:T(8,128)(2,1)}, u32[]{:S(2)}) copy-start(bf16[1,160,1280]{2,1,0:T(8,128)(2,1)} %get-tuple-element.514) | copy-start | bytes 1228804
  395.6 48.5 %collective-permute-start.2 = (bf16[640,640]{1,0:T(8,128)(2,1)}, bf16[640,640]{1,0:T(8,128)(2,1)}, u32[]{:S(2)}, u32[]{:S(2)}) collective-permute-start(bf16[640,640]{1,0:T(8,128)(2,1)} %fusion.36), channel_id=1, source_target_pairs={{0,4},{4,0},{1,5},{5,1},{2,6},{6,2},{3,7},{7,3},{8,12},{12,8},{9,1... | collective-permute-start | bytes 2457608 | tf_op jit(solution)/shard_map/ppermute | solution.py:1202
  398.0 38.4 %copy-start.26 = (bf16[640,640]{1,0:T(8,128)(2,1)S(1)}, bf16[640,640]{1,0:T(8,128)(2,1)}, u32[]{:S(2)}) copy-start(bf16[640,640]{1,0:T(8,128)(2,1)} %refs_2_.3) | copy-start | bytes 2457604
  398.0 38.4 %copy-start.60 = (f32[640]{0:T(1024)S(1)}, f32[640]{0:T(1024)}, u32[]{:S(2)}) copy-start(f32[640]{0:T(1024)} %get-tuple-element.462) | copy-start | bytes 7684
  438.7 5.3 copy-start.18
  475.2 6.0 copy-start.20
  484.1 8.6 copy-start.29
  484.1 15.4 %slice-start = ((s8[4915200]{0:T(1024)(128)(4,1)}), s8[4194304]{0:T(1024)(128)(4,1)S(1)}, s32[]{:S(2)}) async-start(s8[4915200]{0:T(1024)(128)(4,1)} %bitcast.302), calls=%async_computation.8 | async-start | bytes 8388608
  486.3 8.0 copy-start.32
  486.3 177.9 %collective-permute-start.3 = (bf16[160,3840]{1,0:T(8,128)(2,1)}, bf16[160,3840]{1,0:T(8,128)(2,1)S(1)}, u32[]{:S(2)}, u32[]{:S(2)}) collective-permute-start(bf16[160,3840]{1,0:T(8,128)(2,1)} %get-tuple-element.328), channel_id=1, source_target_pairs={{0,8},{16,24},{24,0},{1,9},{17,25},{25,1},{2,10},{18,26},{26,2},{3... | collective-permute-start | bytes 3686408 | tf_op jit(solution)/shard_map/ppermute | solution.py:890
  489.3 176.0 %collective-permute-start.4 = (bf16[160,3840]{1,0:T(8,128)(2,1)}, bf16[160,3840]{1,0:T(8,128)(2,1)}, u32[]{:S(2)}, u32[]{:S(2)}) collective-permute-start(bf16[160,3840]{1,0:T(8,128)(2,1)} %get-tuple-element.329), channel_id=1, source_target_pairs={{8,24},{16,0},{24,8},{9,25},{17,1},{25,9},{10,26},{18,2},{26,10},{... | collective-permute-start | bytes 3686408 | tf_op jit(solution)/shard_map/ppermute | solution.py:890
  491.2 174.1 %collective-permute-start.5 = (bf16[160,3840]{1,0:T(8,128)(2,1)}, bf16[160,3840]{1,0:T(8,128)(2,1)}, u32[]{:S(2)}, u32[]{:S(2)}) collective-permute-start(bf16[160,3840]{1,0:T(8,128)(2,1)} %get-tuple-element.330), channel_id=1, source_target_pairs={{0,24},{8,0},{16,8},{1,25},{9,1},{17,9},{2,26},{10,2},{18,10},{3,2... | collective-permute-start | bytes 3686408 | tf_op jit(solution)/shard_map/ppermute | solution.py:890
  494.3 5.2 slice-start.1
  659.4 3.5 copy-start.22
  666.5 189.6 %copy-start.19 = (f32[2,320,640]{2,1,0:T(8,128)S(1)}, f32[2,320,640]{2,1,0:T(8,128)}, u32[]{:S(2)}) copy-start(f32[2,320,640]{2,1,0:T(8,128)} %get-tuple-element.310) | copy-start | bytes 4915204
  666.5 189.6 %copy-start.23 = (f32[2,320,640]{2,1,0:T(8,128)S(1)}, f32[2,320,640]{2,1,0:T(8,128)}, u32[]{:S(2)}) copy-start(f32[2,320,640]{2,1,0:T(8,128)} %get-tuple-element.309) | copy-start | bytes 4915204
  666.5 189.6 %copy-start.27 = (bf16[640,640]{1,0:T(8,128)(2,1)S(1)}, bf16[640,640]{1,0:T(8,128)(2,1)}, u32[]{:S(2)}) copy-start(bf16[640,640]{1,0:T(8,128)(2,1)} %refs_2_.3) | copy-start | bytes 2457604
  666.5 189.6 %copy-start.39 = (f32[2,320,640]{2,1,0:T(8,128)S(1)}, f32[2,320,640]{2,1,0:T(8,128)}, u32[]{:S(2)}) copy-start(f32[2,320,640]{2,1,0:T(8,128)} %get-tuple-element.317) | copy-start | bytes 4915204
  666.5 189.6 %copy-start.58 = (f32[640]{0:T(1024)S(1)}, f32[640]{0:T(1024)}, u32[]{:S(2)}) copy-start(f32[640]{0:T(1024)} %copy-done.57) | copy-start | bytes 7684
  666.5 189.6 %copy-start.62 = (f32[640]{0:T(1024)S(1)}, f32[640]{0:T(1024)}, u32[]{:S(2)}) copy-start(f32[640]{0:T(1024)} %copy-done.61) | copy-start | bytes 7684
  856.2 3.8 copy-start.75
  858.6 4.6 copy-start.63
  860.0 10.5 %copy-start.52 = (f32[8,1280]{1,0:T(8,128)}, f32[8,1280]{1,0:T(8,128)S(1)}, u32[]{:S(2)}) copy-start(f32[8,1280]{1,0:T(8,128)S(1)} %get-tuple-element.488) | copy-start | bytes 122884
  860.0 9.8 %copy-start.65 = (f32[2,640]{1,0:T(2,128)}, f32[2,640]{1,0:T(2,128)S(1)}, u32[]{:S(2)}) copy-start(f32[2,640]{1,0:T(2,128)S(1)} %get-tuple-element.491) | copy-start | bytes 15364
  863.1 4.8 copy-start.47
  869.8 6.5 copy-start.30
  869.8 3.3 copy-start.5
  (45 other events, 94.9 us)
Sparse Core Ops, SparseCore 0:
  48.0 58.0 reduce-scatter.4
  216.7 87.4 reduce-scatter.6
  306.6 168.4 reduce-scatter.8
  477.4 173.0 reduce-scatter.10

commit v4 on v3

--- a/solution.py
+++ b/solution.py
@@ -193,8 +193,9 @@
     flip, normed, *refs
 ):
     if normed:
-        stream, gain, w, out, low_out, scale_out, lhs, nbuf, nsend, nrecv = refs[:10]
-        refs = refs[10:]
+        stream, gain, cot, w, side_w, out, low_out, scale_out, side_out = refs[:9]
+        lhs, nbuf, side_buf, stage, nsend, nrecv, side_sem, stage_sem = refs[9:17]
+        refs = refs[17:]
     else:
         lhs, w, out = refs[:3]
         refs = refs[3:]
@@ -239,6 +240,28 @@
 
     loop(chunks, lambda j: w_copy(j).start())
     if normed:
+        span = side_buf.shape[1]
+        side_chunks = side_buf.shape[0]
+
+        def side_lines(j):
+            return pl.ds(pl.multiple_of(j * span, span), span)
+
+        def side_copy(j):
+            return pltpu.make_async_copy(
+                side_w.at[side_lines(j), :], side_buf.at[j], side_sem.at[j]
+            )
+
+        def stage_copy(j):
+            return pltpu.make_async_copy(
+                stage.at[j], side_out.at[:, side_lines(j)], stage_sem.at[j]
+            )
+
+        def side_part(j):
+            side_copy(j).wait()
+            stage[j] = dot_nt(cot[...], side_buf[j]).astype(jnp.bfloat16)
+            stage_copy(j).start()
+
+        loop(side_chunks, lambda j: side_copy(j).start())
         greet(col_peers())
         values = stream[...].astype(jnp.float32)
         scales, column = row_scales(values, share_parts("col", nbuf, nsend, nrecv), nbuf)
@@ -279,7 +302,11 @@
 
     loop(chunks - 1, both)
     second(chunks - 1)
+    if normed:
+        loop(side_chunks, side_part)
     loop(chunks, third)
+    if normed:
+        loop(side_chunks, lambda j: stage_copy(j).wait())
 
     def drain(j):
         near_copy(j).wait_send()
@@ -288,7 +315,7 @@
     loop(chunks, drain)
 
 
-def spread_product(lhs, w, flip, width, collective, gain=None):
+def spread_product(lhs, w, flip, width, collective, gain=None, side=None):
     tokens, depth = lhs.shape
     rows = tokens // 4
     pairs = 1 if flip else w.shape[0]
@@ -299,21 +326,31 @@
     local = pl.BlockSpec(memory_space=pltpu.VMEM)
     shapes = [jax.ShapeDtypeStruct((pairs, rows, total), f32)]
     scratch = []
+    anywhere = pl.BlockSpec(memory_space=pl.ANY)
+    weights, remote_outs = [w], []
     if gain is None:
         inputs = [lhs.reshape(2, 2, rows, depth)]
     else:
-        inputs = [lhs, gain[None]]
+        cot, side_w = side
+        span = 768 if side_w.shape[0] % 768 == 0 else 256
+        side_chunks = side_w.shape[0] // span
+        inputs = [lhs, gain[None], cot]
+        weights = [w, side_w]
+        remote_outs = [jax.ShapeDtypeStruct((tokens, side_w.shape[0]), bf16)]
         shapes += [
             jax.ShapeDtypeStruct((tokens, depth), bf16),
             jax.ShapeDtypeStruct((8, tokens), f32),
         ]
         scratch = [pltpu.VMEM((2, 2, rows, depth), bf16), pltpu.VMEM((4, 8, tokens), f32)]
+        scratch += [pltpu.VMEM((side_chunks, span, depth), bf16)]
+        scratch += [pltpu.VMEM((side_chunks, tokens, span), bf16)]
         scratch += [pltpu.SemaphoreType.DMA((4,))] * 2
+        scratch += [pltpu.SemaphoreType.DMA((side_chunks,))] * 2
     result = pl.pallas_call(
         functools.partial(spread_kernel, flip, gain is not None),
-        out_shape=tuple(shapes),
-        in_specs=[local] * len(inputs) + [pl.BlockSpec(memory_space=pl.ANY)],
-        out_specs=[local] * len(shapes),
+        out_shape=tuple(shapes + remote_outs),
+        in_specs=[local] * len(inputs) + [anywhere] * len(weights),
+        out_specs=[local] * len(shapes) + [anywhere] * len(remote_outs),
         scratch_shapes=scratch
         + [
             pltpu.VMEM((chunks,) + tile, bf16),
@@ -327,7 +364,7 @@
         compiler_params=pltpu.CompilerParams(
             collective_id=collective, has_side_effects=True, vmem_limit_bytes=56 * MIB
         ),
-    )(*inputs, w)
+    )(*inputs, *weights)
     return result[0] if gain is None else result
 
 
@@ -871,12 +908,20 @@
 SMALL_OWNER, CON_OWNER, GATE_OWNER, UP_OWNER = (2, 1, 3, 0)
 
 
-def pieces_at_owner(e0, e1, con, later):
+def beside(block, rows):
+    return jnp.concatenate(
+        [block[k * rows : (k + 1) * rows] for k in range(block.shape[0] // rows)], axis=1
+    )
+
+
+def below(block, columns):
+    return jnp.concatenate(
+        [block[:, k * columns : (k + 1) * columns] for k in range(block.shape[1] // columns)]
+    )
+
+
+def pieces_at_owner(e0, e1, packed, later):
     me = lax.axis_index("dp")
-    rows = e0.shape[0]
-    packed = jnp.concatenate(
-        [con[k * rows : (k + 1) * rows] for k in range(con.shape[0] // rows)], axis=1
-    )
 
     def piece_for(owner):
         return jnp.where(owner == GATE_OWNER, e0, jnp.where(owner == UP_OWNER, e1, packed))
@@ -1099,12 +1144,16 @@
         masks.append((earlier == seg_here).astype(f32))
     reset_rows = masks[1][:rows] < 0.5
     stream = block_input.astype(f32)
-    branch_pre, normed_low, scale_rows = spread_product(
-        block_input, branch_weights, False, 640, 2, norm_gains[0]
+    branch_pre, normed_low, scale_rows, contract_term = spread_product(
+        block_input,
+        branch_weights,
+        False,
+        640,
+        2,
+        norm_gains[0],
+        (output_cotangent, contract_weights),
     )
     scale_one = scale_rows[0]
-    contract_term = product_nt(output_cotangent, contract_weights).astype(bf16)
-    contract_term, branch_pre = lax.optimization_barrier((contract_term, branch_pre))
     grad_activated = lax.psum_scatter(contract_term, "col", scatter_dimension=0, tiled=True)
     mixed = branch_pre[0]
     gelu_in = branch_pre[1]
@@ -1219,6 +1268,7 @@
         expand_grad, contract_sum = lax.optimization_barrier((expand_grad, contract_sum))
         expand_sum = pair_sum(expand_grad, 4)
         con_low = (momentum_rate * contract_momentum[0] + contract_sum).astype(bf16)
+        con_low = beside(con_low, expand_momentum.shape[2])
         weighted = grad_normed_one * norm_gains[0][None, :]
         inner_part = jnp.sum(stream * weighted, axis=1)
         gain_one_grad = jnp.sum(grad_normed_one * stream * scale_one[:, None], axis=0)
@@ -1238,7 +1288,7 @@
         small_grad = jnp.concatenate(
             [
                 branch_grad.reshape(4, 2 * piece_rows, lanes),
-                output_grad.astype(bf16).reshape(4, piece_rows, lanes),
+                jnp.stack([beside(part, piece_rows) for part in jnp.split(output_grad.astype(bf16), 4)]),
                 gates_part.reshape(4, -1, lanes),
             ],
             axis=1,
@@ -1255,12 +1305,12 @@
         )
         small_sum = pair_sum(small_grad, 4)
         branch_sum = small_sum[: 2 * piece_rows].reshape(2, piece_rows, lanes)
-        output_sum = small_sum[2 * piece_rows : 3 * piece_rows].reshape(output_momentum.shape[1:])
+        output_sum = below(small_sum[2 * piece_rows : 3 * piece_rows], output_momentum.shape[2])
         branch_low = (momentum_rate * branch_momentum[:, 0] + branch_sum).astype(bf16)
         output_low = (momentum_rate * output_momentum[0] + output_sum).astype(bf16)
         expand_orth, con, branch_orth, out, gates_all, col_total, dp_total = finish_blocks(
             large,
-            con_low.shape,
+            contract_momentum.shape[1:],
             branch_low[0],
             branch_low[1],
             output_low,

time: 893 us -> 882 us (0.988)
  matrix products: 23.1 us -> 8.82 us
    unnamed x176 -> x188, local copies, waits for them, and re-layouts: 21.8 us -> 20.6 us
  transfers between devices with their start and end apart: 10 -> 10, of which waited for: 3 -> 3; matrix products, arithmetic and copies ran while one was open for 11% -> 9% of each run, Pallas kernels for 32% -> 32%
where the time goes in v4:
time: 882 us; the launch traced here: 876 us
  Pallas kernels  509 us (58%)
  waiting for transfers between devices  191 us (22%)
  other arithmetic  84.3 us (10%)
  local copies, waits for them, and re-layouts  37.2 us (4%)
  blocking collectives  18 us (2%)
  between operations  15.3 us (2%)
  starting transfers between devices  11.3 us (1%)
  matrix products  8.82 us (1%)
    pallas_call x1, Pallas kernels, finish_blocks(): pl.pallas_call(tail_kernel, out_shape=tuple(shapes), in_specs=[anywhere]...  196 us
    reduce_scatter x3, waiting for transfers between devices, pair_sum(): return lax.psum_scatter(grad, 'dp', scatter_dimension=0)  191 us
    pallas_call x3, Pallas kernels, meet_product(): pl.pallas_call(functools.partial(meet_kernel, flip, grad_mode), out_shape...  152 us
    pallas_call x3, Pallas kernels, spread_product(): pl.pallas_call(functools.partial(spread_kernel, flip, gain is not None),...  108 us
    pallas_call x1, Pallas kernels, meet_gradient(): pl.pallas_call(functools.partial(meet_kernel, False, 'lone'), out_shape=(...  31.6 us
    unnamed x188, local copies, waits for them, and re-layouts  20.6 us
    pallas_call x1, Pallas kernels, gates_product(): pl.pallas_call(gates_kernel, out_shape=jax.ShapeDtypeStruct((count, lanes...  17.8 us
  transfers between devices with their start and end apart: 10, of which 3 were waited for; matrix products, arithmetic and copies ran while one was open for 9% of the time, Pallas kernels for 32%

profile of v4, /device:TPU:24, one launch (start us, length us, event | category | flops | bytes accessed | tf_op | source)
XLA Modules:
  0.0 875.6 jit_solution(7256633100999518454)
XLA Ops:
  7.2 1.9 slice_reduce_fusion.10
  9.2 30.1 %shard_map.344 = (f32[2,160,1280]{2,1,0:T(8,128)}, bf16[640,640]{1,0:T(8,128)(2,1)}, f32[8,640]{1,0:T(8,128)}, bf16[640,3840]{1,0:T(8,128)(2,1)}) custom-call(bf16[640,640]{1,0:T(8,128)(2,1)} %refs_2_.3, f32[1,640]{1,0:T(1,128)} %get-tuple-element.544.refs_1_, bf16[640,640]{1,0:T(8,128)(2,1)} %refs_1_.8, bf16[2,640,1280]{2,1,0:T(8,128)(2,1)} %refs_1_.11, ...), custom_call_target="tpu_custom_call" | custom-call | tf_op jit(solution)/shard_map/pallas_call | solution.py:349
  47.0 1.7 convolution_bitcast_fusion
  50.1 1.7 shard_map.345
  51.9 5.5 all-gather.2
  57.8 2.5 fusion.88
  60.3 40.5 %shard_map.346 = (bf16[1,2,2,160,1280]{4,3,2,1,0:T(8,128)(2,1)}, f32[2,320,640]{2,1,0:T(8,128)}, bf16[640,640]{1,0:T(8,128)(2,1)}, f32[8,640]{1,0:T(8,128)}) custom-call(bf16[1,160,1280]{2,1,0:T(8,128)(2,1)} %get-tuple-element.498.refs_0_, bf16[1280,640]{1,0:T(8,128)(2,1)} %refs_1_.10, bf16[640,640]{1,0:T(8,128)(2,1)} %refs_2_.3, ...), custom_call_target="tpu_custom_call" | custom-call | tf_op jit(solution)/shard_map/pallas_call | solution.py:633
  100.8 62.3 %shard_map.347 = f32[2,160,3840]{2,1,0:T(8,128)} custom-call(bf16[2,2,160,640]{3,2,1,0:T(8,128)(2,1)} %bitcast.334, bf16[2,640,3840]{2,1,0:T(8,128)(2,1)} %refs_1_.9), custom_call_target="tpu_custom_call" | custom-call | tf_op jit(solution)/shard_map/pallas_call | solution.py:349
  163.1 3.3 fusion.21.refs_0_
  166.4 31.6 %shard_map.348 = (bf16[1,2,2,160,3840]{4,3,2,1,0:T(8,128)(2,1)S(1)}, bf16[3840,640]{1,0:T(8,128)(2,1)S(1)}) custom-call(bf16[1,160,3840]{2,1,0:T(8,128)(2,1)S(1)} %fusion.21.refs_0_, bf16[640,640]{1,0:T(8,128)(2,1)S(1)} %copy-done), custom_call_target="tpu_custom_call" | custom-call | tf_op jit(solution)/shard_map/pallas_call | solution.py:573
  198.1 2.2 copy-done.1
  200.3 2.2 copy-done.14
  202.6 3.9 fusion.40
  206.4 1.7 pad_maximum_fusion.1.refs_0_
  210.5 73.3 %shard_map.349 = (f32[2,320,640]{2,1,0:T(8,128)}, bf16[4,2,160,3840]{3,2,1,0:T(8,128)(2,1)}) custom-call(bf16[2,160,3840]{2,1,0:T(8,128)(2,1)} %pad_maximum_fusion.1.refs_0_, bf16[2,640,3840]{2,1,0:T(8,128)(2,1)} %refs_1_.9, bf16[640,640]{1,0:T(8,128)(2,1)} %bitcast.329), custom_call_target="tpu_custom_call" | custom-call | tf_op jit(solution)/shard_map/pallas_call | solution.py:633
  283.8 12.0 %reduce-scatter.7.cloned.1.call-done = bf16[1,960,640]{2,1,0:T(8,128)(2,1)} async-done(((bf16[4,960,640]{2,1,0:T(8,128)(2,1)}), bf16[1,960,640]{2,1,0:T(8,128)(2,1)}) %reduce-scatter.7.cloned.1.call-update) | async-done | bytes 1228816 | tf_op jit(solution)/shard_map/reduce_scatter | solution.py:779
  302.4 2.0 multiply_reduce_fusion.1
  304.5 7.2 psum.7
  311.7 3.2 fusion.101
  315.0 16.1 %shard_map.350 = f32[1,160,1280]{2,1,0:T(8,128)} custom-call(bf16[2,2,160,640]{3,2,1,0:T(8,128)(2,1)} %bitcast.331, bf16[1280,640]{1,0:T(8,128)(2,1)} %refs_1_.10), custom_call_target="tpu_custom_call" | custom-call | tf_op jit(solution)/shard_map/pallas_call | solution.py:349
  331.1 1.8 fusion.90
  332.9 1.8 shard_map.351
  335.9 5.2 all-gather.3
  341.6 3.7 multiply_reduce_fusion.3
  352.0 1.7 convolution_convert_fusion
  357.3 17.8 %shard_map.353 = bf16[128,1280]{1,0:T(8,128)(2,1)S(1)} custom-call(bf16[160,1280]{1,0:T(8,128)(2,1)S(1)} %get-tuple-element.500.conv, bf16[160,1280]{1,0:T(8,128)(2,1)S(1)} %get-tuple-element.531.first, bf16[160,1280]{1,0:T(8,128)(2,1)S(1)} %get-tuple-element.530.second), custom_call_target="tpu_custom_call" | custom-call | tf_op jit(solution)/shard_map/pallas_call | solution.py:751
  375.7 4.9 fusion.36
  383.0 38.4 %shard_map.352 = (f32[2,320,640]{2,1,0:T(8,128)}, bf16[4,2,160,1280]{3,2,1,0:T(8,128)(2,1)}) custom-call(bf16[2,160,1280]{2,1,0:T(8,128)(2,1)} %pad_maximum_fusion.4.refs_0_, bf16[2,640,1280]{2,1,0:T(8,128)(2,1)} %refs_1_.11, bf16[640,640]{1,0:T(8,128)(2,1)} %bitcast.328), custom_call_target="tpu_custom_call" | custom-call | tf_op jit(solution)/shard_map/pallas_call | solution.py:633
  421.4 2.2 fusion.27
  423.8 7.6 pad_maximum_fusion
  431.4 2.9 fusion.34
  438.8 27.8 %reduce-scatter.9.cloned.1.call-done = bf16[1,2,160,3840]{3,2,1,0:T(8,128)(2,1)} async-done(((bf16[4,2,160,3840]{3,2,1,0:T(8,128)(2,1)}), bf16[1,2,160,3840]{3,2,1,0:T(8,128)(2,1)}) %reduce-scatter.9.cloned.1.call-update) | async-done | bytes 2457616 | tf_op jit(solution)/shard_map/reduce_scatter | solution.py:779
  468.3 3.0 fusion.1
  471.3 3.6 select_select_fusion
  474.9 3.0 collective-permute-start.3
  477.8 1.9 collective-permute-start.4
  482.7 1.7 fusion.5
  485.3 2.6 convert_bitcast_fusion
  487.8 2.7 fusion
  490.6 151.4 %reduce-scatter.11.cloned.1.call-done = bf16[1,512,1280]{2,1,0:T(8,128)(2,1)} async-done(((bf16[4,512,1280]{2,1,0:T(8,128)(2,1)}), bf16[1,512,1280]{2,1,0:T(8,128)(2,1)}) %reduce-scatter.11.cloned.1.call-update) | async-done | bytes 1310736 | tf_op jit(solution)/shard_map/reduce_scatter | solution.py:779
  649.9 195.5 %shard_map.354 = (bf16[2,160,3840]{2,1,0:T(8,128)(2,1)S(1)}, bf16[960,640]{1,0:T(8,128)(2,1)S(1)}, bf16[2,160,1280]{2,1,0:T(8,128)(2,1)S(1)}, bf16[320,640]{1,0:...) custom-call(bf16[160,3840]{1,0:T(8,128)(2,1)S(1)} %get-tuple-element.325.ref, ...), custom_call_target="tpu_custom_call" | custom-call | tf_op jit(solution)/shard_map/pallas_call | solution.py:1064
  845.6 2.2 fusion.30
  849.6 2.9 subtract_bitcast_fusion.2
  852.5 4.7 subtract_bitcast_fusion
  857.3 1.9 multiply_reduce_fusion
  861.9 2.0 subtract_bitcast_fusion.3
  863.9 3.1 subtract_bitcast_fusion.1
  867.0 1.9 multiply_subtract_fusion
  (315 shorter events, 55.8 us)
Async XLA Ops:
  7.2 195.4 %reduce-scatter.5.cloned.1.call-start = ((), (), s32[]{:S(2)}) async-start(), calls=%async_computation.4 | async-start | bytes 6144000 | tf_op jit(solution)/shard_map/reduce_scatter | solution.py:1157
  9.2 302.5 %copy-start.59 = (f32[640]{0:T(1024)}, f32[640]{0:T(1024)S(1)}, u32[]{:S(2)}) copy-start(f32[640]{0:T(1024)S(1)} %get-tuple-element.461) | copy-start | bytes 7684
  39.3 3.9 copy-start.53
  39.4 256.4 %reduce-scatter.7.cloned.1.call-start = ((), (), s32[]{:S(2)}) async-start(), calls=%async_computation.5 | async-start | bytes 6144000 | tf_op jit(solution)/shard_map/reduce_scatter | solution.py:779
  40.2 4.9 collective-permute-start
  45.0 3.7 copy-start.34
  45.1 3.9 copy-start.75
  208.1 258.6 %reduce-scatter.9.cloned.1.call-start = ((), (), s32[]{:S(2)}) async-start(), calls=%async_computation.6 | async-start | bytes 12288000 | tf_op jit(solution)/shard_map/reduce_scatter | solution.py:779
  295.8 346.2 %reduce-scatter.11.cloned.1.call-start = ((), (), s32[]{:S(2)}) async-start(), calls=%async_computation.7 | async-start | bytes 6553600 | tf_op jit(solution)/shard_map/reduce_scatter | solution.py:779
  315.0 16.1 %copy-start.33 = (f32[160,1280]{1,0:T(8,128)S(1)}, f32[160,1280]{1,0:T(8,128)}, u32[]{:S(2)}) copy-start(f32[160,1280]{1,0:T(8,128)} %get-tuple-element.499) | copy-start | bytes 2457604
  315.0 16.1 %copy-start.36 = (f32[2,160,1280]{2,1,0:T(8,128)S(1)}, f32[2,160,1280]{2,1,0:T(8,128)}, u32[]{:S(2)}) copy-start(f32[2,160,1280]{2,1,0:T(8,128)} %get-tuple-element.295) | copy-start | bytes 4915204
  332.9 8.7 copy-start.76
  341.5 3.8 copy-start.16
  341.5 3.8 copy-start.25
  341.5 3.7 copy-start.58
  350.5 24.5 %collective-permute-start.1 = (f32[3,1280]{1,0:T(4,128)S(1)}, f32[3,1280]{1,0:T(4,128)S(1)}, u32[]{:S(2)}, u32[]{:S(2)}) collective-permute-start(f32[3,1280]{1,0:T(4,128)S(1)} %slice.322), channel_id=1, source_target_pairs={{1,0},{2,1},{3,2},{5,4},{6,5},{7,6},{9,8},{10,9},{11,10},{13,12},{... | collective-permute-start | bytes 46088 | tf_op jit(solution)/shard_map/ppermute | solution.py:35
  352.0 23.7 %slice-start = ((s8[4915200]{0:T(1024)(128)(4,1)}), s8[4194304]{0:T(1024)(128)(4,1)S(1)}, s32[]{:S(2)}) async-start(s8[4915200]{0:T(1024)(128)(4,1)} %bitcast.310), calls=%async_computation.8 | async-start | bytes 8388608
  352.0 23.7 %slice-start.4 = ((s8[4915200]{0:T(1024)(128)(4,1)}), s8[4194304]{0:T(1024)(128)(4,1)S(1)}, s32[]{:S(2)}) async-start(s8[4915200]{0:T(1024)(128)(4,1)} %bitcast.324), calls=%async_computation.12 | async-start | bytes 8388608
  353.7 22.0 %slice-start.1 = ((s8[4915200]{0:T(1024)(128)(4,1)}), s8[720896]{0:T(1024)(128)(4,1)S(1)}, s32[]{:S(2)}) async-start(s8[4915200]{0:T(1024)(128)(4,1)} %bitcast.310), calls=%async_computation.9 | async-start | bytes 1441792
  353.7 22.0 %slice-start.5 = ((s8[4915200]{0:T(1024)(128)(4,1)}), s8[720896]{0:T(1024)(128)(4,1)S(1)}, s32[]{:S(2)}) async-start(s8[4915200]{0:T(1024)(128)(4,1)} %bitcast.324), calls=%async_computation.13 | async-start | bytes 1441792
  356.4 18.7 %copy-start.56 = (f32[1280]{0:T(1024)S(1)}, f32[1280]{0:T(1024)}, u32[]{:S(2)}) copy-start(f32[1280]{0:T(1024)} %copy-done.55) | copy-start | bytes 15364
  356.4 18.7 %copy-start.78 = (f32[160]{0:T(256)S(1)}, f32[160]{0:T(256)}, u32[]{:S(2)}) copy-start(f32[160]{0:T(256)} %get-tuple-element.553) | copy-start | bytes 1924
  356.4 18.7 %copy-start.79 = (f32[160]{0:T(256)S(1)}, f32[160]{0:T(256)}, u32[]{:S(2)}) copy-start(f32[160]{0:T(256)} %get-tuple-element.549) | copy-start | bytes 1924
  356.4 18.7 %copy-start.80 = (f32[160]{0:T(256)S(1)}, f32[160]{0:T(256)}, u32[]{:S(2)}) copy-start(f32[160]{0:T(256)} %get-tuple-element.556) | copy-start | bytes 1924
  380.6 50.8 %collective-permute-start.2 = (bf16[640,640]{1,0:T(8,128)(2,1)}, bf16[640,640]{1,0:T(8,128)(2,1)}, u32[]{:S(2)}, u32[]{:S(2)}) collective-permute-start(bf16[640,640]{1,0:T(8,128)(2,1)} %fusion.36), channel_id=1, source_target_pairs={{0,4},{4,0},{1,5},{5,1},{2,6},{6,2},{3,7},{7,3},{8,12},{12,8},{9,1... | collective-permute-start | bytes 2457608 | tf_op jit(solution)/shard_map/ppermute | solution.py:1251
  383.0 38.4 %copy-start.26 = (bf16[640,640]{1,0:T(8,128)(2,1)S(1)}, bf16[640,640]{1,0:T(8,128)(2,1)}, u32[]{:S(2)}) copy-start(bf16[640,640]{1,0:T(8,128)(2,1)} %refs_2_.3) | copy-start | bytes 2457604
  383.0 38.4 %copy-start.62 = (f32[640]{0:T(1024)S(1)}, f32[640]{0:T(1024)}, u32[]{:S(2)}) copy-start(f32[640]{0:T(1024)} %get-tuple-element.460) | copy-start | bytes 7684
  423.8 7.6 copy-start.18
  471.3 9.8 %copy-start.29 = (bf16[1,960,640]{2,1,0:T(8,128)(2,1)S(1)}, bf16[1,960,640]{2,1,0:T(8,128)(2,1)}, u32[]{:S(2)}) copy-start(bf16[1,960,640]{2,1,0:T(8,128)(2,1)} %reduce-scatter.7.cloned.1.call-done) | copy-start | bytes 3686404
  471.3 16.5 %slice-start.2 = ((s8[4915200]{0:T(1024)(128)(4,1)}), s8[4194304]{0:T(1024)(128)(4,1)S(1)}, s32[]{:S(2)}) async-start(s8[4915200]{0:T(1024)(128)(4,1)} %bitcast.316), calls=%async_computation.10 | async-start | bytes 8388608
  474.9 7.8 copy-start.32
  474.9 172.6 %collective-permute-start.3 = (bf16[160,3840]{1,0:T(8,128)(2,1)}, bf16[160,3840]{1,0:T(8,128)(2,1)S(1)}, u32[]{:S(2)}, u32[]{:S(2)}) collective-permute-start(bf16[160,3840]{1,0:T(8,128)(2,1)} %get-tuple-element.326), channel_id=1, source_target_pairs={{0,8},{16,24},{24,0},{1,9},{17,25},{25,1},{2,10},{18,26},{26,2},{3... | collective-permute-start | bytes 3686408 | tf_op jit(solution)/shard_map/ppermute | solution.py:935
  477.8 170.7 %collective-permute-start.4 = (bf16[160,3840]{1,0:T(8,128)(2,1)}, bf16[160,3840]{1,0:T(8,128)(2,1)}, u32[]{:S(2)}, u32[]{:S(2)}) collective-permute-start(bf16[160,3840]{1,0:T(8,128)(2,1)} %get-tuple-element.327), channel_id=1, source_target_pairs={{8,24},{16,0},{24,8},{9,25},{17,1},{25,9},{10,26},{18,2},{26,10},{... | collective-permute-start | bytes 3686408 | tf_op jit(solution)/shard_map/ppermute | solution.py:935
  479.8 168.8 %collective-permute-start.5 = (bf16[160,3840]{1,0:T(8,128)(2,1)}, bf16[160,3840]{1,0:T(8,128)(2,1)}, u32[]{:S(2)}, u32[]{:S(2)}) collective-permute-start(bf16[160,3840]{1,0:T(8,128)(2,1)} %get-tuple-element.328), channel_id=1, source_target_pairs={{0,24},{8,0},{16,8},{1,25},{9,1},{17,9},{2,26},{10,2},{18,10},{3,2... | collective-permute-start | bytes 3686408 | tf_op jit(solution)/shard_map/ppermute | solution.py:935
  482.7 5.2 slice-start.3
  649.8 195.7 %copy-start.19 = (f32[2,320,640]{2,1,0:T(8,128)S(1)}, f32[2,320,640]{2,1,0:T(8,128)}, u32[]{:S(2)}) copy-start(f32[2,320,640]{2,1,0:T(8,128)} %get-tuple-element.308) | copy-start | bytes 4915204
  649.8 195.7 %copy-start.23 = (f32[2,320,640]{2,1,0:T(8,128)S(1)}, f32[2,320,640]{2,1,0:T(8,128)}, u32[]{:S(2)}) copy-start(f32[2,320,640]{2,1,0:T(8,128)} %get-tuple-element.307) | copy-start | bytes 4915204
  649.8 195.7 %copy-start.27 = (bf16[640,640]{1,0:T(8,128)(2,1)S(1)}, bf16[640,640]{1,0:T(8,128)(2,1)}, u32[]{:S(2)}) copy-start(bf16[640,640]{1,0:T(8,128)(2,1)} %refs_2_.3) | copy-start | bytes 2457604
  649.8 195.7 %copy-start.39 = (f32[2,320,640]{2,1,0:T(8,128)S(1)}, f32[2,320,640]{2,1,0:T(8,128)}, u32[]{:S(2)}) copy-start(f32[2,320,640]{2,1,0:T(8,128)} %get-tuple-element.315) | copy-start | bytes 4915204
  649.8 195.7 %copy-start.60 = (f32[640]{0:T(1024)S(1)}, f32[640]{0:T(1024)}, u32[]{:S(2)}) copy-start(f32[640]{0:T(1024)} %copy-done.59) | copy-start | bytes 7684
  649.9 195.7 %copy-start.64 = (f32[640]{0:T(1024)S(1)}, f32[640]{0:T(1024)}, u32[]{:S(2)}) copy-start(f32[640]{0:T(1024)} %copy-done.63) | copy-start | bytes 7684
  845.6 3.8 copy-start.77
  847.9 4.6 copy-start.65
  849.4 11.8 %copy-start.54 = (f32[8,1280]{1,0:T(8,128)}, f32[8,1280]{1,0:T(8,128)S(1)}, u32[]{:S(2)}) copy-start(f32[8,1280]{1,0:T(8,128)S(1)} %get-tuple-element.488) | copy-start | bytes 122884
  849.4 11.2 %copy-start.67 = (f32[2,640]{1,0:T(2,128)}, f32[2,640]{1,0:T(2,128)S(1)}, u32[]{:S(2)}) copy-start(f32[2,640]{1,0:T(2,128)S(1)} %get-tuple-element.491) | copy-start | bytes 15364
  852.5 4.8 copy-start.47
  859.2 7.8 copy-start.30
  859.3 4.6 copy-start.5
  (51 other events, 107.1 us)
Sparse Core Ops, SparseCore 0:
  39.5 58.0 reduce-scatter.4
  208.2 87.5 reduce-scatter.6
  298.2 168.4 reduce-scatter.8
  468.9 173.0 reduce-scatter.10

commit v5 on v4

--- a/solution.py
+++ b/solution.py
@@ -971,6 +971,23 @@
         [("dp", lax.rem(me + step, 4)) for step in range(1, 4)]
         + [("col", lax.rem(place + step, 4)) for step in range(1, 4)]
     )
+    def loads(owner, target):
+        return [
+            pltpu.make_async_copy(large[step], target((owner - step) % 4), load_sem.at[step])
+            for step in range(4)
+        ]
+
+    for owner in (CON_OWNER, GATE_OWNER, UP_OWNER):
+
+        @pl.when(me == owner)
+        def _():
+            if owner == CON_OWNER:
+                copies = loads(owner, lambda j: packed.at[j])
+            else:
+                copies = loads(owner, lambda j: x.at[pl.ds(j * rows, rows)])
+            for copy in copies:
+                copy.start()
+
     shares[0][0](col_part[...])
     shares[2][0](gates_piece[...])
     start(0, 1, 2)
@@ -981,31 +998,21 @@
     shares[2][1]()
     shares[3][0](gates_dp[...].reshape(gates_col.shape[1:]))
 
-    def load(owner, target):
-        copies = [
-            pltpu.make_async_copy(large[step], target((owner - step) % 4), load_sem.at[step])
-            for step in range(4)
-        ]
-        for copy in copies:
-            copy.start()
-        for copy in copies:
-            copy.wait()
-
     @pl.when(me == CON_OWNER)
     def _():
-        load(CON_OWNER, lambda j: packed.at[j])
+        for copy in loads(CON_OWNER, lambda j: packed.at[j]):
+            copy.wait()
         for j in range(4):
             for k in range(width // rows):
                 first_column = j * width + k * rows
                 x[:, first_column : first_column + rows] = packed[j, :, k * side : (k + 1) * side].T
 
-    @pl.when(me == GATE_OWNER)
-    def _():
-        load(GATE_OWNER, lambda j: x.at[pl.ds(j * rows, rows)])
-
-    @pl.when(me == UP_OWNER)
-    def _():
-        load(UP_OWNER, lambda j: x.at[pl.ds(j * rows, rows)])
+    for owner in (GATE_OWNER, UP_OWNER):
+
+        @pl.when(me == owner)
+        def _():
+            for copy in loads(owner, lambda j: x.at[pl.ds(j * rows, rows)]):
+                copy.wait()
 
     @pl.when(me != SMALL_OWNER)
     def _():
@@ -1205,10 +1212,11 @@
 
     activated, pull_geglu = jax.vjp(geglu, expand_pre[0], expand_pre[1])
     activated_low = activated.astype(bf16)
+    activated_low, grad_activated = lax.optimization_barrier((activated_low, grad_activated))
     activated_all, contract_grad = meet_gradient(activated_low[None], 640, 5, output_cotangent)
     cot_values = output_cotangent.astype(f32)
-    grad_activated = grad_activated.astype(f32)
-    grad_gate, grad_up = pull_geglu(grad_activated)
+    grad_activated, contract_grad = lax.optimization_barrier((grad_activated, contract_grad))
+    grad_gate, grad_up = pull_geglu(grad_activated.astype(f32))
     grad_expand_low = jnp.stack([grad_gate, grad_up]).astype(bf16)
     grad_expand_low, contract_grad = lax.optimization_barrier((grad_expand_low, contract_grad))
     parts = dp_count if feature_count % (16 * dp_count) == 0 else 1

time: 882 us -> 882 us (level)
    unnamed x188 -> x190, local copies, waits for them, and re-layouts: 20.6 us -> 18.3 us
  transfers between devices with their start and end apart: 10 -> 10, of which waited for: 3 -> 3; matrix products, arithmetic and copies ran while one was open for 9% -> 9% of each run, Pallas kernels for 32% -> 29%
where the time goes in v5:
time: 882 us; the launch traced here: 876 us
  Pallas kernels  510 us (58%)
  waiting for transfers between devices  191 us (22%)
  other arithmetic  85.9 us (10%)
  local copies, waits for them, and re-layouts  35 us (4%)
  blocking collectives  18 us (2%)
  between operations  15.4 us (2%)
  starting transfers between devices  11.3 us (1%)
  matrix products  8.82 us (1%)
    pallas_call x1, Pallas kernels, finish_blocks(): pl.pallas_call(tail_kernel, out_shape=tuple(shapes), in_specs=[anywhere]...  196 us
    reduce_scatter x3, waiting for transfers between devices, pair_sum(): return lax.psum_scatter(grad, 'dp', scatter_dimension=0)  191 us
    pallas_call x3, Pallas kernels, meet_product(): pl.pallas_call(functools.partial(meet_kernel, flip, grad_mode), out_shape...  152 us
    pallas_call x3, Pallas kernels, spread_product(): pl.pallas_call(functools.partial(spread_kernel, flip, gain is not None),...  108 us
    pallas_call x1, Pallas kernels, meet_gradient(): pl.pallas_call(functools.partial(meet_kernel, False, 'lone'), out_shape=(...  31.6 us
    unnamed x190, local copies, waits for them, and re-layouts  18.3 us
    pallas_call x1, Pallas kernels, gates_product(): pl.pallas_call(gates_kernel, out_shape=jax.ShapeDtypeStruct((count, lanes...  17.8 us
  transfers between devices with their start and end apart: 10, of which 3 were waited for; matrix products, arithmetic and copies ran while one was open for 9% of the time, Pallas kernels for 29%

profile of v5, /device:TPU:24, one launch (start us, length us, event | category | flops | bytes accessed | tf_op | source)
XLA Modules:
  0.0 875.7 jit_solution(17426029462201911614)
XLA Ops:
  7.2 1.9 slice_reduce_fusion.10
  9.2 30.1 %shard_map.344 = (f32[2,160,1280]{2,1,0:T(8,128)}, bf16[640,640]{1,0:T(8,128)(2,1)}, f32[8,640]{1,0:T(8,128)}, bf16[640,3840]{1,0:T(8,128)(2,1)}) custom-call(bf16[640,640]{1,0:T(8,128)(2,1)} %refs_2_.3, f32[1,640]{1,0:T(1,128)} %get-tuple-element.552.refs_1_, bf16[640,640]{1,0:T(8,128)(2,1)} %refs_1_.8, bf16[2,640,1280]{2,1,0:T(8,128)(2,1)} %refs_1_.11, ...), custom_call_target="tpu_custom_call" | custom-call | tf_op jit(solution)/shard_map/pallas_call | solution.py:349
  47.0 1.7 convolution_bitcast_fusion
  50.1 1.7 shard_map.345
  51.9 5.5 all-gather.2
  57.8 2.5 fusion.80
  60.3 40.5 %shard_map.346 = (bf16[1,2,2,160,1280]{4,3,2,1,0:T(8,128)(2,1)}, f32[2,320,640]{2,1,0:T(8,128)}, bf16[640,640]{1,0:T(8,128)(2,1)}, f32[8,640]{1,0:T(8,128)}) custom-call(bf16[1,160,1280]{2,1,0:T(8,128)(2,1)} %get-tuple-element.506.refs_0_, bf16[1280,640]{1,0:T(8,128)(2,1)} %refs_1_.10, bf16[640,640]{1,0:T(8,128)(2,1)} %refs_2_.3, ...), custom_call_target="tpu_custom_call" | custom-call | tf_op jit(solution)/shard_map/pallas_call | solution.py:633
  100.8 62.2 %shard_map.347 = f32[2,160,3840]{2,1,0:T(8,128)} custom-call(bf16[2,2,160,640]{3,2,1,0:T(8,128)(2,1)} %bitcast.339, bf16[2,640,3840]{2,1,0:T(8,128)(2,1)} %refs_1_.9), custom_call_target="tpu_custom_call" | custom-call | tf_op jit(solution)/shard_map/pallas_call | solution.py:349
  163.1 3.3 fusion.13
  166.5 31.6 %shard_map.348 = (bf16[1,2,2,160,3840]{4,3,2,1,0:T(8,128)(2,1)S(1)}, bf16[3840,640]{1,0:T(8,128)(2,1)S(1)}) custom-call(bf16[1,160,3840]{2,1,0:T(8,128)(2,1)S(1)} %bitcast.313, bf16[640,640]{1,0:T(8,128)(2,1)S(1)} %copy-done), custom_call_target="tpu_custom_call" | custom-call | tf_op jit(solution)/shard_map/pallas_call | solution.py:573
  198.1 2.2 copy-done.14
  200.3 5.5 fusion.32
  205.8 1.7 pad_maximum_fusion.1.refs_0_
  209.9 73.3 %shard_map.349 = (f32[2,320,640]{2,1,0:T(8,128)}, bf16[4,2,160,3840]{3,2,1,0:T(8,128)(2,1)}) custom-call(bf16[2,160,3840]{2,1,0:T(8,128)(2,1)} %pad_maximum_fusion.1.refs_0_, bf16[2,640,3840]{2,1,0:T(8,128)(2,1)} %refs_1_.9, bf16[640,640]{1,0:T(8,128)(2,1)} %bitcast.334), custom_call_target="tpu_custom_call" | custom-call | tf_op jit(solution)/shard_map/pallas_call | solution.py:633
  283.2 12.0 %reduce-scatter.7.cloned.1.call-done = bf16[1,960,640]{2,1,0:T(8,128)(2,1)} async-done(((bf16[4,960,640]{2,1,0:T(8,128)(2,1)}), bf16[1,960,640]{2,1,0:T(8,128)(2,1)}) %reduce-scatter.7.cloned.1.call-update) | async-done | bytes 1228816 | tf_op jit(solution)/shard_map/reduce_scatter | solution.py:779
  301.8 2.0 multiply_reduce_fusion.1
  303.9 7.2 psum.7
  311.2 3.2 fusion.93
  314.4 16.1 %shard_map.350 = f32[1,160,1280]{2,1,0:T(8,128)} custom-call(bf16[2,2,160,640]{3,2,1,0:T(8,128)(2,1)} %bitcast.336, bf16[1280,640]{1,0:T(8,128)(2,1)} %refs_1_.10), custom_call_target="tpu_custom_call" | custom-call | tf_op jit(solution)/shard_map/pallas_call | solution.py:349
  330.5 1.8 fusion.82
  332.3 1.8 shard_map.351
  335.3 5.2 all-gather.3
  341.0 3.7 multiply_reduce_fusion.3
  351.5 1.7 convolution_convert_fusion
  356.7 17.8 %shard_map.353 = bf16[128,1280]{1,0:T(8,128)(2,1)S(1)} custom-call(bf16[160,1280]{1,0:T(8,128)(2,1)S(1)} %get-tuple-element.508.conv, bf16[160,1280]{1,0:T(8,128)(2,1)S(1)} %get-tuple-element.539.first, bf16[160,1280]{1,0:T(8,128)(2,1)S(1)} %get-tuple-element.538.second), custom_call_target="tpu_custom_call" | custom-call | tf_op jit(solution)/shard_map/pallas_call | solution.py:751
  375.1 4.9 fusion.28
  382.5 38.3 %shard_map.352 = (f32[2,320,640]{2,1,0:T(8,128)}, bf16[4,2,160,1280]{3,2,1,0:T(8,128)(2,1)}) custom-call(bf16[2,160,1280]{2,1,0:T(8,128)(2,1)} %pad_maximum_fusion.4.refs_0_, bf16[2,640,1280]{2,1,0:T(8,128)(2,1)} %refs_1_.11, bf16[640,640]{1,0:T(8,128)(2,1)} %bitcast.333), custom_call_target="tpu_custom_call" | custom-call | tf_op jit(solution)/shard_map/pallas_call | solution.py:633
  420.8 2.2 fusion.19
  423.2 7.6 pad_maximum_fusion
  430.8 2.9 fusion.26
  438.2 27.8 %reduce-scatter.9.cloned.1.call-done = bf16[1,2,160,3840]{3,2,1,0:T(8,128)(2,1)} async-done(((bf16[4,2,160,3840]{3,2,1,0:T(8,128)(2,1)}), bf16[1,2,160,3840]{3,2,1,0:T(8,128)(2,1)}) %reduce-scatter.9.cloned.1.call-update) | async-done | bytes 2457616 | tf_op jit(solution)/shard_map/reduce_scatter | solution.py:779
  466.1 1.6 copy-done.20
  467.8 3.0 fusion.1
  470.7 3.6 select_select_fusion
  474.3 3.0 collective-permute-start.3
  477.3 1.9 collective-permute-start.4
  482.1 1.7 fusion.5
  484.7 2.6 convert_bitcast_fusion
  487.3 2.7 fusion
  490.0 151.4 %reduce-scatter.11.cloned.1.call-done = bf16[1,512,1280]{2,1,0:T(8,128)(2,1)} async-done(((bf16[4,512,1280]{2,1,0:T(8,128)(2,1)}), bf16[1,512,1280]{2,1,0:T(8,128)(2,1)}) %reduce-scatter.11.cloned.1.call-update) | async-done | bytes 1310736 | tf_op jit(solution)/shard_map/reduce_scatter | solution.py:779
  649.3 196.2 %shard_map.354 = (bf16[2,160,3840]{2,1,0:T(8,128)(2,1)S(1)}, bf16[960,640]{1,0:T(8,128)(2,1)S(1)}, bf16[2,160,1280]{2,1,0:T(8,128)(2,1)S(1)}, bf16[320,640]{1,0:...) custom-call(bf16[160,3840]{1,0:T(8,128)(2,1)S(1)} %get-tuple-element.333.ref, ...), custom_call_target="tpu_custom_call" | custom-call | tf_op jit(solution)/shard_map/pallas_call | solution.py:1071
  845.7 2.2 fusion.22
  849.7 2.9 subtract_bitcast_fusion.2
  852.6 4.7 subtract_bitcast_fusion
  857.4 1.9 multiply_reduce_fusion
  862.0 2.0 subtract_bitcast_fusion.3
  864.0 3.1 subtract_bitcast_fusion.1
  867.1 1.9 multiply_subtract_fusion
  (317 shorter events, 54.2 us)
Async XLA Ops:
  7.2 159.2 %reduce-scatter.5.cloned.1.call-start = ((), (), s32[]{:S(2)}) async-start(), calls=%async_computation.4 | async-start | bytes 6144000 | tf_op jit(solution)/shard_map/reduce_scatter | solution.py:1164
  9.2 302.0 %copy-start.60 = (f32[640]{0:T(1024)}, f32[640]{0:T(1024)S(1)}, u32[]{:S(2)}) copy-start(f32[640]{0:T(1024)S(1)} %get-tuple-element.469) | copy-start | bytes 7684
  39.3 3.9 copy-start.54
  39.4 255.8 %reduce-scatter.7.cloned.1.call-start = ((), (), s32[]{:S(2)}) async-start(), calls=%async_computation.5 | async-start | bytes 6144000 | tf_op jit(solution)/shard_map/reduce_scatter | solution.py:779
  40.2 4.9 collective-permute-start
  45.1 3.9 copy-start.76
  166.4 33.9 %copy-start.50 = (bf16[160,3840]{1,0:T(8,128)(2,1)S(1)}, bf16[160,3840]{1,0:T(8,128)(2,1)}, u32[]{:S(2)}) copy-start(bf16[160,3840]{1,0:T(8,128)(2,1)} %reduce-scatter.5.cloned.1.call-done) | copy-start | bytes 3686404
  200.3 5.5 copy-start.1
  207.5 258.6 %reduce-scatter.9.cloned.1.call-start = ((), (), s32[]{:S(2)}) async-start(), calls=%async_computation.6 | async-start | bytes 12288000 | tf_op jit(solution)/shard_map/reduce_scatter | solution.py:779
  295.2 346.2 %reduce-scatter.11.cloned.1.call-start = ((), (), s32[]{:S(2)}) async-start(), calls=%async_computation.7 | async-start | bytes 6553600 | tf_op jit(solution)/shard_map/reduce_scatter | solution.py:779
  314.4 16.1 %copy-start.33 = (f32[160,1280]{1,0:T(8,128)S(1)}, f32[160,1280]{1,0:T(8,128)}, u32[]{:S(2)}) copy-start(f32[160,1280]{1,0:T(8,128)} %get-tuple-element.507) | copy-start | bytes 2457604
  314.4 16.1 %copy-start.36 = (f32[2,160,1280]{2,1,0:T(8,128)S(1)}, f32[2,160,1280]{2,1,0:T(8,128)}, u32[]{:S(2)}) copy-start(f32[2,160,1280]{2,1,0:T(8,128)} %get-tuple-element.298) | copy-start | bytes 4915204
  332.3 8.7 copy-start.77
  340.9 3.8 copy-start.16
  340.9 3.8 copy-start.25
  349.9 24.5 %collective-permute-start.1 = (f32[3,1280]{1,0:T(4,128)S(1)}, f32[3,1280]{1,0:T(4,128)S(1)}, u32[]{:S(2)}, u32[]{:S(2)}) collective-permute-start(f32[3,1280]{1,0:T(4,128)S(1)} %slice.322), channel_id=1, source_target_pairs={{1,0},{2,1},{3,2},{5,4},{6,5},{7,6},{9,8},{10,9},{11,10},{13,12},{... | collective-permute-start | bytes 46088 | tf_op jit(solution)/shard_map/ppermute | solution.py:35
  351.4 23.7 %slice-start = ((s8[4915200]{0:T(1024)(128)(4,1)}), s8[4194304]{0:T(1024)(128)(4,1)S(1)}, s32[]{:S(2)}) async-start(s8[4915200]{0:T(1024)(128)(4,1)} %bitcast.315), calls=%async_computation.8 | async-start | bytes 8388608
  351.4 23.7 %slice-start.4 = ((s8[4915200]{0:T(1024)(128)(4,1)}), s8[4194304]{0:T(1024)(128)(4,1)S(1)}, s32[]{:S(2)}) async-start(s8[4915200]{0:T(1024)(128)(4,1)} %bitcast.329), calls=%async_computation.12 | async-start | bytes 8388608
  353.1 22.0 %slice-start.1 = ((s8[4915200]{0:T(1024)(128)(4,1)}), s8[720896]{0:T(1024)(128)(4,1)S(1)}, s32[]{:S(2)}) async-start(s8[4915200]{0:T(1024)(128)(4,1)} %bitcast.315), calls=%async_computation.9 | async-start | bytes 1441792
  353.2 22.0 %slice-start.5 = ((s8[4915200]{0:T(1024)(128)(4,1)}), s8[720896]{0:T(1024)(128)(4,1)S(1)}, s32[]{:S(2)}) async-start(s8[4915200]{0:T(1024)(128)(4,1)} %bitcast.329), calls=%async_computation.13 | async-start | bytes 1441792
  355.8 18.7 %copy-start.57 = (f32[1280]{0:T(1024)S(1)}, f32[1280]{0:T(1024)}, u32[]{:S(2)}) copy-start(f32[1280]{0:T(1024)} %copy-done.56) | copy-start | bytes 15364
  355.8 18.7 %copy-start.79 = (f32[160]{0:T(256)S(1)}, f32[160]{0:T(256)}, u32[]{:S(2)}) copy-start(f32[160]{0:T(256)} %get-tuple-element.561) | copy-start | bytes 1924
  355.8 18.7 %copy-start.80 = (f32[160]{0:T(256)S(1)}, f32[160]{0:T(256)}, u32[]{:S(2)}) copy-start(f32[160]{0:T(256)} %get-tuple-element.557) | copy-start | bytes 1924
  355.8 18.7 %copy-start.81 = (f32[160]{0:T(256)S(1)}, f32[160]{0:T(256)}, u32[]{:S(2)}) copy-start(f32[160]{0:T(256)} %get-tuple-element.564) | copy-start | bytes 1924
  380.0 50.8 %collective-permute-start.2 = (bf16[640,640]{1,0:T(8,128)(2,1)}, bf16[640,640]{1,0:T(8,128)(2,1)}, u32[]{:S(2)}, u32[]{:S(2)}) collective-permute-start(bf16[640,640]{1,0:T(8,128)(2,1)} %fusion.28), channel_id=1, source_target_pairs={{0,4},{4,0},{1,5},{5,1},{2,6},{6,2},{3,7},{7,3},{8,12},{12,8},{9,1... | collective-permute-start | bytes 2457608 | tf_op jit(solution)/shard_map/ppermute | solution.py:1259
  382.4 38.4 %copy-start.26 = (bf16[640,640]{1,0:T(8,128)(2,1)S(1)}, bf16[640,640]{1,0:T(8,128)(2,1)}, u32[]{:S(2)}) copy-start(bf16[640,640]{1,0:T(8,128)(2,1)} %refs_2_.3) | copy-start | bytes 2457604
  382.5 38.4 %copy-start.63 = (f32[640]{0:T(1024)S(1)}, f32[640]{0:T(1024)}, u32[]{:S(2)}) copy-start(f32[640]{0:T(1024)} %get-tuple-element.468) | copy-start | bytes 7684
  423.2 7.6 copy-start.18
  470.7 9.8 %copy-start.29 = (bf16[1,960,640]{2,1,0:T(8,128)(2,1)S(1)}, bf16[1,960,640]{2,1,0:T(8,128)(2,1)}, u32[]{:S(2)}) copy-start(bf16[1,960,640]{2,1,0:T(8,128)(2,1)} %reduce-scatter.7.cloned.1.call-done) | copy-start | bytes 3686404
  470.7 16.6 %slice-start.2 = ((s8[4915200]{0:T(1024)(128)(4,1)}), s8[4194304]{0:T(1024)(128)(4,1)S(1)}, s32[]{:S(2)}) async-start(s8[4915200]{0:T(1024)(128)(4,1)} %bitcast.321), calls=%async_computation.10 | async-start | bytes 8388608
  474.3 7.8 copy-start.32
  474.3 172.6 %collective-permute-start.3 = (bf16[160,3840]{1,0:T(8,128)(2,1)}, bf16[160,3840]{1,0:T(8,128)(2,1)S(1)}, u32[]{:S(2)}, u32[]{:S(2)}) collective-permute-start(bf16[160,3840]{1,0:T(8,128)(2,1)} %get-tuple-element.334), channel_id=1, source_target_pairs={{0,8},{16,24},{24,0},{1,9},{17,25},{25,1},{2,10},{18,26},{26,2},{3... | collective-permute-start | bytes 3686408 | tf_op jit(solution)/shard_map/ppermute | solution.py:935
  477.3 170.7 %collective-permute-start.4 = (bf16[160,3840]{1,0:T(8,128)(2,1)}, bf16[160,3840]{1,0:T(8,128)(2,1)}, u32[]{:S(2)}, u32[]{:S(2)}) collective-permute-start(bf16[160,3840]{1,0:T(8,128)(2,1)} %get-tuple-element.335), channel_id=1, source_target_pairs={{8,24},{16,0},{24,8},{9,25},{17,1},{25,9},{10,26},{18,2},{26,10},{... | collective-permute-start | bytes 3686408 | tf_op jit(solution)/shard_map/ppermute | solution.py:935
  479.2 168.7 %collective-permute-start.5 = (bf16[160,3840]{1,0:T(8,128)(2,1)}, bf16[160,3840]{1,0:T(8,128)(2,1)}, u32[]{:S(2)}, u32[]{:S(2)}) collective-permute-start(bf16[160,3840]{1,0:T(8,128)(2,1)} %get-tuple-element.336), channel_id=1, source_target_pairs={{0,24},{8,0},{16,8},{1,25},{9,1},{17,9},{2,26},{10,2},{18,10},{3,2... | collective-permute-start | bytes 3686408 | tf_op jit(solution)/shard_map/ppermute | solution.py:935
  482.1 5.2 slice-start.3
  649.3 196.3 %copy-start.19 = (f32[2,320,640]{2,1,0:T(8,128)S(1)}, f32[2,320,640]{2,1,0:T(8,128)}, u32[]{:S(2)}) copy-start(f32[2,320,640]{2,1,0:T(8,128)} %get-tuple-element.316) | copy-start | bytes 4915204
  649.3 196.4 %copy-start.23 = (f32[2,320,640]{2,1,0:T(8,128)S(1)}, f32[2,320,640]{2,1,0:T(8,128)}, u32[]{:S(2)}) copy-start(f32[2,320,640]{2,1,0:T(8,128)} %get-tuple-element.315) | copy-start | bytes 4915204
  649.3 196.4 %copy-start.27 = (bf16[640,640]{1,0:T(8,128)(2,1)S(1)}, bf16[640,640]{1,0:T(8,128)(2,1)}, u32[]{:S(2)}) copy-start(bf16[640,640]{1,0:T(8,128)(2,1)} %refs_2_.3) | copy-start | bytes 2457604
  649.3 196.4 %copy-start.39 = (f32[2,320,640]{2,1,0:T(8,128)S(1)}, f32[2,320,640]{2,1,0:T(8,128)}, u32[]{:S(2)}) copy-start(f32[2,320,640]{2,1,0:T(8,128)} %get-tuple-element.323) | copy-start | bytes 4915204
  649.3 196.4 %copy-start.61 = (f32[640]{0:T(1024)S(1)}, f32[640]{0:T(1024)}, u32[]{:S(2)}) copy-start(f32[640]{0:T(1024)} %copy-done.60) | copy-start | bytes 7684
  649.3 196.4 %copy-start.65 = (f32[640]{0:T(1024)S(1)}, f32[640]{0:T(1024)}, u32[]{:S(2)}) copy-start(f32[640]{0:T(1024)} %copy-done.64) | copy-start | bytes 7684
  845.7 3.8 copy-start.78
  848.0 4.6 copy-start.66
  849.5 11.8 %copy-start.55 = (f32[8,1280]{1,0:T(8,128)}, f32[8,1280]{1,0:T(8,128)S(1)}, u32[]{:S(2)}) copy-start(f32[8,1280]{1,0:T(8,128)S(1)} %get-tuple-element.496) | copy-start | bytes 122884
  849.5 11.2 %copy-start.68 = (f32[2,640]{1,0:T(2,128)}, f32[2,640]{1,0:T(2,128)S(1)}, u32[]{:S(2)}) copy-start(f32[2,640]{1,0:T(2,128)S(1)} %get-tuple-element.499) | copy-start | bytes 15364
  852.6 4.8 copy-start.47
  859.3 7.8 copy-start.30
  859.4 4.6 copy-start.5
  (52 other events, 112.3 us)
Sparse Core Ops, SparseCore 0:
  39.5 58.0 reduce-scatter.4
  207.6 87.5 reduce-scatter.6
  297.6 168.4 reduce-scatter.8
  468.3 173.0 reduce-scatter.10

commit v6 on v4

--- a/solution.py
+++ b/solution.py
@@ -952,7 +952,7 @@
     place = lax.axis_index("col")
     me = lax.axis_index("dp")
     small = out.shape[0]
-    width = pieces.shape[1]
+    width = pieces.shape[2]
     side = x.shape[0]
     rows = side // 4
     moves = [
@@ -995,9 +995,9 @@
     def _():
         load(CON_OWNER, lambda j: packed.at[j])
         for j in range(4):
-            for k in range(width // rows):
-                first_column = j * width + k * rows
-                x[:, first_column : first_column + rows] = packed[j, :, k * side : (k + 1) * side].T
+            for k in range(4):
+                part = packed[j, :, k * width : (k + 1) * width]
+                x[k * rows : (k + 1) * rows, j * width : (j + 1) * width] = part
 
     @pl.when(me == GATE_OWNER)
     def _():
@@ -1014,7 +1014,7 @@
     @pl.when(me == CON_OWNER)
     def _():
         for j in range(4):
-            pieces[j] = x[:, j * width : (j + 1) * width].T
+            pieces[j] = x[:, j * width : (j + 1) * width]
 
     start(3, 4, 5)
     for k, part in enumerate((first, second, third)):
@@ -1268,7 +1268,7 @@
         expand_grad, contract_sum = lax.optimization_barrier((expand_grad, contract_sum))
         expand_sum = pair_sum(expand_grad, 4)
         con_low = (momentum_rate * contract_momentum[0] + contract_sum).astype(bf16)
-        con_low = beside(con_low, expand_momentum.shape[2])
+        con_low = beside(con_low.T, expand_momentum.shape[2])
         weighted = grad_normed_one * norm_gains[0][None, :]
         inner_part = jnp.sum(stream * weighted, axis=1)
         gain_one_grad = jnp.sum(grad_normed_one * stream * scale_one[:, None], axis=0)
@@ -1310,7 +1310,7 @@
         output_low = (momentum_rate * output_momentum[0] + output_sum).astype(bf16)
         expand_orth, con, branch_orth, out, gates_all, col_total, dp_total = finish_blocks(
             large,
-            contract_momentum.shape[1:],
+            contract_momentum.shape[:0:-1],
             branch_low[0],
             branch_low[1],
             output_low,
@@ -1319,6 +1319,7 @@
             dp_part,
         )
         output_sum = output_sum.astype(f32)
+        con = con.T
         gates_total = gates_all.astype(f32)
         vectors_total = dp_total[:8]
         gains_total = dp_total[8, : 2 * feature_count].reshape(2, feature_count)

time: 882 us -> 902 us (1.023)
  local copies, waits for them, and re-layouts: 37.2 us -> 58.3 us
  waiting for transfers between devices: 191 us -> 181 us
    unnamed x188 -> x158, local copies, waits for them, and re-layouts: 20.6 us -> 33.1 us
    reduce_scatter x3, waiting for transfers between devices: 191 us -> 181 us  [pair_sum(): return lax.psum_scatter(grad, 'dp', scatter_dimension=0)]
    unnamed x13 -> x12, other arithmetic: 14.4 us -> 18.5 us
  transfers between devices with their start and end apart: 10 -> 10, of which waited for: 3 -> 3; matrix products, arithmetic and copies ran while one was open for 9% -> 11% of each run, Pallas kernels for 32% -> 32%
where the time goes in v6:
time: 902 us; the launch traced here: 896 us
  Pallas kernels  514 us (57%)
  waiting for transfers between devices  181 us (20%)
  other arithmetic  89.6 us (10%)
  local copies, waits for them, and re-layouts  58.3 us (6%)
  blocking collectives  18.4 us (2%)
  between operations  15.5 us (2%)
  starting transfers between devices  10.5 us (1%)
  matrix products  9.2 us (1%)
    pallas_call x1, Pallas kernels, finish_blocks(): pl.pallas_call(tail_kernel, out_shape=tuple(shapes), in_specs=[anywhere]...  199 us
    reduce_scatter x3, waiting for transfers between devices, pair_sum(): return lax.psum_scatter(grad, 'dp', scatter_dimension=0)  181 us
    pallas_call x3, Pallas kernels, meet_product(): pl.pallas_call(functools.partial(meet_kernel, flip, grad_mode), out_shape...  153 us
    pallas_call x3, Pallas kernels, spread_product(): pl.pallas_call(functools.partial(spread_kernel, flip, gain is not None),...  108 us
    unnamed x158, local copies, waits for them, and re-layouts  33.1 us
    pallas_call x1, Pallas kernels, meet_gradient(): pl.pallas_call(functools.partial(meet_kernel, False, 'lone'), out_shape=(...  31.8 us
    unnamed x12, other arithmetic  18.5 us
  transfers between devices with their start and end apart: 10, of which 3 were waited for; matrix products, arithmetic and copies ran while one was open for 11% of the time, Pallas kernels for 32%

profile of v6, /device:TPU:24, one launch (start us, length us, event | category | flops | bytes accessed | tf_op | source)
XLA Modules:
  0.0 895.9 jit_solution(15786782949731217221)
XLA Ops:
  8.6 30.1 %shard_map.344 = (f32[2,160,1280]{2,1,0:T(8,128)}, bf16[640,640]{1,0:T(8,128)(2,1)}, f32[8,640]{1,0:T(8,128)}, bf16[640,3840]{1,0:T(8,128)(2,1)}) custom-call(bf16[640,640]{1,0:T(8,128)(2,1)} %refs_2_.3, f32[1,640]{1,0:T(1,128)} %get-tuple-element.548.refs_1_, bf16[640,640]{1,0:T(8,128)(2,1)} %refs_1_.8, bf16[2,640,1280]{2,1,0:T(8,128)(2,1)} %refs_1_.11, ...), custom_call_target="tpu_custom_call" | custom-call | tf_op jit(solution)/shard_map/pallas_call | solution.py:349
  44.4 2.1 convolution_bitcast_fusion
  50.5 5.5 all-gather.2
  56.4 2.7 fusion.90
  59.1 41.3 %shard_map.346 = (bf16[1,2,2,160,1280]{4,3,2,1,0:T(8,128)(2,1)}, f32[2,320,640]{2,1,0:T(8,128)}, bf16[640,640]{1,0:T(8,128)(2,1)}, f32[8,640]{1,0:T(8,128)}) custom-call(bf16[1,160,1280]{2,1,0:T(8,128)(2,1)} %get-tuple-element.498.refs_0_, bf16[1280,640]{1,0:T(8,128)(2,1)} %refs_1_.10, bf16[640,640]{1,0:T(8,128)(2,1)} %refs_2_.3, ...), custom_call_target="tpu_custom_call" | custom-call | tf_op jit(solution)/shard_map/pallas_call | solution.py:633
  100.4 62.1 %shard_map.347 = f32[2,160,3840]{2,1,0:T(8,128)} custom-call(bf16[2,2,160,640]{3,2,1,0:T(8,128)(2,1)} %bitcast.340, bf16[2,640,3840]{2,1,0:T(8,128)(2,1)} %refs_1_.9), custom_call_target="tpu_custom_call" | custom-call | tf_op jit(solution)/shard_map/pallas_call | solution.py:349
  162.5 3.3 fusion.23.refs_0_
  165.9 31.8 %shard_map.348 = (bf16[1,2,2,160,3840]{4,3,2,1,0:T(8,128)(2,1)S(1)}, bf16[3840,640]{1,0:T(8,128)(2,1)S(1)}) custom-call(bf16[1,160,3840]{2,1,0:T(8,128)(2,1)S(1)} %fusion.23.refs_0_, bf16[640,640]{1,0:T(8,128)(2,1)S(1)} %copy-done), custom_call_target="tpu_custom_call" | custom-call | tf_op jit(solution)/shard_map/pallas_call | solution.py:573
  197.7 2.2 copy-done.1
  199.9 2.2 copy-done.15
  202.2 3.9 fusion.42
  207.7 7.9 copy.88
  218.0 73.3 %shard_map.349 = (f32[2,320,640]{2,1,0:T(8,128)}, bf16[4,2,160,3840]{3,2,1,0:T(8,128)(2,1)}) custom-call(bf16[2,160,3840]{2,1,0:T(8,128)(2,1)} %pad_maximum_fusion.1.refs_0_, bf16[2,640,3840]{2,1,0:T(8,128)(2,1)} %refs_1_.9, bf16[640,640]{1,0:T(8,128)(2,1)} %bitcast.335), custom_call_target="tpu_custom_call" | custom-call | tf_op jit(solution)/shard_map/pallas_call | solution.py:633
  291.3 17.3 %reduce-scatter.7.cloned.1.call-done = bf16[1,960,640]{1,2,0:T(8,128)(2,1)} async-done(((bf16[4,960,640]{1,2,0:T(8,128)(2,1)}), bf16[1,960,640]{1,2,0:T(8,128)(2,1)}) %reduce-scatter.7.cloned.1.call-update) | async-done | bytes 1228816 | tf_op jit(solution)/shard_map/reduce_scatter | solution.py:779
  308.7 3.3 copy.83
  317.5 2.2 multiply_reduce_fusion.1
  319.8 7.2 psum.7
  327.0 3.3 fusion.103
  330.3 16.0 %shard_map.350 = f32[1,160,1280]{2,1,0:T(8,128)} custom-call(bf16[2,2,160,640]{3,2,1,0:T(8,128)(2,1)} %bitcast.337, bf16[1280,640]{1,0:T(8,128)(2,1)} %refs_1_.10), custom_call_target="tpu_custom_call" | custom-call | tf_op jit(solution)/shard_map/pallas_call | solution.py:349
  351.2 5.7 all-gather.3
  357.3 3.8 multiply_reduce_fusion.3
  372.8 17.9 %shard_map.353 = bf16[128,1280]{1,0:T(8,128)(2,1)S(1)} custom-call(bf16[160,1280]{1,0:T(8,128)(2,1)S(1)} %get-tuple-element.500.conv, bf16[160,1280]{1,0:T(8,128)(2,1)S(1)} %get-tuple-element.535.first, bf16[160,1280]{1,0:T(8,128)(2,1)S(1)} %get-tuple-element.534.second), custom_call_target="tpu_custom_call" | custom-call | tf_op jit(solution)/shard_map/pallas_call | solution.py:751
  391.4 4.9 fusion.37
  398.6 38.6 %shard_map.352 = (f32[2,320,640]{2,1,0:T(8,128)}, bf16[4,2,160,1280]{3,2,1,0:T(8,128)(2,1)}) custom-call(bf16[2,160,1280]{2,1,0:T(8,128)(2,1)} %pad_maximum_fusion.4.refs_0_, bf16[2,640,1280]{2,1,0:T(8,128)(2,1)} %refs_1_.11, bf16[640,640]{1,0:T(8,128)(2,1)} %bitcast.334), custom_call_target="tpu_custom_call" | custom-call | tf_op jit(solution)/shard_map/pallas_call | solution.py:633
  437.2 2.2 fusion.28
  439.6 7.6 pad_maximum_fusion
  447.2 2.8 fusion.35
  450.6 2.2 concatenate.59
  452.8 26.9 %reduce-scatter.9.cloned.1.call-done = bf16[1,2,160,3840]{3,2,1,0:T(8,128)(2,1)} async-done(((bf16[4,2,160,3840]{3,2,1,0:T(8,128)(2,1)}), bf16[1,2,160,3840]{3,2,1,0:T(8,128)(2,1)}) %reduce-scatter.9.cloned.1.call-update) | async-done | bytes 2457616 | tf_op jit(solution)/shard_map/reduce_scatter | solution.py:779
  479.7 2.4 constant_dynamic-slice_fusion
  482.2 2.6 copy.113
  484.7 3.0 fusion.1
  487.8 2.2 select_select_fusion
  491.5 1.9 fusion.4
  493.4 3.2 copy.104
  496.6 2.7 collective-permute-start.3
  502.5 3.1 convert_bitcast_fusion.1
  505.6 3.3 copy.98
  509.0 4.4 convert_bitcast_fusion
  513.4 5.2 fusion
  518.6 136.3 %reduce-scatter.11.cloned.1.call-done = bf16[1,512,1280]{2,1,0:T(8,128)(2,1)} async-done(((bf16[4,512,1280]{2,1,0:T(8,128)(2,1)}), bf16[1,512,1280]{2,1,0:T(8,128)(2,1)}) %reduce-scatter.11.cloned.1.call-update) | async-done | bytes 1310736 | tf_op jit(solution)/shard_map/reduce_scatter | solution.py:779
  662.8 199.1 %shard_map.354 = (bf16[2,160,3840]{2,1,0:T(8,128)(2,1)S(1)}, bf16[640,960]{1,0:T(8,128)(2,1)S(1)}, bf16[2,160,1280]{2,1,0:T(8,128)(2,1)S(1)}, bf16[320,640]{1,0:...) custom-call(bf16[160,3840]{1,0:T(8,128)(2,1)S(1)} %get-tuple-element.325.ref, ...), custom_call_target="tpu_custom_call" | custom-call | tf_op jit(solution)/shard_map/pallas_call | solution.py:1064
  862.0 2.2 fusion.31
  866.1 3.7 fusion.5
  869.8 3.2 copy.101
  873.1 2.7 subtract_bitcast_fusion.1
  875.8 4.7 subtract_bitcast_fusion
  885.1 2.0 subtract_bitcast_fusion.2
  (287 shorter events, 62.5 us)
Async XLA Ops:
  7.2 195.0 %reduce-scatter.5.cloned.1.call-start = ((), (), s32[]{:S(2)}) async-start(), calls=%async_computation.4 | async-start | bytes 6144000 | tf_op jit(solution)/shard_map/reduce_scatter | solution.py:1157
  38.7 2.9 copy-start.68
  38.8 4.4 copy-start.55
  38.8 269.9 %reduce-scatter.7.cloned.1.call-start = ((), (), s32[]{:S(2)}) async-start(), calls=%async_computation.5 | async-start | bytes 6553600 | tf_op jit(solution)/shard_map/reduce_scatter | solution.py:779
  40.2 3.2 collective-permute-start
  43.3 3.2 copy-start.35
  43.4 3.4 copy-start.61
  162.5 3.4 copy-start
  215.6 264.1 %reduce-scatter.9.cloned.1.call-start = ((), (), s32[]{:S(2)}) async-start(), calls=%async_computation.6 | async-start | bytes 12288000 | tf_op jit(solution)/shard_map/reduce_scatter | solution.py:779
  308.7 346.3 %reduce-scatter.11.cloned.1.call-start = ((), (), s32[]{:S(2)}) async-start(), calls=%async_computation.7 | async-start | bytes 6553600 | tf_op jit(solution)/shard_map/reduce_scatter | solution.py:779
  308.7 3.3 copy-start.54
  330.3 16.0 %copy-start.34 = (f32[160,1280]{1,0:T(8,128)S(1)}, f32[160,1280]{1,0:T(8,128)}, u32[]{:S(2)}) copy-start(f32[160,1280]{1,0:T(8,128)} %get-tuple-element.499) | copy-start | bytes 2457604
  330.3 16.0 %copy-start.38 = (f32[2,160,1280]{2,1,0:T(8,128)S(1)}, f32[2,160,1280]{2,1,0:T(8,128)}, u32[]{:S(2)}) copy-start(f32[2,160,1280]{2,1,0:T(8,128)} %get-tuple-element.295) | copy-start | bytes 4915204
  348.2 9.1 %copy-start.62 = (pred[160]{0:T(512)(128)(4,1)S(1)}, pred[160]{0:T(512)(128)(4,1)}, u32[]{:S(2)}) copy-start(pred[160]{0:T(512)(128)(4,1)} %copy-done.61) | copy-start | bytes 484
  357.3 3.8 copy-start.17
  357.3 3.8 copy-start.28
  366.3 24.4 %collective-permute-start.1 = (f32[3,1280]{1,0:T(4,128)S(1)}, f32[3,1280]{1,0:T(4,128)S(1)}, u32[]{:S(2)}, u32[]{:S(2)}) collective-permute-start(f32[3,1280]{1,0:T(4,128)S(1)} %slice.312), channel_id=1, source_target_pairs={{1,0},{2,1},{3,2},{5,4},{6,5},{7,6},{9,8},{10,9},{11,10},{13,12},{... | collective-permute-start | bytes 46088 | tf_op jit(solution)/shard_map/ppermute | solution.py:35
  367.6 23.7 %slice-start = ((s8[4915200]{0:T(1024)(128)(4,1)}), s8[4194304]{0:T(1024)(128)(4,1)S(1)}, s32[]{:S(2)}) async-start(s8[4915200]{0:T(1024)(128)(4,1)} %bitcast.318), calls=%async_computation.8 | async-start | bytes 8388608
  367.6 23.7 %slice-start.2 = ((s8[4915200]{0:T(1024)(128)(4,1)}), s8[4194304]{0:T(1024)(128)(4,1)S(1)}, s32[]{:S(2)}) async-start(s8[4915200]{0:T(1024)(128)(4,1)} %bitcast.330), calls=%async_computation.10 | async-start | bytes 8388608
  369.3 22.0 %slice-start.1 = ((s8[4915200]{0:T(1024)(128)(4,1)}), s8[720896]{0:T(1024)(128)(4,1)S(1)}, s32[]{:S(2)}) async-start(s8[4915200]{0:T(1024)(128)(4,1)} %bitcast.318), calls=%async_computation.9 | async-start | bytes 1441792
  369.3 22.0 %slice-start.3 = ((s8[4915200]{0:T(1024)(128)(4,1)}), s8[720896]{0:T(1024)(128)(4,1)S(1)}, s32[]{:S(2)}) async-start(s8[4915200]{0:T(1024)(128)(4,1)} %bitcast.330), calls=%async_computation.11 | async-start | bytes 1441792
  371.9 18.8 %copy-start.65 = (f32[160]{0:T(256)S(1)}, f32[160]{0:T(256)}, u32[]{:S(2)}) copy-start(f32[160]{0:T(256)} %get-tuple-element.557) | copy-start | bytes 1924
  371.9 18.8 %copy-start.66 = (f32[160]{0:T(256)S(1)}, f32[160]{0:T(256)}, u32[]{:S(2)}) copy-start(f32[160]{0:T(256)} %get-tuple-element.553) | copy-start | bytes 1924
  372.0 18.8 %copy-start.67 = (f32[160]{0:T(256)S(1)}, f32[160]{0:T(256)}, u32[]{:S(2)}) copy-start(f32[160]{0:T(256)} %get-tuple-element.560) | copy-start | bytes 1924
  396.2 51.0 %collective-permute-start.2 = (bf16[640,640]{1,0:T(8,128)(2,1)}, bf16[640,640]{1,0:T(8,128)(2,1)}, u32[]{:S(2)}, u32[]{:S(2)}) collective-permute-start(bf16[640,640]{1,0:T(8,128)(2,1)} %fusion.37), channel_id=1, source_target_pairs={{0,4},{4,0},{1,5},{5,1},{2,6},{6,2},{3,7},{7,3},{8,12},{12,8},{9,1... | collective-permute-start | bytes 2457608 | tf_op jit(solution)/shard_map/ppermute | solution.py:1251
  398.6 38.6 %copy-start.29 = (bf16[640,640]{1,0:T(8,128)(2,1)S(1)}, bf16[640,640]{1,0:T(8,128)(2,1)}, u32[]{:S(2)}) copy-start(bf16[640,640]{1,0:T(8,128)(2,1)} %refs_2_.3) | copy-start | bytes 2457604
  439.6 7.6 copy-start.19
  447.2 2.8 copy-start.21
  447.2 2.8 copy-start.31
  484.7 3.1 copy-start.44
  487.8 3.1 copy-start.22
  487.8 3.7 copy-start.32
  496.6 163.8 %collective-permute-start.3 = (bf16[160,3840]{1,0:T(8,128)(2,1)}, bf16[160,3840]{1,0:T(8,128)(2,1)S(1)}, u32[]{:S(2)}, u32[]{:S(2)}) collective-permute-start(bf16[160,3840]{1,0:T(8,128)(2,1)} %get-tuple-element.326), channel_id=1, source_target_pairs={{0,8},{16,24},{24,0},{1,9},{17,25},{25,1},{2,10},{18,26},{26,2},{3... | collective-permute-start | bytes 3686408 | tf_op jit(solution)/shard_map/ppermute | solution.py:935
  499.3 162.2 %collective-permute-start.4 = (bf16[160,3840]{1,0:T(8,128)(2,1)}, bf16[160,3840]{1,0:T(8,128)(2,1)}, u32[]{:S(2)}, u32[]{:S(2)}) collective-permute-start(bf16[160,3840]{1,0:T(8,128)(2,1)} %get-tuple-element.327), channel_id=1, source_target_pairs={{8,24},{16,0},{24,8},{9,25},{17,1},{25,9},{10,26},{18,2},{26,10},{... | collective-permute-start | bytes 3686408 | tf_op jit(solution)/shard_map/ppermute | solution.py:935
  501.2 160.3 %collective-permute-start.5 = (bf16[160,3840]{1,0:T(8,128)(2,1)}, bf16[160,3840]{1,0:T(8,128)(2,1)}, u32[]{:S(2)}, u32[]{:S(2)}) collective-permute-start(bf16[160,3840]{1,0:T(8,128)(2,1)} %get-tuple-element.328), channel_id=1, source_target_pairs={{0,24},{8,0},{16,8},{1,25},{9,1},{17,9},{2,26},{10,2},{18,10},{3,2... | collective-permute-start | bytes 3686408 | tf_op jit(solution)/shard_map/ppermute | solution.py:935
  509.0 4.4 copy-start.24
  662.8 199.2 %copy-start.20 = (f32[2,320,640]{2,1,0:T(8,128)S(1)}, f32[2,320,640]{2,1,0:T(8,128)}, u32[]{:S(2)}) copy-start(f32[2,320,640]{2,1,0:T(8,128)} %get-tuple-element.308) | copy-start | bytes 4915204
  662.8 199.2 %copy-start.26 = (f32[2,320,640]{2,1,0:T(8,128)S(1)}, f32[2,320,640]{2,1,0:T(8,128)}, u32[]{:S(2)}) copy-start(f32[2,320,640]{2,1,0:T(8,128)} %get-tuple-element.307) | copy-start | bytes 4915204
  662.8 199.2 %copy-start.30 = (bf16[640,640]{1,0:T(8,128)(2,1)S(1)}, bf16[640,640]{1,0:T(8,128)(2,1)}, u32[]{:S(2)}) copy-start(bf16[640,640]{1,0:T(8,128)(2,1)} %refs_2_.3) | copy-start | bytes 2457604
  662.8 199.2 %copy-start.41 = (f32[2,320,640]{2,1,0:T(8,128)S(1)}, f32[2,320,640]{2,1,0:T(8,128)}, u32[]{:S(2)}) copy-start(f32[2,320,640]{2,1,0:T(8,128)} %get-tuple-element.315) | copy-start | bytes 4915204
  862.0 3.9 copy-start.64
  864.4 5.4 copy-start.58
  865.9 18.5 %copy-start.56 = (f32[8,1280]{1,0:T(8,128)}, f32[8,1280]{1,0:T(8,128)S(1)}, u32[]{:S(2)}) copy-start(f32[8,1280]{1,0:T(8,128)S(1)} %get-tuple-element.488) | copy-start | bytes 122884
  865.9 17.9 %copy-start.60 = (f32[2,640]{1,0:T(2,128)}, f32[2,640]{1,0:T(2,128)S(1)}, u32[]{:S(2)}) copy-start(f32[2,640]{1,0:T(2,128)S(1)} %get-tuple-element.491) | copy-start | bytes 15364
  869.8 3.2 copy-start.11
  875.7 4.7 copy-start.49
  882.4 4.6 copy-start.33
  882.5 4.6 copy-start.43
  (36 other events, 67.9 us)
Sparse Core Ops, SparseCore 0:
  38.9 58.0 reduce-scatter.4
  215.7 92.8 reduce-scatter.6
  311.2 168.4 reduce-scatter.8
  481.8 173.0 reduce-scatter.10
